TPU v7x, 256 devices: a whole 4x4x8 slice. The times are simulated.
256 devices in a mesh: ctx: 32 (over x_lo, z, core), head: 8 (over x_hi, y).
Axes of the slice: x: 4 (x_hi: 2, x_lo: 2; x = x_hi * 2 + x_lo), y: 4, z: 8, core: 2. Of those that a mesh axis runs over, the one named last changes fastest.
Arguments:
- queries: bfloat16 [65536, 4096], P('ctx', 'head'), may hold values from -8 to 8
- key_state_matrix: bfloat16 [65536, 1024], P('ctx', 'head'), may hold values from -4.5 to 4.5
- value_state_matrix: bfloat16 [65536, 1024], P('ctx', 'head'), may hold values from -6 to 6
- selected: int32 [128, 3], P('ctx'), may hold values from -1 to 123, as said below
- out_weight: bfloat16 [4096, 2048], P('head'), may hold values from -0.09375 to 0.09375
Outputs:
- mixed: bfloat16 [65536, 2048], P('ctx', 'head')
Inputs may be any that keep to these rules, and one draw needn't show every extreme that they name: `selected`: row j names blocks that lie on lower indices of ctx than block j (the block's index // 4 is the owning index), on three different indices; all rows of one index of ctx name at most one distinct block of each other index; a slot is -1 only when block j's index has fewer than three lower indices, and then exactly the missing slots are -1.
All inputs are finite; a program needn't handle non-finite values.
Results may differ from a plain program's by a relative error of at most 0.015.
Values may be sent and summed in bfloat16 or wider, within the bound.
No kernel may reach another device: no remote copies, remote signals or barrier semaphores. Data moves between devices by JAX's collectives and lax.ppermute only.
A program may use at most 128 MiB of HBM per device.

v0:
```python
import jax
import jax.numpy as jnp
from jax import lax
from jax.sharding import PartitionSpec as P

HEAD_SIZE = 128
BLOCK_TOKENS = 512


def per_device(queries, key_state_matrix, value_state_matrix, selected, out_weight):
    ctx_count = lax.axis_size("ctx")
    ctx_index = lax.axis_index("ctx")
    tok_rows = queries.shape[0]
    blk_dev = tok_rows // BLOCK_TOKENS
    kv_width = key_state_matrix.shape[1]
    kv_heads = kv_width // HEAD_SIZE
    q_heads = queries.shape[1] // HEAD_SIZE
    query_group_size = q_heads // kv_heads
    request_count = blk_dev * 3
    wanted = selected.reshape(request_count)
    owners = wanted // blk_dev
    everyone = lax.all_gather(selected, "ctx", axis=0, tiled=True).reshape(ctx_count, request_count)
    asked = jnp.max(jnp.where(everyone // blk_dev == ctx_index, everyone, -1), axis=1)
    local_block = jnp.clip(asked - ctx_index * blk_dev, 0, blk_dev - 1)
    stacked = jnp.concatenate([key_state_matrix, value_state_matrix], axis=1).reshape(
        blk_dev, BLOCK_TOKENS, 2 * kv_width
    )
    outgoing = jnp.where(
        (asked >= 0)[:, None, None], stacked[local_block], jnp.zeros((), jnp.bfloat16)
    )
    arrived = lax.all_to_all(outgoing, "ctx", split_axis=0, concat_axis=0, tiled=True)
    source = jnp.clip(owners, 0, ctx_count - 1)
    chosen = arrived[source]
    fetched_keys = chosen[:, :, :kv_width]
    fetched_values = chosen[:, :, kv_width:]
    score_scale = HEAD_SIZE ** (-0.5)
    causal = jnp.arange(BLOCK_TOKENS)[:, None] >= jnp.arange(BLOCK_TOKENS)[None, :]
    own_keys = key_state_matrix.reshape(blk_dev, BLOCK_TOKENS, kv_width)
    own_values = value_state_matrix.reshape(blk_dev, BLOCK_TOKENS, kv_width)
    far_keys = fetched_keys.reshape(blk_dev, 3 * BLOCK_TOKENS, kv_width)
    far_values = fetched_values.reshape(blk_dev, 3 * BLOCK_TOKENS, kv_width)
    live_slots = selected >= 0
    blocked_queries = queries.reshape(blk_dev, BLOCK_TOKENS, q_heads * HEAD_SIZE)

    def one_block(inputs):
        query_here, near_key, near_value, remote_key, remote_value, live_here = inputs
        gathered_keys = jnp.concatenate([near_key, remote_key], axis=0).reshape(
            4 * BLOCK_TOKENS, kv_heads, HEAD_SIZE
        )
        gathered_values = jnp.concatenate([near_value, remote_value], axis=0).reshape(
            4 * BLOCK_TOKENS, kv_heads, HEAD_SIZE
        )
        live_sel = jnp.broadcast_to(
            jnp.repeat(live_here, BLOCK_TOKENS)[None, :], (BLOCK_TOKENS, 3 * BLOCK_TOKENS)
        )
        live = jnp.concatenate([causal, live_sel], axis=1)
        grouped = query_here.reshape(BLOCK_TOKENS, kv_heads, query_group_size, HEAD_SIZE)
        scores = (
            jnp.einsum("qhgd,khd->hgqk", grouped, gathered_keys, preferred_element_type=jnp.float32)
            * score_scale
        )
        scores = jnp.where(live[None, None], scores, -1e30)
        highest = jnp.max(scores, axis=-1, keepdims=True)
        expon = jnp.exp(scores - highest)
        weights = (expon / jnp.sum(expon, axis=-1, keepdims=True)).astype(jnp.bfloat16)
        output = jnp.einsum(
            "hgqk,khd->qhgd", weights, gathered_values, preferred_element_type=jnp.float32
        )
        return output.reshape(BLOCK_TOKENS, q_heads * HEAD_SIZE).astype(jnp.bfloat16)

    attended = lax.map(
        one_block, (blocked_queries, own_keys, own_values, far_keys, far_values, live_slots)
    )
    attended = attended.reshape(tok_rows, q_heads * HEAD_SIZE)
    partial_value = jnp.dot(attended, out_weight, preferred_element_type=jnp.float32)
    return lax.psum_scatter(partial_value, "head", scatter_dimension=1, tiled=True).astype(
        jnp.bfloat16
    )


def solution(mesh):
    return jax.shard_map(
        per_device,
        mesh=mesh,
        in_specs=(
            P("ctx", "head"),
            P("ctx", "head"),
            P("ctx", "head"),
            P("ctx", None),
            P("head", None),
        ),
        out_specs=P("ctx", "head"),
        check_vma=False,
    )
```

profile of v0, /device:TPU:226, one launch (start us, length us, event | category | flops | bytes accessed | tf_op | source)
XLA Modules:
  0.0 600.9 jit_solution(18328958841582590714)
XLA Ops:
  6.5 30.3 %all-gather = s32[32,4,3]{2,1,0:T(4,128)S(1)} all-gather(s32[1,4,3]{2,1,0:T(4,128)} %bitcast.99), channel_id=1, replica_groups=mesh['ctx'=32,'head'=8] {'ctx'}, dimensions={0}, use_global_device_ids=true | all-gather | bytes 1584 | tf_op jit(solution)/shard_map/all_gather | solution.py:22
  38.6 4.7 gather_fusion
  43.3 7.2 %broadcast_select_fusion = bf16[32,512,256]{2,1,0:T(8,128)(2,1)} fusion(bf16[32,512,256]{2,1,0:T(8,128)(2,1)} %gather_fusion, pred[32]{0:T(512)(128)(4,1)S(1)} %broadcast_compare_fusion.1), kind=kLoop, calls=%fused_computation.32 | loop fusion | flops 4194304 | bytes 16777248 | tf_op jit(solution)/shard_map/jit(_where)/select_n | solution.py:28
  50.5 9.8 %all-to-all-start = ((bf16[32,512,256]{2,1,0:T(8,128)(2,1)}), bf16[32,512,256]{2,1,0:T(8,128)(2,1)}, u32[]{:S(2)}, u32[]{:S(2)}) async-start(bf16[32,512,256]{2,1,0:T(8,128)(2,1)} %broadcast_select_fusion), calls=%async_computation | async-start | bytes 16777216 | tf_op jit(solution)/shard_map/all_to_all | solution.py:31
  61.1 184.1 %all-to-all-done = bf16[32,512,256]{2,1,0:T(8,128)(2,1)} async-done(((bf16[32,512,256]{2,1,0:T(8,128)(2,1)}), bf16[32,512,256]{2,1,0:T(8,128)(2,1)}, u32[]{:S(2)}, u32[]{:S(2)}) %all-to-all-start) | async-done | bytes 8388640 | tf_op jit(solution)/shard_map/all_to_all | solution.py:31
  245.2 6.0 gather_fusion.1
  251.2 3.9 fusion.24
  255.1 126.3 %while.11 = (s32[]{:T(128)}, bf16[4,512,512]{2,1,0:T(8,128)(2,1)}, bf16[4,512,128]{2,1,0:T(8,128)(2,1)}, bf16[4,1536,128]{2,1,0:T(8,128)(2,1)}, pred[4,3]{1,0:T(...) while((s32[]{:T(128)}, bf16[4,512,512]{2,1,0:T(8,128)(2,1)}, ...), condition=%wide.region_5.6_spmd.clone, body=%wide.region_2.5_spmd.clone.sunk | while | flops 2201481216 | bytes 131648168 | solution.py:71
  256.5 1.9 constant_dynamic-slice_fusion.7
  258.4 2.0 copy.35
  262.4 4.2 fusion.38
  266.6 3.7 fusion.39
  270.3 2.0 copy-done.1
  275.3 9.2 %fusion.40 = bf16[128,4,512]{2,0,1:T(8,128)(2,1)} fusion(f32[4,512]{1,0:T(4,128)S(1)} %fusion.39, f32[4,512]{1,0:T(4,128)S(1)} %get-tuple-element.167, f32[2048,512,4]{1,0,2:T(8,128)} %copy-done.1, pred[512,2048]{0,1:T(8,128)(4,1)S(1)} %pad_add_fusion.2, bf16[1536,128]{0,1:T(8,128)(2,1)} %bitcast.91, bf16[512,128]{0,1:T(8,128)(2,1)S(1)} %bitcast.94), kind=kOutput, calls=%fused_computation.11.clone.1 | convolution fusion | flops 1096024064 | bytes 18890752 | tf_op jit(solution)/shard_map/while/body/eval_jaxpr/hgqk,khd->qhgd/dot_general | solution.py:66
  289.9 2.0 copy.35
  293.9 4.2 fusion.38
  298.1 3.7 fusion.39
  301.8 2.0 copy-done.1
  306.8 9.2 %fusion.40 = bf16[128,4,512]{2,0,1:T(8,128)(2,1)} fusion(f32[4,512]{1,0:T(4,128)S(1)} %fusion.39, f32[4,512]{1,0:T(4,128)S(1)} %get-tuple-element.167, f32[2048,512,4]{1,0,2:T(8,128)} %copy-done.1, pred[512,2048]{0,1:T(8,128)(4,1)S(1)} %pad_add_fusion.2, bf16[1536,128]{0,1:T(8,128)(2,1)} %bitcast.91, bf16[512,128]{0,1:T(8,128)(2,1)S(1)} %bitcast.94), kind=kOutput, calls=%fused_computation.11.clone.1 | convolution fusion | flops 1096024064 | bytes 18890752 | tf_op jit(solution)/shard_map/while/body/eval_jaxpr/hgqk,khd->qhgd/dot_general | solution.py:66
  321.5 2.0 copy.35
  325.5 4.2 fusion.38
  329.7 3.7 fusion.39
  333.4 2.0 copy-done.1
  338.4 9.2 %fusion.40 = bf16[128,4,512]{2,0,1:T(8,128)(2,1)} fusion(f32[4,512]{1,0:T(4,128)S(1)} %fusion.39, f32[4,512]{1,0:T(4,128)S(1)} %get-tuple-element.167, f32[2048,512,4]{1,0,2:T(8,128)} %copy-done.1, pred[512,2048]{0,1:T(8,128)(4,1)S(1)} %pad_add_fusion.2, bf16[1536,128]{0,1:T(8,128)(2,1)} %bitcast.91, bf16[512,128]{0,1:T(8,128)(2,1)S(1)} %bitcast.94), kind=kOutput, calls=%fused_computation.11.clone.1 | convolution fusion | flops 1096024064 | bytes 18890752 | tf_op jit(solution)/shard_map/while/body/eval_jaxpr/hgqk,khd->qhgd/dot_general | solution.py:66
  353.0 2.0 copy.35
  357.0 4.2 fusion.38
  361.3 3.7 fusion.39
  365.0 2.0 copy-done.1
  370.0 9.2 %fusion.40 = bf16[128,4,512]{2,0,1:T(8,128)(2,1)} fusion(f32[4,512]{1,0:T(4,128)S(1)} %fusion.39, f32[4,512]{1,0:T(4,128)S(1)} %get-tuple-element.167, f32[2048,512,4]{1,0,2:T(8,128)} %copy-done.1, pred[512,2048]{0,1:T(8,128)(4,1)S(1)} %pad_add_fusion.2, bf16[1536,128]{0,1:T(8,128)(2,1)} %bitcast.91, bf16[512,128]{0,1:T(8,128)(2,1)S(1)} %bitcast.94), kind=kOutput, calls=%fused_computation.11.clone.1 | convolution fusion | flops 1096024064 | bytes 18890752 | tf_op jit(solution)/shard_map/while/body/eval_jaxpr/hgqk,khd->qhgd/dot_general | solution.py:66
  381.3 9.6 %fusion.25 = f32[2048,2048]{1,0:T(8,128)} fusion(bf16[2048,512]{1,0:T(8,128)(2,1)} %bitcast.100, bf16[512,2048]{1,0:T(8,128)(2,1)S(1)} %copy-done), kind=kOutput, calls=%fused_computation.56 | convolution fusion | flops 4294967296 | bytes 20971520 | tf_op jit(solution)/shard_map/dot_general | solution.py:75
  391.0 200.4 %reduce-scatter.2.cloned.1.call-done = f32[2048,256]{1,0:T(8,128)} async-done(((f32[2048,2048]{1,0:T(8,128)}), f32[2048,256]{1,0:T(8,128)}) %reduce-scatter.2.cloned.1.call-update) | async-done | bytes 2097168 | tf_op jit(solution)/shard_map/reduce_scatter | solution.py:76
  591.4 2.7 convert_element_type.25
  (81 shorter events, 41.9 us)
Async XLA Ops:
  6.5 374.8 %copy-start = (bf16[512,2048]{1,0:T(8,128)(2,1)S(1)}, bf16[512,2048]{1,0:T(8,128)(2,1)}, u32[]{:S(2)}) copy-start(bf16[512,2048]{1,0:T(8,128)(2,1)} %param.11) | copy-start | bytes 6291460
  50.5 10.0 %copy-start.2 = (s32[4,3]{1,0:T(4,128)S(1)}, s32[4,3]{1,0:T(4,128)}, u32[]{:S(2)}) copy-start(s32[4,3]{1,0:T(4,128)} %param.10) | copy-start | bytes 148
  50.5 194.7 %all-to-all-start = ((bf16[32,512,256]{2,1,0:T(8,128)(2,1)}), bf16[32,512,256]{2,1,0:T(8,128)(2,1)}, u32[]{:S(2)}, u32[]{:S(2)}) async-start(bf16[32,512,256]{2,1,0:T(8,128)(2,1)} %broadcast_select_fusion), calls=%async_computation | async-start | bytes 16777216 | tf_op jit(solution)/shard_map/all_to_all | solution.py:31
  60.3 531.1 %reduce-scatter.2.cloned.1.call-start = ((), (), s32[]{:S(2)}) async-start(), calls=%async_computation.2 | async-start | bytes 18874368 | tf_op jit(solution)/shard_map/reduce_scatter | solution.py:76
  266.6 5.7 copy-start.1
  298.1 5.7 copy-start.1
  329.7 5.7 copy-start.1
  361.3 5.7 copy-start.1
Sparse Core Ops, SparseCore 0:
  391.1 200.2 reduce-scatter.1
where the time goes:
time: 605 us; the launch traced here: 601 us
  waiting for transfers between devices  385 us (64%)
  local copies, waits for them, and re-layouts  69.4 us (11%)
  matrix products  63.5 us (10%)
  blocking collectives  30.3 us (5%)
  other arithmetic  29.5 us (5%)
  between operations  13.5 us (2%)
  starting transfers between devices  9.99 us (2%)
    reduce_scatter x1, waiting for transfers between devices, per_device(): lax.psum_scatter(partial_value, 'head', scatter_dimension=1, tiled=True)  200 us
    all_to_all x1, waiting for transfers between devices, per_device(): lax.all_to_all(outgoing, 'ctx', split_axis=0, concat_axis=0, tiled=True)  184 us
    dot_general x4, matrix products, one_block(): jnp.einsum('hgqk,khd->qhgd', weights, gathered_values, preferred_element_...  36.9 us
    all_gather x1, blocking collectives, per_device(): lax.all_gather(selected, 'ctx', axis=0, tiled=True)  30.3 us
    dynamic_slice x24, local copies, waits for them, and re-layouts, per_device(): lax.map(one_block, (blocked_queries, own_keys, own_values, far_keys, far_...  27.5 us
    dot_general x4, matrix products, one_block(): jnp.einsum('qhgd,khd->hgqk', grouped, gathered_keys, preferred_element_ty...  16.9 us
    reduce_sum x4, other arithmetic, one_block(): jnp.sum(expon, axis=-1, keepdims=True)  14.7 us
  transfers between devices with their start and end apart: 2, of which 2 were waited for; matrix products, arithmetic and copies ran while one was open for 0% of the time, Pallas kernels for 0%

commit v1 on v0

v1 whole, which is shorter than its diff:
```python
import functools

import jax
import jax.numpy as jnp
from jax import lax
from jax.experimental import pallas as pl
from jax.experimental.pallas import tpu as pltpu
from jax.sharding import PartitionSpec as P

HEAD_SIZE = 128
BLOCK_TOKENS = 512
TILE = 256
SLOTS = 4
SCORE_SCALE = HEAD_SIZE ** (-0.5)
EXP2_SCALE = SCORE_SCALE * 1.4426950408889634


def attention_kernel(q_heads, table, q_ref, kv_ref, o_ref, keys, values, sems):
    step = pl.program_id(0)
    steps = pl.num_programs(0)
    here = lax.rem(step, 2)

    def copies(at, buf):
        out = []
        for slot in range(SLOTS):
            own = table[at * SLOTS + SLOTS - 1]
            block = table[at * SLOTS + slot]
            block = jnp.where(block < 0, own, block)
            rows = pl.ds(pl.multiple_of(block * BLOCK_TOKENS, BLOCK_TOKENS), BLOCK_TOKENS)
            to = pl.ds(slot * BLOCK_TOKENS, BLOCK_TOKENS)
            out.append(
                pltpu.make_async_copy(
                    kv_ref.at[rows, pl.ds(0, HEAD_SIZE)], keys.at[buf, to], sems.at[buf, slot, 0]
                )
            )
            out.append(
                pltpu.make_async_copy(
                    kv_ref.at[rows, pl.ds(HEAD_SIZE, HEAD_SIZE)],
                    values.at[buf, to, pl.ds(0, HEAD_SIZE)],
                    sems.at[buf, slot, 1],
                )
            )
        return out

    @pl.when(step == 0)
    def _():
        for copy in copies(step, here):
            copy.start()

    @pl.when(step + 1 < steps)
    def _():
        for copy in copies(step + 1, 1 - here):
            copy.start()

    for copy in copies(step, here):
        copy.wait()

    values[here, pl.ds(0, SLOTS * BLOCK_TOKENS), pl.ds(HEAD_SIZE, HEAD_SIZE)] = jnp.ones(
        (SLOTS * BLOCK_TOKENS, HEAD_SIZE), jnp.bfloat16
    )
    for slot in range(SLOTS - 1):

        @pl.when(table[step * SLOTS + slot] < 0)
        def _():
            to = pl.ds(slot * BLOCK_TOKENS, BLOCK_TOKENS)
            first = keys[here, pl.ds((SLOTS - 1) * BLOCK_TOKENS, 16), :][0:1, :]
            keys[here, to, :] = jnp.broadcast_to(first, (BLOCK_TOKENS, HEAD_SIZE))
            values[here, to, :] = jnp.zeros((BLOCK_TOKENS, 2 * HEAD_SIZE), jnp.bfloat16)

    row = lax.broadcasted_iota(jnp.int32, (TILE, TILE), 0)
    col = lax.broadcasted_iota(jnp.int32, (TILE, TILE), 1)
    causal = row >= col
    dims = (((1,), (1,)), ((), ()))

    for head in range(q_heads):
        lanes = pl.ds(head * HEAD_SIZE, HEAD_SIZE)
        for tile in range(BLOCK_TOKENS // TILE):
            rows = pl.ds(tile * TILE, TILE)
            full = (SLOTS - 1) * BLOCK_TOKENS + tile * TILE
            query = q_ref[rows, lanes]
            far = lax.dot_general(
                query, keys[here, pl.ds(0, full), :], dims, preferred_element_type=jnp.float32
            )
            near = lax.dot_general(
                query, keys[here, pl.ds(full, TILE), :], dims, preferred_element_type=jnp.float32
            )
            near = jnp.where(causal, near, -1e30)
            highest = jnp.maximum(
                jnp.max(far, axis=1, keepdims=True), jnp.max(near, axis=1, keepdims=True)
            )
            far = jnp.exp2((far - highest) * EXP2_SCALE).astype(jnp.bfloat16)
            near = jnp.exp2((near - highest) * EXP2_SCALE).astype(jnp.bfloat16)
            total = jnp.dot(
                far, values[here, pl.ds(0, full), :], preferred_element_type=jnp.float32
            ) + jnp.dot(
                near, values[here, pl.ds(full, TILE), :], preferred_element_type=jnp.float32
            )
            o_ref[rows, lanes] = (total[:, :HEAD_SIZE] / total[:, HEAD_SIZE:]).astype(jnp.bfloat16)


def attention(queries, gathered, table):
    rows, width = queries.shape
    blocks = rows // BLOCK_TOKENS
    keys = SLOTS * BLOCK_TOKENS
    return pl.pallas_call(
        functools.partial(attention_kernel, width // HEAD_SIZE),
        out_shape=jax.ShapeDtypeStruct((rows, width), jnp.bfloat16),
        grid_spec=pltpu.PrefetchScalarGridSpec(
            num_scalar_prefetch=1,
            grid=(blocks,),
            in_specs=[
                pl.BlockSpec((BLOCK_TOKENS, width), lambda i, t: (i, 0)),
                pl.BlockSpec(memory_space=pl.ANY),
            ],
            out_specs=pl.BlockSpec((BLOCK_TOKENS, width), lambda i, t: (i, 0)),
            scratch_shapes=[
                pltpu.VMEM((2, keys, HEAD_SIZE), jnp.bfloat16),
                pltpu.VMEM((2, keys, 2 * HEAD_SIZE), jnp.bfloat16),
                pltpu.SemaphoreType.DMA((2, SLOTS, 2)),
            ],
        ),
        compiler_params=pltpu.CompilerParams(
            dimension_semantics=("arbitrary",), vmem_limit_bytes=48 * 1024 * 1024
        ),
        cost_estimate=pl.CostEstimate(
            flops=4 * rows * (width // HEAD_SIZE) * keys * HEAD_SIZE,
            bytes_accessed=4 * rows * width + 4 * blocks * keys * HEAD_SIZE,
            transcendentals=rows * (width // HEAD_SIZE) * keys,
        ),
    )(table, queries, gathered)


def project_kernel(parts, a_ref, w_ref, o_ref):
    total = jnp.dot(a_ref[0], w_ref[0], preferred_element_type=jnp.float32)
    for part in range(1, parts):
        total += jnp.dot(a_ref[part], w_ref[part], preferred_element_type=jnp.float32)
    o_ref[0] = total.astype(jnp.bfloat16)


def project(attended, weight):
    parts, rows, features = attended.shape
    columns = weight.shape[2] // parts
    return pl.pallas_call(
        functools.partial(project_kernel, parts),
        out_shape=jax.ShapeDtypeStruct((parts, rows, columns), jnp.bfloat16),
        grid=(parts,),
        in_specs=[
            pl.BlockSpec((parts, rows, features), lambda i: (0, 0, 0)),
            pl.BlockSpec((parts, features, columns), lambda i: (0, 0, i)),
        ],
        out_specs=pl.BlockSpec((1, rows, columns), lambda i: (i, 0, 0)),
        compiler_params=pltpu.CompilerParams(
            dimension_semantics=("arbitrary",), vmem_limit_bytes=32 * 1024 * 1024
        ),
        cost_estimate=pl.CostEstimate(
            flops=2 * parts * parts * rows * features * columns,
            bytes_accessed=2 * parts * parts * features * columns + 4 * parts * rows * features,
            transcendentals=0,
        ),
    )(attended, weight)


def gather_weight(out_weight, ctx_count):
    half = out_weight.shape[0] // 2
    core = lax.rem(lax.axis_index("ctx"), 2)
    head = lax.axis_index("head")
    mine = lax.dynamic_slice_in_dim(out_weight, core * half, half, 0)

    def along(dx, dy):
        return [
            (i, ((i // 4 + dx) % 2) * 4 + (i % 4 + dy) % 4) for i in range(8)
        ]

    def send(value, dx, dy):
        return lax.ppermute(value, "head", along(dx, dy))

    other = send(mine, 1, 0)
    mine_up, mine_down = send(mine, 0, 1), send(mine, 0, -1)
    other_up, other_down = send(other, 0, 1), send(other, 0, -1)
    mine_far, other_far = send(mine_up, 0, 1), send(other_down, 0, -1)
    pieces = [mine, mine_up, mine_far, mine_down, other, other_up, other_far, other_down]
    stacked = jnp.stack(pieces)
    swapped = lax.ppermute(stacked, "ctx", [(i, i ^ 1) for i in range(ctx_count)])
    both = jnp.concatenate([stacked, swapped])
    owner = jnp.arange(8)
    dx = jnp.where(owner // 4 == head // 4, 0, 1)
    dy = (head % 4 - owner % 4) % 4
    which = dx * 4 + dy
    order = jnp.stack(
        [jnp.where(core == 0, which, which + 8), jnp.where(core == 0, which + 8, which)], axis=1
    ).reshape(16)
    return both[order].reshape(8, 2 * half, out_weight.shape[1])


def per_device(queries, key_state_matrix, value_state_matrix, selected, out_weight):
    ctx_count = lax.axis_size("ctx")
    head_count = lax.axis_size("head")
    ctx_index = lax.axis_index("ctx")
    rows, width = queries.shape
    blocks = rows // BLOCK_TOKENS
    stacked = jnp.concatenate([key_state_matrix, value_state_matrix], axis=1)
    gathered = lax.all_gather(stacked, "ctx", axis=0, tiled=True)
    weight = gather_weight(out_weight, ctx_count)
    own = (ctx_index * blocks + jnp.arange(blocks, dtype=jnp.int32))[:, None]
    table = jnp.concatenate([selected, own], axis=1).reshape(-1)
    attended = attention(queries, gathered, table)
    tokens = lax.all_to_all(
        attended.reshape(head_count, rows // head_count, width), "head", 0, 0, tiled=True
    )
    mixed = project(tokens, weight)
    return lax.all_to_all(mixed, "head", 0, 0, tiled=True).reshape(rows, -1)


def solution(mesh):
    return jax.shard_map(
        per_device,
        mesh=mesh,
        in_specs=(
            P("ctx", "head"),
            P("ctx", "head"),
            P("ctx", "head"),
            P("ctx", None),
            P("head", None),
        ),
        out_specs=P("ctx", "head"),
        check_vma=False,
    )
```

time: 605 us -> 312 us (0.52)
  waiting for transfers between devices: 385 us -> 176 us
  matrix products: 63.5 us -> 0 us
  Pallas kernels: 0 us -> 33.8 us
  other arithmetic: 29.5 us -> 2.4 us
  local copies, waits for them, and re-layouts: 69.4 us -> 44.2 us
  starting transfers between devices: 9.99 us -> 18.4 us
  blocking collectives: 30.3 us -> 22 us
    reduce_scatter x1 -> x0, waiting for transfers between devices: 200 us -> none  [per_device(): lax.psum_scatter(partial_value, 'head', scatter_dimension=1, tiled=True)]
    all_to_all x1, waiting for transfers between devices: 184 us -> 5.3 us  [per_device(): lax.all_to_all(attended.reshape(head_count, rows // head_count, width), '...]
    ppermute x0 -> x8, waiting for transfers between devices: none -> 85.7 us  [the longest x7 85.7 us: send(): return lax.ppermute(value, 'head', along(dx, dy))]
    all_gather x0 -> x1, waiting for transfers between devices: none -> 84.7 us  [per_device(): gathered = lax.all_gather(stacked, 'ctx', axis=0, tiled=True)]
    dot_general x9 -> x0, matrix products: 63.5 us -> none  [the longest x4 36.9 us: one_block(): jnp.einsum('hgqk,khd->qhgd', weights, gathered_values, preferred_element_...]
    pallas_call x0 -> x2, Pallas kernels: none -> 33.8 us  [the longest x1 25.6 us: attention(): pl.pallas_call(functools.partial(attention_kernel, width // HEAD_SIZE), o...]
    all_gather x1 -> x0, blocking collectives: 30.3 us -> none  [per_device(): lax.all_gather(selected, 'ctx', axis=0, tiled=True)]
    dynamic_slice x24 -> x0, local copies, waits for them, and re-layouts: 27.5 us -> none  [per_device(): lax.map(one_block, (blocked_queries, own_keys, own_values, far_keys, far_...]
  transfers between devices with their start and end apart: 2 -> 10, of which waited for: 2 -> 6; matrix products, arithmetic and copies ran while one was open for 0% -> 12% of each run, Pallas kernels for 0% -> 8%
where the time goes in v1:
time: 312 us; the launch traced here: 310 us
  waiting for transfers between devices  176 us (56%)
  local copies, waits for them, and re-layouts  44.2 us (14%)
  Pallas kernels  33.8 us (11%)
  blocking collectives  22 us (7%)
  starting transfers between devices  18.4 us (6%)
  between operations  13.5 us (4%)
    ppermute x7, waiting for transfers between devices, send(): return lax.ppermute(value, 'head', along(dx, dy))  85.7 us
    all_gather x1, waiting for transfers between devices, per_device(): gathered = lax.all_gather(stacked, 'ctx', axis=0, tiled=True)  84.7 us
    pallas_call x1, Pallas kernels, attention(): pl.pallas_call(functools.partial(attention_kernel, width // HEAD_SIZE), o...  25.6 us
    all_to_all x1, blocking collectives, per_device(): return lax.all_to_all(mixed, 'head', 0, 0, tiled=True).reshape(rows, -1)  22 us
    unnamed x17, local copies, waits for them, and re-layouts  21 us
    ppermute x7, starting transfers between devices, send(): return lax.ppermute(value, 'head', along(dx, dy))  13.9 us
    gather x1, local copies, waits for them, and re-layouts, gather_weight(): return both[order].reshape(8, 2 * half, out_weight.shape[1])  13 us
    concatenate x1, local copies, waits for them, and re-layouts, gather_weight(): both = jnp.concatenate([stacked, swapped])  8.27 us
  transfers between devices with their start and end apart: 10, of which 6 were waited for; matrix products, arithmetic and copies ran while one was open for 12% of the time, Pallas kernels for 8%

profile of v1, /device:TPU:226, one launch (start us, length us, event | category | flops | bytes accessed | tf_op | source)
XLA Modules:
  0.0 310.0 jit_solution(16075222715150490044)
XLA Ops:
  6.5 2.3 pad_maximum_fusion
  8.9 2.4 bitcast_dynamic-update-slice_fusion.15
  11.2 2.1 collective-permute-start.3
  13.3 1.6 collective-permute-start
  14.9 37.5 %collective-permute-done.3 = bf16[256,2048]{1,0:T(8,128)(2,1)S(1)} collective-permute-done((bf16[256,2048]{1,0:T(8,128)(2,1)S(1)}, bf16[256,2048]{1,0:T(8,128)(2,1)S(1)}, u32[]{:S(2)}, u32[]{:S(2)}) %collective-permute-start.3) | collective-permute-done | bytes 1048608 | tf_op jit(solution)/shard_map/ppermute | solution.py:175
  52.4 3.3 %collective-permute-start.5 = (bf16[256,2048]{1,0:T(8,128)(2,1)S(1)}, bf16[256,2048]{1,0:T(8,128)(2,1)S(1)}, u32[]{:S(2)}, u32[]{:S(2)}) collective-permute-start(bf16[256,2048]{1,0:T(8,128)(2,1)S(1)} %collective-permute-done.3), channel_id=1, source_target_pairs={{0,3},{1,0},{2,1},{3,2},{4,7},{5,4},{6,5},{7,6},{8,11},{9,8},{10,9... | collective-permute-start | bytes 3145736 | tf_op jit(solution)/shard_map/ppermute | solution.py:175
  55.7 3.2 %collective-permute-start.2 = (bf16[256,2048]{1,0:T(8,128)(2,1)S(1)}, bf16[256,2048]{1,0:T(8,128)(2,1)S(1)}, u32[]{:S(2)}, u32[]{:S(2)}) collective-permute-start(bf16[256,2048]{1,0:T(8,128)(2,1)S(1)} %get-tuple-element.6), channel_id=1, source_target_pairs={{0,3},{1,0},{2,1},{3,2},{4,7},{5,4},{6,5},{7,6},{8,11},{9,8},{10,9... | collective-permute-start | bytes 3145736 | tf_op jit(solution)/shard_map/ppermute | solution.py:175
  58.9 1.1 bitcast_dynamic-update-slice_fusion.14
  60.0 1.6 bitcast_dynamic-update-slice_fusion.13
  61.6 17.7 %collective-permute-done.5 = bf16[256,2048]{1,0:T(8,128)(2,1)S(1)} collective-permute-done((bf16[256,2048]{1,0:T(8,128)(2,1)S(1)}, bf16[256,2048]{1,0:T(8,128)(2,1)S(1)}, u32[]{:S(2)}, u32[]{:S(2)}) %collective-permute-start.5) | collective-permute-done | bytes 1048608 | tf_op jit(solution)/shard_map/ppermute | solution.py:175
  79.3 3.7 %collective-permute-start.6 = (bf16[256,2048]{1,0:T(8,128)(2,1)S(1)}, bf16[256,2048]{1,0:T(8,128)(2,1)S(1)}, u32[]{:S(2)}, u32[]{:S(2)}) collective-permute-start(bf16[256,2048]{1,0:T(8,128)(2,1)S(1)} %collective-permute-done.5), channel_id=1, source_target_pairs={{0,3},{1,0},{2,1},{3,2},{4,7},{5,4},{6,5},{7,6},{8,11},{9,8},{10,9... | collective-permute-start | bytes 3145736 | tf_op jit(solution)/shard_map/ppermute | solution.py:175
  83.0 1.6 bitcast_dynamic-update-slice_fusion.11
  84.6 17.2 %collective-permute-done.2 = bf16[256,2048]{1,0:T(8,128)(2,1)S(1)} collective-permute-done((bf16[256,2048]{1,0:T(8,128)(2,1)S(1)}, bf16[256,2048]{1,0:T(8,128)(2,1)S(1)}, u32[]{:S(2)}, u32[]{:S(2)}) %collective-permute-start.2) | collective-permute-done | bytes 1048608 | tf_op jit(solution)/shard_map/ppermute | solution.py:175
  101.8 1.6 bitcast_dynamic-update-slice_fusion.9
  103.4 1.6 bitcast_dynamic-update-slice_fusion.7
  105.0 1.6 bitcast_dynamic-update-slice_fusion.5
  106.5 13.3 %collective-permute-done.6 = bf16[256,2048]{1,0:T(8,128)(2,1)S(1)} collective-permute-done((bf16[256,2048]{1,0:T(8,128)(2,1)S(1)}, bf16[256,2048]{1,0:T(8,128)(2,1)S(1)}, u32[]{:S(2)}, u32[]{:S(2)}) %collective-permute-start.6) | collective-permute-done | bytes 1048608 | tf_op jit(solution)/shard_map/ppermute | solution.py:175
  119.9 1.6 bitcast_dynamic-update-slice_fusion.3
  121.4 1.6 bitcast_dynamic-update-slice_fusion.1
  123.2 0.1 reshape.157.table
  123.2 84.7 %all-gather.2.cloned.1.call-done.kv_ref = bf16[65536,256]{1,0:T(8,128)(2,1)} async-done(((bf16[2048,256]{1,0:T(8,128)(2,1)}), bf16[65536,256]{1,0:T(8,128)(2,1)}) %all-gather.2.cloned.1.call-update) | async-done | bytes 33554448 | tf_op jit(solution)/shard_map/all_gather | solution.py:202
  208.0 25.6 %shard_map.55 = bf16[2048,512]{1,0:T(8,128)(2,1)S(1)} custom-call(s32[16]{0:T(128)S(1)} %reshape.157.table, bf16[2048,512]{1,0:T(8,128)(2,1)S(1)} %copy-done.2, bf16[65536,256]{1,0:T(8,128)(2,1)} %all-gather.2.cloned.1.call-done.kv_ref), custom_call_target="tpu_custom_call" | custom-call | flops 8589934592 | bytes 8388608 | tf_op jit(solution)/shard_map/pallas_call | solution.py:105
  233.6 1.3 copy-done.1
  235.0 4.5 %all-to-all-start = ((bf16[8,256,512]{2,1,0:T(8,128)(2,1)}), bf16[8,256,512]{2,1,0:T(8,128)(2,1)S(1)}, u32[]{:S(2)}, u32[]{:S(2)}) async-start(bf16[8,256,512]{2,1,0:T(8,128)(2,1)} %bitcast.30), calls=%async_computation | async-start | bytes 4194304 | tf_op jit(solution)/shard_map/all_to_all | solution.py:207
  239.5 0.1 copy.6
  239.7 8.3 %constant_dynamic-update-slice_fusion = bf16[16,256,2048]{2,1,0:T(8,128)(2,1)} fusion(bf16[16,256,2048]{2,1,0:T(8,128)(2,1)} %get-tuple-element.8, bf16[8,256,2048]{2,1,0:T(8,128)(2,1)} %collective-permute-done.7), kind=kLoop, calls=%fused_computation.18 | loop fusion | bytes 16777216 | tf_op jit(solution)/shard_map/concatenate | solution.py:184
  247.9 13.0 %gather_fusion = bf16[16,256,2048]{2,1,0:T(8,128)(2,1)} fusion(bf16[16,256,2048]{2,1,0:T(8,128)(2,1)} %constant_dynamic-update-slice_fusion, s32[1024]{0:T(1024)S(1)} %pad_clamp_fusion), kind=kCustom, calls=%fused_computation | custom fusion | bytes 33554496 | tf_op jit(solution)/shard_map/gather | solution.py:192
  261.0 5.3 %all-to-all-done.a_ref = bf16[8,256,512]{2,1,0:T(8,128)(2,1)S(1)} async-done(((bf16[8,256,512]{2,1,0:T(8,128)(2,1)}), bf16[8,256,512]{2,1,0:T(8,128)(2,1)S(1)}, u32[]{:S(2)}, u32[]{:S(2)}) %all-to-all-start) | async-done | bytes 2097184 | tf_op jit(solution)/shard_map/all_to_all | solution.py:207
  266.3 5.8 %copy-done = bf16[16,256,2048]{2,1,0:T(8,128)(2,1)S(1)} copy-done((bf16[16,256,2048]{2,1,0:T(8,128)(2,1)S(1)}, bf16[16,256,2048]{2,1,0:T(8,128)(2,1)}, u32[]{:S(2)}) %copy-start) | copy-done | bytes 16777240
  272.0 8.2 %shard_map.56 = bf16[8,256,256]{2,1,0:T(8,128)(2,1)S(1)} custom-call(bf16[8,256,512]{2,1,0:T(8,128)(2,1)S(1)} %all-to-all-done.a_ref, bf16[8,512,2048]{2,1,0:T(8,128)(2,1)S(1)} %bitcast.29), custom_call_target="tpu_custom_call" | custom-call | flops 4294967296 | bytes 20971520 | tf_op jit(solution)/shard_map/pallas_call | solution.py:143
  280.2 22.0 %all_to_all.10 = bf16[8,256,256]{2,1,0:T(8,128)(2,1)S(1)} all-to-all(bf16[8,256,256]{2,1,0:T(8,128)(2,1)S(1)} %shard_map.56), channel_id=1, replica_groups=mesh['ctx'=32,'head'=8] {'head'}, dimensions={0} | all-to-all | bytes 2097152 | tf_op jit(solution)/shard_map/all_to_all | solution.py:211
  302.2 1.0 copy.23
  (22 shorter events, 0.3 us)
Async XLA Ops:
  6.5 201.4 %all-gather.2.cloned.1.call-start = ((), (), s32[]{:S(2)}) async-start(), calls=%async_computation.2 | async-start | bytes 34603008 | tf_op jit(solution)/shard_map/all_gather | solution.py:202
  11.2 41.2 %collective-permute-start.3 = (bf16[256,2048]{1,0:T(8,128)(2,1)S(1)}, bf16[256,2048]{1,0:T(8,128)(2,1)S(1)}, u32[]{:S(2)}, u32[]{:S(2)}) collective-permute-start(bf16[256,2048]{1,0:T(8,128)(2,1)S(1)} %get-tuple-element.6), channel_id=1, source_target_pairs={{0,4},{1,5},{2,6},{3,7},{4,0},{5,1},{6,2},{7,3},{8,12},{9,13},{10,... | collective-permute-start | bytes 3145736 | tf_op jit(solution)/shard_map/ppermute | solution.py:175
  13.3 42.3 %collective-permute-start = (bf16[256,2048]{1,0:T(8,128)(2,1)S(1)}, bf16[256,2048]{1,0:T(8,128)(2,1)S(1)}, u32[]{:S(2)}, u32[]{:S(2)}) collective-permute-start(bf16[256,2048]{1,0:T(8,128)(2,1)S(1)} %get-tuple-element.6), channel_id=1, source_target_pairs={{0,1},{1,2},{2,3},{3,0},{4,5},{5,6},{6,7},{7,4},{8,9},{9,10},{10,1... | collective-permute-start | bytes 3145736 | tf_op jit(solution)/shard_map/ppermute | solution.py:175
  52.4 26.9 %collective-permute-start.5 = (bf16[256,2048]{1,0:T(8,128)(2,1)S(1)}, bf16[256,2048]{1,0:T(8,128)(2,1)S(1)}, u32[]{:S(2)}, u32[]{:S(2)}) collective-permute-start(bf16[256,2048]{1,0:T(8,128)(2,1)S(1)} %collective-permute-done.3), channel_id=1, source_target_pairs={{0,3},{1,0},{2,1},{3,2},{4,7},{5,4},{6,5},{7,6},{8,11},{9,8},{10,9... | collective-permute-start | bytes 3145736 | tf_op jit(solution)/shard_map/ppermute | solution.py:175
  55.7 27.3 %collective-permute-start.1 = (bf16[256,2048]{1,0:T(8,128)(2,1)S(1)}, bf16[256,2048]{1,0:T(8,128)(2,1)S(1)}, u32[]{:S(2)}, u32[]{:S(2)}) collective-permute-start(bf16[256,2048]{1,0:T(8,128)(2,1)S(1)} %collective-permute-done), channel_id=1, source_target_pairs={{0,1},{1,2},{2,3},{3,0},{4,5},{5,6},{6,7},{7,4},{8,9},{9,10},{10,1... | collective-permute-start | bytes 3145736 | tf_op jit(solution)/shard_map/ppermute | solution.py:175
  55.7 46.1 %collective-permute-start.2 = (bf16[256,2048]{1,0:T(8,128)(2,1)S(1)}, bf16[256,2048]{1,0:T(8,128)(2,1)S(1)}, u32[]{:S(2)}, u32[]{:S(2)}) collective-permute-start(bf16[256,2048]{1,0:T(8,128)(2,1)S(1)} %get-tuple-element.6), channel_id=1, source_target_pairs={{0,3},{1,0},{2,1},{3,2},{4,7},{5,4},{6,5},{7,6},{8,11},{9,8},{10,9... | collective-permute-start | bytes 3145736 | tf_op jit(solution)/shard_map/ppermute | solution.py:175
  60.0 45.0 %collective-permute-start.4 = (bf16[256,2048]{1,0:T(8,128)(2,1)S(1)}, bf16[256,2048]{1,0:T(8,128)(2,1)S(1)}, u32[]{:S(2)}, u32[]{:S(2)}) collective-permute-start(bf16[256,2048]{1,0:T(8,128)(2,1)S(1)} %collective-permute-done.3), channel_id=1, source_target_pairs={{0,1},{1,2},{2,3},{3,0},{4,5},{5,6},{6,7},{7,4},{8,9},{9,10},{10,1... | collective-permute-start | bytes 3145736 | tf_op jit(solution)/shard_map/ppermute | solution.py:175
  79.3 40.6 %collective-permute-start.6 = (bf16[256,2048]{1,0:T(8,128)(2,1)S(1)}, bf16[256,2048]{1,0:T(8,128)(2,1)S(1)}, u32[]{:S(2)}, u32[]{:S(2)}) collective-permute-start(bf16[256,2048]{1,0:T(8,128)(2,1)S(1)} %collective-permute-done.5), channel_id=1, source_target_pairs={{0,3},{1,0},{2,1},{3,2},{4,7},{5,4},{6,5},{7,6},{8,11},{9,8},{10,9... | collective-permute-start | bytes 3145736 | tf_op jit(solution)/shard_map/ppermute | solution.py:175
  84.6 38.5 %copy-start.3 = (s32[4,3]{1,0:T(4,128)S(1)}, s32[4,3]{1,0:T(4,128)}, u32[]{:S(2)}) copy-start(s32[4,3]{1,0:T(4,128)} %param.8) | copy-start | bytes 148
  84.6 123.4 %copy-start.2 = (bf16[2048,512]{1,0:T(8,128)(2,1)S(1)}, bf16[2048,512]{1,0:T(8,128)(2,1)}, u32[]{:S(2)}) copy-start(bf16[2048,512]{1,0:T(8,128)(2,1)} %q_ref.1) | copy-start | bytes 6291460
  123.1 116.6 %collective-permute-start.7 = (bf16[8,256,2048]{2,1,0:T(8,128)(2,1)}, bf16[8,256,2048]{2,1,0:T(8,128)(2,1)}, u32[]{:S(2)}, u32[]{:S(2)}) collective-permute-start(bf16[8,256,2048]{2,1,0:T(8,128)(2,1)} %get-tuple-element.7), channel_id=1, source_target_pairs={{0,8},{8,0},{16,24},{24,16},{32,40},{40,32},{48,56},{56,48},{64,72... | collective-permute-start | bytes 25165832 | tf_op jit(solution)/shard_map/ppermute | solution.py:183
  233.6 1.3 copy-start.1
  235.0 31.3 %all-to-all-start = ((bf16[8,256,512]{2,1,0:T(8,128)(2,1)}), bf16[8,256,512]{2,1,0:T(8,128)(2,1)S(1)}, u32[]{:S(2)}, u32[]{:S(2)}) async-start(bf16[8,256,512]{2,1,0:T(8,128)(2,1)} %bitcast.30), calls=%async_computation | async-start | bytes 4194304 | tf_op jit(solution)/shard_map/all_to_all | solution.py:207
  266.3 5.8 %copy-start = (bf16[16,256,2048]{2,1,0:T(8,128)(2,1)S(1)}, bf16[16,256,2048]{2,1,0:T(8,128)(2,1)}, u32[]{:S(2)}) copy-start(bf16[16,256,2048]{2,1,0:T(8,128)(2,1)} %gather_fusion) | copy-start | bytes 50331652
Sparse Core Ops, SparseCore 0:
  9.2 198.7 all-gather.1

commit v2 on v1

v2 whole, which is shorter than its diff:
```python
import functools

import jax
import jax.numpy as jnp
import numpy as np
from jax import lax
from jax.experimental import pallas as pl
from jax.experimental.pallas import tpu as pltpu
from jax.sharding import PartitionSpec as P

HEAD_SIZE = 128
BLOCK_TOKENS = 512
TILE = 256
SLOTS = 4
BLOCKS = 4
ROWS = BLOCKS * BLOCK_TOKENS
RING = 8
CORES = 4 * RING
EXP2_SCALE = HEAD_SIZE ** (-0.5) * 1.4426950408889634

SCHEDULE = (
    (
        (
            0, 1, 2, 3, 4, -1, 6, -1, 8, -1, 10, -1, 12, -1, 14, -1,
            16, 17, 18, 19, 20, -1, 22, -1, 24, -1, 26, -1, 28, -1, -1, -1,
        ),
        (
            -1, 1, -1, 3, -1, 5, -1, 7, -1, 9, -1, 11, -1, 13, -1, 15,
            -1, -1, -1, -1, -1, -1, -1, -1, -1, -1, -1, -1, -1, -1, -1, -1,
        ),
    ),
    (
        (
            1, 0, 3, 2, 5, -1, 7, -1, 9, -1, 11, -1, 13, -1, 15, -1,
            17, 16, 19, 18, 21, -1, 23, -1, 25, -1, 27, -1, 29, -1, -1, -1,
        ),
        (
            -1, 0, -1, 2, -1, 4, -1, 6, -1, 8, -1, 10, -1, 12, -1, 14,
            -1, -1, -1, -1, -1, -1, -1, -1, -1, -1, -1, -1, -1, -1, -1, -1,
        ),
    ),
    (
        (
            -1, 3, 0, -1, 2, -1, 4, -1, 6, -1, 8, -1, 10, -1, -1, 1,
            -1, 1, 16, 3, 18, 5, 20, 7, 22, 9, 24, 11, 26, 13, -1, 15,
        ),
        (
            14, -1, 0, -1, 2, -1, 4, -1, 6, -1, 8, -1, 10, -1, 12, -1,
            -1, -1, -1, -1, -1, -1, -1, -1, -1, -1, -1, -1, -1, -1, -1, -1,
        ),
    ),
    (
        (
            -1, 2, 1, -1, 3, -1, 5, -1, 7, -1, 9, -1, 11, -1, -1, 0,
            -1, 18, 17, 2, 19, 4, 21, 6, 23, 8, 25, 10, 27, 12, -1, 14,
        ),
        (
            15, -1, 1, -1, 3, -1, 5, -1, 7, -1, 9, -1, 11, -1, 13, -1,
            -1, -1, -1, -1, -1, -1, -1, -1, -1, -1, -1, -1, -1, -1, -1, -1,
        ),
    ),
    (
        (
            -1, -1, -1, -1, 0, -1, 2, -1, 4, -1, 6, -1, 8, 1, -1, 3,
            14, 19, -1, 5, 16, 7, 18, 9, 20, 11, 22, 13, 24, 15, 12, 1,
        ),
        (
            -1, -1, -1, -1, 0, -1, 2, -1, 4, -1, 6, -1, 8, -1, 10, -1,
            -1, -1, -1, -1, -1, -1, -1, -1, -1, -1, -1, -1, -1, -1, -1, -1,
        ),
    ),
    (
        (
            -1, -1, -1, -1, 1, -1, 3, -1, 5, -1, 7, -1, 9, 0, -1, 2,
            15, 0, -1, 4, 17, 6, 19, 8, 21, 10, 23, 12, 25, 14, 13, 16,
        ),
        (
            -1, -1, -1, -1, 1, -1, 3, -1, 5, -1, 7, -1, -1, 0, 11, -1,
            -1, -1, -1, -1, -1, -1, -1, -1, -1, -1, -1, -1, -1, -1, -1, -1,
        ),
    ),
    (
        (
            -1, -1, -1, -1, -1, -1, 0, -1, 2, -1, 4, 1, 6, 3, -1, -1,
            12, 5, 14, 7, 0, 9, 16, 11, 18, 13, 20, 15, 22, 1, 10, 19,
        ),
        (
            -1, -1, -1, -1, -1, -1, -1, -1, 2, -1, 4, -1, -1, 3, 8, -1,
            -1, -1, -1, -1, -1, -1, -1, -1, -1, -1, -1, -1, -1, -1, -1, -1,
        ),
    ),
    (
        (
            -1, -1, -1, -1, -1, -1, -1, -1, -1, -1, 5, -1, 7, -1, -1, -1,
            13, 4, 15, 6, -1, 8, 17, 10, 5, 12, 21, 14, 23, 16, 11, 17,
        ),
        (
            -1, -1, -1, -1, -1, -1, 1, -1, 3, -1, -1, 0, 7, -1, 9, -1,
            -1, -1, -1, -1, -1, -1, -1, -1, -1, -1, -1, -1, -1, -1, -1, -1,
        ),
    ),
    (
        (
            -1, -1, -1, -1, -1, -1, -1, -1, -1, -1, -1, -1, 4, -1, -1, -1,
            10, 2, 12, 9, 14, 11, 0, 13, 2, 15, 18, -1, 20, 19, 8, 5,
        ),
        (
            -1, -1, -1, -1, -1, -1, -1, -1, -1, 1, -1, 3, 6, -1, -1, 3,
            -1, -1, -1, -1, -1, -1, -1, -1, -1, -1, -1, -1, -1, -1, -1, -1,
        ),
    ),
    (
        (
            -1, -1, -1, -1, -1, -1, -1, -1, -1, -1, -1, -1, 5, -1, -1, -1,
            -1, 6, -1, -1, -1, -1, -1, -1, 17, -1, 9, -1, 21, -1, -1, 4,
        ),
        (
            -1, -1, -1, -1, -1, -1, -1, -1, -1, -1, -1, -1, -1, 2, 7, -1,
            -1, -1, -1, -1, -1, -1, -1, -1, -1, -1, -1, -1, -1, -1, -1, -1,
        ),
    ),
)
CHECKPOINTS = (5, 7, 9)
COST = 12


def target(way, core):
    if way == 1:
        return core + CORES // 2
    side, place = divmod(core, CORES // 2)
    return side * (CORES // 2) + (place + (2 if core % 2 == 0 else -2)) % (CORES // 2)


def plan():
    found = [{core: "own", core ^ 1: "other"} for core in range(CORES)]
    for step, sends in enumerate(SCHEDULE):
        for way, row in enumerate(sends):
            for core, owner in enumerate(row):
                if owner >= 0:
                    found[target(way, core)].setdefault(owner, (step, way))
    return found


def batches(found):
    out = []
    for number, last in enumerate(CHECKPOINTS):
        first = -2 if number == 0 else CHECKPOINTS[number - 1]
        out.append(
            [
                [
                    owner
                    for owner, place in sorted(held.items())
                    if (owner // 2 < core // 2 or owner == core ^ 1)
                    and first < (-1 if isinstance(place, str) else place[0]) <= last
                ]
                for core, held in enumerate(found)
            ]
        )
    return out


def start_from(refs, numbers, source, first, rows, to, sem):
    for number in numbers:

        @pl.when(source == number)
        def _():
            at = pl.ds(pl.multiple_of(first, BLOCK_TOKENS), rows)
            pltpu.make_async_copy(refs[number].at[at], to, sem).start()


def wait_for(refs, source, rows, to, sem):
    @pl.when(source >= 0)
    def _():
        pltpu.make_async_copy(refs[0].at[pl.ds(0, rows)], to, sem).wait()


def move_kernel(ways, way_base, slots, slot_base, row, want, *refs):
    outs = len(ways) + (2 if slots else 0)
    ins, outs, sems = refs[: -outs - 1], refs[-outs - 1 : -1], refs[-1]

    def block_of(slot, which):
        owner = row[slot_base + 2 * slot]
        block = jnp.where(owner >= 0, want[which * CORES + jnp.maximum(owner, 0)], -1)
        source = jnp.where(block >= 0, row[slot_base + 2 * slot + 1], -1)
        return source, jnp.maximum(block, 0) * BLOCK_TOKENS

    jobs = [(numbers, row[way_base + i], 0, ROWS, outs[i]) for i, numbers in enumerate(ways)]
    for slot, numbers in enumerate(slots):
        for which in range(2):
            source, first = block_of(slot, which)
            jobs.append((numbers, source, first, BLOCK_TOKENS, outs[len(ways) + which].at[slot]))
    for i, (numbers, source, first, rows, to) in enumerate(jobs):
        start_from(ins, numbers, source, first, rows, to, sems.at[i])
    for i, (numbers, source, first, rows, to) in enumerate(jobs):
        wait_for(ins, source, rows, to, sems.at[i])


def move(ways, slots, scalars, arrays, width, after=()):
    out_shapes = [(ROWS, width)] * len(ways[0]) + [(len(slots[0]), BLOCK_TOKENS, width)] * (2 if slots[0] else 0)

    def whole(shape):
        return pl.BlockSpec(shape, lambda *_: (0,) * len(shape))

    return pl.pallas_call(
        functools.partial(move_kernel, *ways, *slots),
        out_shape=[jax.ShapeDtypeStruct(s, arrays[0].dtype) for s in out_shapes],
        grid_spec=pltpu.PrefetchScalarGridSpec(
            num_scalar_prefetch=len(scalars),
            grid=(1,),
            in_specs=[pl.BlockSpec(memory_space=pltpu.HBM)] * (len(arrays) + len(after)),
            out_specs=[whole(s) for s in out_shapes],
            scratch_shapes=[pltpu.SemaphoreType.DMA((len(ways[0]) + 2 * len(slots[0]),))],
        ),
        compiler_params=pltpu.CompilerParams(vmem_limit_bytes=24 * 1024 * 1024),
        cost_estimate=pl.CostEstimate(
            flops=0,
            bytes_accessed=4 * COST * sum(int(np.prod(s)) for s in out_shapes),
            transcendentals=0,
        ),
    )(*scalars, *arrays, *after)


class Plan:
    def __init__(self):
        found = plan()
        groups = batches(found)
        columns = []
        self.ways, self.slots, self.sources = {}, {}, {}

        def number_of(place, sources):
            if place not in sources:
                sources.append(place)
            return sources.index(place)

        def add(table):
            base = sum(c.shape[1] for c in columns)
            columns.append(table.reshape(CORES, -1))
            return base

        for step in range(1, len(SCHEDULE)):
            sources, numbers = self.sources.setdefault(step, []), []
            table = np.full((CORES, 2), -1, np.int32)
            for way in range(2):
                used = set()
                for core, owner in enumerate(SCHEDULE[step][way]):
                    if owner >= 0:
                        table[core, way] = number_of(found[core][owner], sources)
                        used.add(int(table[core, way]))
                numbers.append(tuple(sorted(used)))
            self.ways[step] = (tuple(numbers), add(table))

        held = np.full((CORES, CORES, 2), -1, np.int32)
        for batch, group in enumerate(groups):
            depth = max(len(owners) for owners in group)
            step = CHECKPOINTS[batch] + 2
            sources, numbers = self.sources.setdefault(step, []), [set() for _ in range(depth)]
            table = np.full((CORES, depth, 2), -1, np.int32)
            for core, owners in enumerate(group):
                for slot, owner in enumerate(owners):
                    held[core, owner] = (batch, slot)
                    table[core, slot] = owner, number_of(found[core][owner], sources)
                    numbers[slot].add(int(table[core, slot, 1]))
            self.slots[step] = (tuple(tuple(sorted(n)) for n in numbers), add(table))
        place = held.copy()
        for core in range(CORES):
            for owner in range(CORES):
                if held[core, owner, 0] < 0 <= held[core ^ 1, owner, 0]:
                    place[core, owner] = held[core ^ 1, owner]
                    place[core, owner, 0] += len(CHECKPOINTS)
        self.place = add(place)
        self.table = np.concatenate(columns, axis=1)


SWAP = [(i, i ^ 1) for i in range(CORES)]


def exchange(kv, selected, other_selected, index):
    tables = Plan()
    row = jnp.asarray(tables.table)[index]
    arrived = {"own": kv, "other": lax.ppermute(kv, "ctx", SWAP)}

    def pairs(step, way):
        return [(a, target(way, a)) for a, owner in enumerate(SCHEDULE[step][way]) if owner >= 0]

    choices = jnp.stack([selected.reshape(-1), other_selected.reshape(-1)])[:, None, :]
    owner = jnp.arange(CORES, dtype=jnp.int32)[None, :, None]
    named = (choices >= 0) & (choices // BLOCKS == owner)
    want = jnp.max(jnp.where(named, choices % BLOCKS, -1), axis=2).reshape(-1)

    kept, passed = [], []
    for step in range(CHECKPOINTS[-1] + 3):
        none = ((), 0)
        ways, slots = tables.ways.get(step, none), tables.slots.get(step, none)
        if step == 0:
            buffers = [kv, kv]
        elif ways[0] or slots[0]:
            buffers = move(
                ways,
                slots,
                [row, want],
                [arrived[key] for key in tables.sources[step]],
                kv.shape[1],
                after=buffers[:1] if ways[0] else passed,
            )
        else:
            continue
        if step < len(SCHEDULE):
            for way in range(2):
                arrived[step, way] = lax.ppermute(buffers[way], "ctx", pairs(step, way))
        if slots[0]:
            keep, give = buffers[-2:]
            kept.append(keep)
            passed.append(lax.ppermute(give, "ctx", SWAP))
    return kept + passed, row, tables.place


def attention_kernel(q_heads, sources, place, info, row_ref, q_ref, kv_ref, *refs):
    chosen, (o_ref, keys, values, sems) = refs[:sources], refs[sources:]
    step = pl.program_id(0)
    steps = pl.num_programs(0)
    here = lax.rem(step, 2)
    own_to = pl.ds((SLOTS - 1) * BLOCK_TOKENS, BLOCK_TOKENS)

    def pair(block_ref, to, buf, slot):
        return (
            pltpu.make_async_copy(
                block_ref.at[:, pl.ds(0, HEAD_SIZE)], keys.at[buf, to], sems.at[buf, slot, 0]
            ),
            pltpu.make_async_copy(
                block_ref.at[:, pl.ds(HEAD_SIZE, HEAD_SIZE)],
                values.at[buf, to, pl.ds(0, HEAD_SIZE)],
                sems.at[buf, slot, 1],
            ),
        )

    def own_rows(at):
        return kv_ref.at[pl.ds(pl.multiple_of(at * BLOCK_TOKENS, BLOCK_TOKENS), BLOCK_TOKENS)]

    def choice(at, slot):
        block = info[at * (SLOTS - 1) + slot]
        owner = jnp.maximum(block, 0) // BLOCKS
        return jnp.where(block < 0, -1, row_ref[place + 2 * owner]), row_ref[place + 2 * owner + 1]

    def start(at, buf):
        for copy in pair(own_rows(at), own_to, buf, SLOTS - 1):
            copy.start()
        for slot in range(SLOTS - 1):
            to = pl.ds(slot * BLOCK_TOKENS, BLOCK_TOKENS)
            array, block = choice(at, slot)
            for number in range(sources):

                @pl.when(array == number)
                def _():
                    for copy in pair(chosen[number].at[block], to, buf, slot):
                        copy.start()

    @pl.when(step == 0)
    def _():
        start(step, here)

    @pl.when(step + 1 < steps)
    def _():
        start(step + 1, 1 - here)

    values[here, :, pl.ds(HEAD_SIZE, HEAD_SIZE)] = jnp.ones(
        (SLOTS * BLOCK_TOKENS, HEAD_SIZE), jnp.bfloat16
    )
    for copy in pair(own_rows(step), own_to, here, SLOTS - 1):
        copy.wait()
    for slot in range(SLOTS - 1):
        to = pl.ds(slot * BLOCK_TOKENS, BLOCK_TOKENS)
        array, _ = choice(step, slot)

        @pl.when(array >= 0)
        def _():
            for copy in pair(own_rows(step), to, here, slot):
                copy.wait()

        @pl.when(array < 0)
        def _():
            first = keys[here, pl.ds((SLOTS - 1) * BLOCK_TOKENS, 16), :][0:1, :]
            keys[here, to, :] = jnp.broadcast_to(first, (BLOCK_TOKENS, HEAD_SIZE))
            values[here, to, :] = jnp.zeros((BLOCK_TOKENS, 2 * HEAD_SIZE), jnp.bfloat16)

    row = lax.broadcasted_iota(jnp.int32, (TILE, TILE), 0)
    col = lax.broadcasted_iota(jnp.int32, (TILE, TILE), 1)
    causal = row >= col
    dims = (((1,), (1,)), ((), ()))

    for head in range(q_heads):
        lanes = pl.ds(head * HEAD_SIZE, HEAD_SIZE)
        for tile in range(BLOCK_TOKENS // TILE):
            rows = pl.ds(tile * TILE, TILE)
            full = (SLOTS - 1) * BLOCK_TOKENS + tile * TILE
            query = q_ref[rows, lanes]
            far = lax.dot_general(
                query, keys[here, pl.ds(0, full), :], dims, preferred_element_type=jnp.float32
            )
            near = lax.dot_general(
                query, keys[here, pl.ds(full, TILE), :], dims, preferred_element_type=jnp.float32
            )
            near = jnp.where(causal, near, -1e30)
            highest = jnp.maximum(
                jnp.max(far, axis=1, keepdims=True), jnp.max(near, axis=1, keepdims=True)
            )
            far = jnp.exp2((far - highest) * EXP2_SCALE).astype(jnp.bfloat16)
            near = jnp.exp2((near - highest) * EXP2_SCALE).astype(jnp.bfloat16)
            total = jnp.dot(
                far, values[here, pl.ds(0, full), :], preferred_element_type=jnp.float32
            ) + jnp.dot(
                near, values[here, pl.ds(full, TILE), :], preferred_element_type=jnp.float32
            )
            o_ref[rows, lanes] = (total[:, :HEAD_SIZE] / total[:, HEAD_SIZE:]).astype(jnp.bfloat16)


def attention(queries, kv, chosen, info, row, place):
    rows, width = queries.shape
    blocks = rows // BLOCK_TOKENS
    keys = SLOTS * BLOCK_TOKENS
    return pl.pallas_call(
        functools.partial(attention_kernel, width // HEAD_SIZE, len(chosen), place),
        out_shape=jax.ShapeDtypeStruct((rows, width), jnp.bfloat16),
        grid_spec=pltpu.PrefetchScalarGridSpec(
            num_scalar_prefetch=2,
            grid=(blocks,),
            in_specs=[pl.BlockSpec((BLOCK_TOKENS, width), lambda i, *_: (i, 0))]
            + [pl.BlockSpec(memory_space=pltpu.HBM)] * (1 + len(chosen)),
            out_specs=pl.BlockSpec((BLOCK_TOKENS, width), lambda i, *_: (i, 0)),
            scratch_shapes=[
                pltpu.VMEM((2, keys, HEAD_SIZE), jnp.bfloat16),
                pltpu.VMEM((2, keys, 2 * HEAD_SIZE), jnp.bfloat16),
                pltpu.SemaphoreType.DMA((2, SLOTS, 2)),
            ],
        ),
        compiler_params=pltpu.CompilerParams(
            dimension_semantics=("arbitrary",), vmem_limit_bytes=48 * 1024 * 1024
        ),
        cost_estimate=pl.CostEstimate(
            flops=4 * rows * (width // HEAD_SIZE) * keys * HEAD_SIZE,
            bytes_accessed=4 * rows * width + 4 * blocks * keys * HEAD_SIZE,
            transcendentals=rows * (width // HEAD_SIZE) * keys,
        ),
    )(info, row, queries, kv, *chosen)


def project_kernel(parts, depth, core, a_ref, mine_ref, other_ref, o_ref):
    first = pl.ds(pl.multiple_of(core[0] * depth, depth), depth)
    second = pl.ds(pl.multiple_of((1 - core[0]) * depth, depth), depth)
    total = jnp.zeros(o_ref.shape[1:], jnp.float32)
    for part in range(parts):
        total += jnp.dot(a_ref[part, :, first], mine_ref[part], preferred_element_type=jnp.float32)
        total += jnp.dot(a_ref[part, :, second], other_ref[part], preferred_element_type=jnp.float32)
    o_ref[0] = total.astype(jnp.bfloat16)


def project(attended, mine, other, core):
    parts, rows, features = attended.shape
    depth = mine.shape[1]
    columns = mine.shape[2] // parts
    return pl.pallas_call(
        functools.partial(project_kernel, parts, depth),
        out_shape=jax.ShapeDtypeStruct((parts, rows, columns), jnp.bfloat16),
        grid_spec=pltpu.PrefetchScalarGridSpec(
            num_scalar_prefetch=1,
            grid=(parts,),
            in_specs=[
                pl.BlockSpec((parts, rows, features), lambda i, t: (0, 0, 0)),
                pl.BlockSpec((parts, depth, columns), lambda i, t: (0, 0, i)),
                pl.BlockSpec((parts, depth, columns), lambda i, t: (0, 0, i)),
            ],
            out_specs=pl.BlockSpec((1, rows, columns), lambda i, t: (i, 0, 0)),
        ),
        compiler_params=pltpu.CompilerParams(
            dimension_semantics=("arbitrary",), vmem_limit_bytes=32 * 1024 * 1024
        ),
        cost_estimate=pl.CostEstimate(
            flops=2 * parts * parts * rows * features * columns,
            bytes_accessed=2 * parts * parts * features * columns + 4 * parts * rows * features,
            transcendentals=0,
        ),
    )(core, attended, mine, other)


def gather_weight(out_weight, core):
    half = out_weight.shape[0] // 2
    mine = lax.dynamic_slice_in_dim(out_weight, core * half, half, 0)
    groups = [
        [((side ^ x_hi) * (CORES // 2) + rest) * 8 + x_hi * 4 + y for x_hi in range(2) for y in range(4)]
        for side in range(2)
        for rest in range(CORES // 2)
    ]
    return lax.all_gather(mine, ("ctx", "head"), axis=0, axis_index_groups=groups)


def per_device(queries, key_state_matrix, value_state_matrix, selected, out_weight):
    head_count = lax.axis_size("head")
    index = lax.axis_index("ctx")
    core = index % 2
    rows, width = queries.shape
    kv = jnp.concatenate([key_state_matrix, value_state_matrix], axis=1)
    other_selected = lax.ppermute(selected, "ctx", SWAP)
    mine = gather_weight(out_weight, core)
    chosen, row, place = exchange(kv, selected, other_selected, index)
    mine, chosen[-1] = lax.optimization_barrier((mine, chosen[-1]))
    other = lax.ppermute(mine, "ctx", SWAP)
    attended = attention(queries, kv, chosen, selected.reshape(-1), row, place)
    tokens = lax.all_to_all(
        attended.reshape(head_count, rows // head_count, width), "head", 0, 0, tiled=True
    )
    mixed = project(tokens, mine, other, core[None])
    return lax.all_to_all(mixed, "head", 0, 0, tiled=True).reshape(rows, -1)


def solution(mesh):
    return jax.shard_map(
        per_device,
        mesh=mesh,
        in_specs=(
            P("ctx", "head"),
            P("ctx", "head"),
            P("ctx", "head"),
            P("ctx", None),
            P("head", None),
        ),
        out_specs=P("ctx", "head"),
        check_vma=False,
    )
```

time: 312 us -> 251 us (0.80)
  waiting for transfers between devices: 176 us -> 77.3 us
  blocking collectives: 22 us -> 54.7 us
  local copies, waits for them, and re-layouts: 44.2 us -> 15.4 us
  starting transfers between devices: 18.4 us -> 43 us
  Pallas kernels: 33.8 us -> 45.8 us
    all_gather x1, waiting for transfers between devices: 84.7 us -> 0.01 us  [gather_weight(): lax.all_gather(mine, ('ctx', 'head'), axis=0, axis_index_groups=groups)]
    all_to_all x0 -> x1, blocking collectives: none -> 34.9 us  [per_device(): lax.all_to_all(attended.reshape(head_count, rows // head_count, width), '...]
    ppermute x8 -> x26, starting transfers between devices: 13.9 us -> 43 us  [the longest x20 36.3 us: exchange(): arrived[step, way] = lax.ppermute(buffers[way], 'ctx', pairs(step, way))]
    gather x1 -> x0, local copies, waits for them, and re-layouts: 13 us -> none  [gather_weight(): return both[order].reshape(8, 2 * half, out_weight.shape[1])]
    pallas_call x2 -> x12, Pallas kernels: 33.8 us -> 45.8 us  [the longest x1 27.9 us: attention(): pl.pallas_call(functools.partial(attention_kernel, width // HEAD_SIZE, le...]
    unnamed x17 -> x36, local copies, waits for them, and re-layouts: 21 us -> 12.2 us
    ppermute x8 -> x26, waiting for transfers between devices: 85.7 us -> 77.2 us  [the longest x20 74.9 us: exchange(): arrived[step, way] = lax.ppermute(buffers[way], 'ctx', pairs(step, way))]
    concatenate x1, local copies, waits for them, and re-layouts: 8.27 us -> 0.83 us  [per_device(): kv = jnp.concatenate([key_state_matrix, value_state_matrix], axis=1)]
  transfers between devices with their start and end apart: 10 -> 27, of which waited for: 6 -> 15; matrix products, arithmetic and copies ran while one was open for 12% -> 1% of each run, Pallas kernels for 8% -> 14%
where the time goes in v2:
time: 251 us; the launch traced here: 250 us
  waiting for transfers between devices  77.3 us (31%)
  blocking collectives  54.7 us (22%)
  Pallas kernels  45.8 us (18%)
  starting transfers between devices  43 us (17%)
  local copies, waits for them, and re-layouts  15.4 us (6%)
  between operations  13.8 us (5%)
    ppermute x20, waiting for transfers between devices, exchange(): arrived[step, way] = lax.ppermute(buffers[way], 'ctx', pairs(step, way))  74.9 us
    ppermute x20, starting transfers between devices, exchange(): arrived[step, way] = lax.ppermute(buffers[way], 'ctx', pairs(step, way))  36.3 us
    all_to_all x1, blocking collectives, per_device(): lax.all_to_all(attended.reshape(head_count, rows // head_count, width), '...  34.9 us
    pallas_call x1, Pallas kernels, attention(): pl.pallas_call(functools.partial(attention_kernel, width // HEAD_SIZE, le...  27.9 us
    all_to_all x1, blocking collectives, per_device(): return lax.all_to_all(mixed, 'head', 0, 0, tiled=True).reshape(rows, -1)  19.8 us
    unnamed x36, local copies, waits for them, and re-layouts  12.2 us
    pallas_call x1, Pallas kernels, project(): pl.pallas_call(functools.partial(project_kernel, parts, depth), out_shape...  9.57 us
    pallas_call x10, Pallas kernels, move(): pl.pallas_call(functools.partial(move_kernel, *ways, *slots), out_shape=[...  8.35 us
  transfers between devices with their start and end apart: 27, of which 15 were waited for; matrix products, arithmetic and copies ran while one was open for 1% of the time, Pallas kernels for 14%

profile of v2, /device:TPU:226, one launch (start us, length us, event | category | flops | bytes accessed | tf_op | source)
XLA Modules:
  0.0 250.2 jit_solution(18281438065626121703)
XLA Ops:
  6.6 1.5 copy-done
  16.1 1.3 collective-permute-start.2
  18.2 9.6 %collective-permute-done.4.refs_0_.refs_2_ = bf16[2048,256]{1,0:T(8,128)(2,1)S(1)} collective-permute-done((bf16[2048,256]{1,0:T(8,128)(2,1)}, bf16[2048,256]{1,0:T(8,128)(2,1)S(1)}, u32[]{:S(2)}, u32[]{:S(2)}) %collective-permute-start.4) | collective-permute-done | bytes 1048608 | tf_op jit(solution)/shard_map/ppermute | solution.py:309
  28.4 1.3 collective-permute-start.8
  29.7 1.3 collective-permute-start.9
  31.0 8.0 %collective-permute-done.2.refs_0_.refs_3_.refs_4_ = bf16[2048,256]{1,0:T(8,128)(2,1)S(1)} collective-permute-done((bf16[2048,256]{1,0:T(8,128)(2,1)S(1)}, bf16[2048,256]{1,0:T(8,128)(2,1)S(1)}, u32[]{:S(2)}, u32[]{:S(2)}) %collective-permute-start.2) | collective-permute-done | bytes 1048608 | tf_op jit(solution)/shard_map/ppermute | solution.py:309
  39.6 1.3 collective-permute-start.6
  40.9 1.3 collective-permute-start.7
  42.2 8.0 %collective-permute-done.8.refs_0_.refs_5_.refs_4_ = bf16[2048,256]{1,0:T(8,128)(2,1)S(1)} collective-permute-done((bf16[2048,256]{1,0:T(8,128)(2,1)S(1)}, bf16[2048,256]{1,0:T(8,128)(2,1)S(1)}, u32[]{:S(2)}, u32[]{:S(2)}) %collective-permute-start.8) | collective-permute-done | bytes 1048608 | tf_op jit(solution)/shard_map/ppermute | solution.py:309
  51.7 5.5 %collective-permute-start.12 = (bf16[2048,256]{1,0:T(8,128)(2,1)S(1)}, bf16[2048,256]{1,0:T(8,128)(2,1)S(1)}, u32[]{:S(2)}, u32[]{:S(2)}) collective-permute-start(bf16[2048,256]{1,0:T(8,128)(2,1)S(1)} %get-tuple-element.37.refs_4_), channel_id=1, source_target_pairs={{32,48},{48,64},{64,80},{80,96},{96,112},{104,88},{120,104},{128,1... | collective-permute-start | bytes 3145736 | tf_op jit(solution)/shard_map/ppermute | solution.py:309
  58.5 2.9 %collective-permute-done.6.refs_0_.refs_6_.refs_1_ = bf16[2048,256]{1,0:T(8,128)(2,1)S(1)} collective-permute-done((bf16[2048,256]{1,0:T(8,128)(2,1)S(1)}, bf16[2048,256]{1,0:T(8,128)(2,1)S(1)}, u32[]{:S(2)}, u32[]{:S(2)}) %collective-permute-start.6) | collective-permute-done | bytes 1048608 | tf_op jit(solution)/shard_map/ppermute | solution.py:309
  63.0 5.6 %collective-permute-start.10 = (bf16[2048,256]{1,0:T(8,128)(2,1)S(1)}, bf16[2048,256]{1,0:T(8,128)(2,1)S(1)}, u32[]{:S(2)}, u32[]{:S(2)}) collective-permute-start(bf16[2048,256]{1,0:T(8,128)(2,1)S(1)} %get-tuple-element.38.refs_2_), channel_id=1, source_target_pairs={{32,48},{48,64},{64,80},{80,96},{96,112},{104,88},{120,104},{128,1... | collective-permute-start | bytes 3145736 | tf_op jit(solution)/shard_map/ppermute | solution.py:309
  69.9 2.8 %collective-permute-done.12.refs_0_.refs_7_.refs_3_ = bf16[2048,256]{1,0:T(8,128)(2,1)S(1)} collective-permute-done((bf16[2048,256]{1,0:T(8,128)(2,1)S(1)}, bf16[2048,256]{1,0:T(8,128)(2,1)S(1)}, u32[]{:S(2)}, u32[]{:S(2)}) %collective-permute-start.12) | collective-permute-done | bytes 1048608 | tf_op jit(solution)/shard_map/ppermute | solution.py:309
  74.6 1.9 collective-permute-start.15
  77.8 6.1 %collective-permute-done.10.refs_0_.refs_2_ = bf16[2048,256]{1,0:T(8,128)(2,1)S(1)} collective-permute-done((bf16[2048,256]{1,0:T(8,128)(2,1)S(1)}, bf16[2048,256]{1,0:T(8,128)(2,1)S(1)}, u32[]{:S(2)}, u32[]{:S(2)}) %collective-permute-start.10) | collective-permute-done | bytes 1048608 | tf_op jit(solution)/shard_map/ppermute | solution.py:309
  84.0 1.4 collective-permute-done.11.refs_1_
  85.3 2.2 shard_map.70
  87.5 1.5 copy-done.5
  89.0 5.3 %collective-permute-start.22 = (bf16[11,512,256]{2,1,0:T(8,128)(2,1)S(1)}, bf16[11,512,256]{2,1,0:T(8,128)(2,1)S(1)}, u32[]{:S(2)}, u32[]{:S(2)}) collective-permute-start(bf16[11,512,256]{2,1,0:T(8,128)(2,1)S(1)} %get-tuple-element.51), channel_id=1, source_target_pairs={{0,8},{8,0},{16,24},{24,16},{32,40},{40,32},{48,56},{56,48},{64,72... | collective-permute-start | bytes 8650760 | tf_op jit(solution)/shard_map/ppermute | solution.py:313
  94.4 3.7 %collective-permute-start.14 = (bf16[2048,256]{1,0:T(8,128)(2,1)S(1)}, bf16[2048,256]{1,0:T(8,128)(2,1)S(1)}, u32[]{:S(2)}, u32[]{:S(2)}) collective-permute-start(bf16[2048,256]{1,0:T(8,128)(2,1)S(1)} %get-tuple-element.43.refs_5_), channel_id=1, source_target_pairs={{80,96},{96,112},{128,144},{136,248},{144,160},{152,136},{168,152}... | collective-permute-start | bytes 3145736 | tf_op jit(solution)/shard_map/ppermute | solution.py:309
  100.0 1.9 collective-permute-start.18
  102.7 8.3 %collective-permute-done.14.refs_0_ = bf16[2048,256]{1,0:T(8,128)(2,1)S(1)} collective-permute-done((bf16[2048,256]{1,0:T(8,128)(2,1)S(1)}, bf16[2048,256]{1,0:T(8,128)(2,1)S(1)}, u32[]{:S(2)}, u32[]{:S(2)}) %collective-permute-start.14) | collective-permute-done | bytes 1048608 | tf_op jit(solution)/shard_map/ppermute | solution.py:309
  111.0 9.4 %collective-permute-done.16.refs_4_ = bf16[2048,256]{1,0:T(8,128)(2,1)S(1)} collective-permute-done((bf16[2048,256]{1,0:T(8,128)(2,1)S(1)}, bf16[2048,256]{1,0:T(8,128)(2,1)S(1)}, u32[]{:S(2)}, u32[]{:S(2)}) %collective-permute-start.16) | collective-permute-done | bytes 1048608 | tf_op jit(solution)/shard_map/ppermute | solution.py:309
  125.0 14.0 %collective-permute-done.19.refs_1_ = bf16[2048,256]{1,0:T(8,128)(2,1)S(1)} collective-permute-done((bf16[2048,256]{1,0:T(8,128)(2,1)S(1)}, bf16[2048,256]{1,0:T(8,128)(2,1)S(1)}, u32[]{:S(2)}, u32[]{:S(2)}) %collective-permute-start.19) | collective-permute-done | bytes 1048608 | tf_op jit(solution)/shard_map/ppermute | solution.py:309
  139.0 1.3 collective-permute-done.21.refs_3_
  142.8 2.3 collective-permute-done.24.refs_5_
  146.3 1.4 copy-done.7
  147.7 1.3 copy-done.9
  150.1 27.9 %shard_map.74 = bf16[2048,512]{1,0:T(8,128)(2,1)} custom-call(s32[12]{0:T(128)S(1)} %reshape.172.info, s32[118]{0:T(128)S(1)} %dynamic-slice_bitcast_fusion.row.row_ref, bf16[2048,512]{1,0:T(8,128)(2,1)} %q_ref.1, bf16[2048,256]{1,0:T(8,128)(2,1)} %constant_dynamic-update-slice_fusion.refs_1_.kv_ref, bf16[11,512,256]{2,1,0:T(8,128)(2,1)} %copy-done.5, ...), custom_call_target="tpu_custom_call" | custom-call | flops 8589934592 | bytes 8388608 | tf_op jit(solution)/shard_map/pallas_call | solution.py:420
  178.0 34.9 %all_to_all.10.a_ref = bf16[8,256,512]{2,1,0:T(8,128)(2,1)S(1)} all-to-all(bf16[8,256,512]{2,1,0:T(8,128)(2,1)} %bitcast.11), channel_id=1, replica_groups=mesh['ctx'=32,'head'=8] {'head'}, dimensions={0} | all-to-all | bytes 4194304 | tf_op jit(solution)/shard_map/all_to_all | solution.py:507
  213.0 9.6 %shard_map.75 = bf16[8,256,256]{2,1,0:T(8,128)(2,1)S(1)} custom-call(s32[1]{0:T(128)} %bitcast.core, bf16[8,256,512]{2,1,0:T(8,128)(2,1)S(1)} %all_to_all.10.a_ref, bf16[8,256,2048]{2,1,0:T(8,128)(2,1)S(1)} %bitcast.9, bf16[8,256,2048]{2,1,0:T(8,128)(2,1)} %collective-permute-done.25.other_ref), custom_call_target="tpu_custom_call" | custom-call | flops 4294967296 | bytes 20971520 | tf_op jit(solution)/shard_map/pallas_call | solution.py:460
  222.6 19.8 %all_to_all.11 = bf16[8,256,256]{2,1,0:T(8,128)(2,1)S(1)} all-to-all(bf16[8,256,256]{2,1,0:T(8,128)(2,1)S(1)} %shard_map.75), channel_id=1, replica_groups=mesh['ctx'=32,'head'=8] {'head'}, dimensions={0} | all-to-all | bytes 2097152 | tf_op jit(solution)/shard_map/all_to_all | solution.py:511
  (87 shorter events, 31.6 us)
Async XLA Ops:
  6.5 139.5 %all-gather.3.cloned.1.call-start = ((), (), s32[]{:S(2)}) async-start(), calls=%async_computation.2 | async-start | bytes 9437184 | tf_op jit(solution)/shard_map/all_gather | solution.py:492
  10.9 4.6 %collective-permute-start.1 = (bf16[2048,256]{1,0:T(8,128)(2,1)}, bf16[2048,256]{1,0:T(8,128)(2,1)S(1)}, u32[]{:S(2)}, u32[]{:S(2)}) collective-permute-start(bf16[2048,256]{1,0:T(8,128)(2,1)} %constant_dynamic-update-slice_fusion.refs_1_.kv_ref), channel_id=1, source_target_pairs={{0,8},{8,0},{16,24},{24,16},{32,40},{40,32},{48,56},{56,48},{64,72... | collective-permute-start | bytes 3145736 | tf_op jit(solution)/shard_map/ppermute | solution.py:280
  10.9 16.9 %collective-permute-start.4 = (bf16[2048,256]{1,0:T(8,128)(2,1)}, bf16[2048,256]{1,0:T(8,128)(2,1)S(1)}, u32[]{:S(2)}, u32[]{:S(2)}) collective-permute-start(bf16[2048,256]{1,0:T(8,128)(2,1)} %constant_dynamic-update-slice_fusion.refs_1_.kv_ref), channel_id=1, source_target_pairs={{0,16},{8,120},{16,32},{24,8},{32,48},{48,64},{64,80},{80,96},{96,... | collective-permute-start | bytes 3145736 | tf_op jit(solution)/shard_map/ppermute | solution.py:309
  12.2 15.6 %collective-permute-start.5 = (bf16[2048,256]{1,0:T(8,128)(2,1)}, bf16[2048,256]{1,0:T(8,128)(2,1)S(1)}, u32[]{:S(2)}, u32[]{:S(2)}) collective-permute-start(bf16[2048,256]{1,0:T(8,128)(2,1)} %constant_dynamic-update-slice_fusion.refs_1_.kv_ref), channel_id=1, source_target_pairs={{8,136},{24,152},{40,168},{56,184},{72,200},{88,216},{104,232},{12... | collective-permute-start | bytes 3145736 | tf_op jit(solution)/shard_map/ppermute | solution.py:309
  12.9 2.0 collective-permute-start
  15.5 12.3 %copy-start.2 = (bf16[2048,256]{1,0:T(8,128)(2,1)}, bf16[2048,256]{1,0:T(8,128)(2,1)S(1)}, u32[]{:S(2)}) copy-start(bf16[2048,256]{1,0:T(8,128)(2,1)S(1)} %collective-permute-done.1.refs_0_.refs_3_) | copy-start | bytes 3145732
  16.1 22.9 %collective-permute-start.2 = (bf16[2048,256]{1,0:T(8,128)(2,1)S(1)}, bf16[2048,256]{1,0:T(8,128)(2,1)S(1)}, u32[]{:S(2)}, u32[]{:S(2)}) collective-permute-start(bf16[2048,256]{1,0:T(8,128)(2,1)S(1)} %get-tuple-element.31.refs_2_), channel_id=1, source_target_pairs={{0,16},{8,120},{16,32},{24,8},{32,48},{48,64},{64,80},{80,96},{96,... | collective-permute-start | bytes 3145736 | tf_op jit(solution)/shard_map/ppermute | solution.py:309
  17.4 21.6 %collective-permute-start.3 = (bf16[2048,256]{1,0:T(8,128)(2,1)S(1)}, bf16[2048,256]{1,0:T(8,128)(2,1)S(1)}, u32[]{:S(2)}, u32[]{:S(2)}) collective-permute-start(bf16[2048,256]{1,0:T(8,128)(2,1)S(1)} %get-tuple-element.32), channel_id=1, source_target_pairs={{8,136},{24,152},{40,168},{56,184},{72,200},{88,216},{104,232},{12... | collective-permute-start | bytes 3145736 | tf_op jit(solution)/shard_map/ppermute | solution.py:309
  28.4 21.9 %collective-permute-start.8 = (bf16[2048,256]{1,0:T(8,128)(2,1)S(1)}, bf16[2048,256]{1,0:T(8,128)(2,1)S(1)}, u32[]{:S(2)}, u32[]{:S(2)}) collective-permute-start(bf16[2048,256]{1,0:T(8,128)(2,1)S(1)} %get-tuple-element.33.refs_2_), channel_id=1, source_target_pairs={{8,120},{16,32},{32,48},{48,64},{64,80},{80,96},{96,112},{120,104}... | collective-permute-start | bytes 3145736 | tf_op jit(solution)/shard_map/ppermute | solution.py:309
  29.7 21.4 %collective-permute-start.9 = (bf16[2048,256]{1,0:T(8,128)(2,1)S(1)}, bf16[2048,256]{1,0:T(8,128)(2,1)S(1)}, u32[]{:S(2)}, u32[]{:S(2)}) collective-permute-start(bf16[2048,256]{1,0:T(8,128)(2,1)S(1)} %get-tuple-element.36), channel_id=1, source_target_pairs={{0,128},{16,144},{32,160},{48,176},{64,192},{80,208},{96,224},{112... | collective-permute-start | bytes 3145736 | tf_op jit(solution)/shard_map/ppermute | solution.py:309
  39.6 21.9 %collective-permute-start.6 = (bf16[2048,256]{1,0:T(8,128)(2,1)S(1)}, bf16[2048,256]{1,0:T(8,128)(2,1)S(1)}, u32[]{:S(2)}, u32[]{:S(2)}) collective-permute-start(bf16[2048,256]{1,0:T(8,128)(2,1)S(1)} %get-tuple-element.34.refs_3_), channel_id=1, source_target_pairs={{8,120},{16,32},{32,48},{48,64},{64,80},{80,96},{96,112},{120,104}... | collective-permute-start | bytes 3145736 | tf_op jit(solution)/shard_map/ppermute | solution.py:309
  40.9 21.4 %collective-permute-start.7 = (bf16[2048,256]{1,0:T(8,128)(2,1)S(1)}, bf16[2048,256]{1,0:T(8,128)(2,1)S(1)}, u32[]{:S(2)}, u32[]{:S(2)}) collective-permute-start(bf16[2048,256]{1,0:T(8,128)(2,1)S(1)} %get-tuple-element.35), channel_id=1, source_target_pairs={{0,128},{16,144},{32,160},{48,176},{64,192},{80,208},{96,224},{112... | collective-permute-start | bytes 3145736 | tf_op jit(solution)/shard_map/ppermute | solution.py:309
  51.7 21.0 %collective-permute-start.12 = (bf16[2048,256]{1,0:T(8,128)(2,1)S(1)}, bf16[2048,256]{1,0:T(8,128)(2,1)S(1)}, u32[]{:S(2)}, u32[]{:S(2)}) collective-permute-start(bf16[2048,256]{1,0:T(8,128)(2,1)S(1)} %get-tuple-element.37.refs_4_), channel_id=1, source_target_pairs={{32,48},{48,64},{64,80},{80,96},{96,112},{104,88},{120,104},{128,1... | collective-permute-start | bytes 3145736 | tf_op jit(solution)/shard_map/ppermute | solution.py:309
  57.2 16.7 %collective-permute-start.13 = (bf16[2048,256]{1,0:T(8,128)(2,1)S(1)}, bf16[2048,256]{1,0:T(8,128)(2,1)S(1)}, u32[]{:S(2)}, u32[]{:S(2)}) collective-permute-start(bf16[2048,256]{1,0:T(8,128)(2,1)S(1)} %get-tuple-element.40), channel_id=1, source_target_pairs={{32,160},{48,176},{64,192},{80,208},{96,224},{112,240},{33,161},{4... | collective-permute-start | bytes 3145736 | tf_op jit(solution)/shard_map/ppermute | solution.py:309
  63.0 22.3 %copy-start.3 = (bf16[2048,256]{1,0:T(8,128)(2,1)S(1)}, bf16[2048,256]{1,0:T(8,128)(2,1)}, u32[]{:S(2)}) copy-start(bf16[2048,256]{1,0:T(8,128)(2,1)} %copy-done.2) | copy-start | bytes 3145732
  63.0 21.0 %collective-permute-start.10 = (bf16[2048,256]{1,0:T(8,128)(2,1)S(1)}, bf16[2048,256]{1,0:T(8,128)(2,1)S(1)}, u32[]{:S(2)}, u32[]{:S(2)}) collective-permute-start(bf16[2048,256]{1,0:T(8,128)(2,1)S(1)} %get-tuple-element.38.refs_2_), channel_id=1, source_target_pairs={{32,48},{48,64},{64,80},{80,96},{96,112},{104,88},{120,104},{128,1... | collective-permute-start | bytes 3145736 | tf_op jit(solution)/shard_map/ppermute | solution.py:309
  68.6 16.7 %collective-permute-start.11 = (bf16[2048,256]{1,0:T(8,128)(2,1)S(1)}, bf16[2048,256]{1,0:T(8,128)(2,1)S(1)}, u32[]{:S(2)}, u32[]{:S(2)}) collective-permute-start(bf16[2048,256]{1,0:T(8,128)(2,1)S(1)} %get-tuple-element.39), channel_id=1, source_target_pairs={{32,160},{48,176},{64,192},{80,208},{104,232},{112,240},{33,161},{... | collective-permute-start | bytes 3145736 | tf_op jit(solution)/shard_map/ppermute | solution.py:309
  74.6 24.7 %collective-permute-start.15 = (bf16[2048,256]{1,0:T(8,128)(2,1)S(1)}, bf16[2048,256]{1,0:T(8,128)(2,1)S(1)}, u32[]{:S(2)}, u32[]{:S(2)}) collective-permute-start(bf16[2048,256]{1,0:T(8,128)(2,1)S(1)} %get-tuple-element.41.refs_13_), channel_id=1, source_target_pairs={{48,64},{64,80},{80,96},{88,72},{96,112},{104,88},{128,144},{136,2... | collective-permute-start | bytes 3145736 | tf_op jit(solution)/shard_map/ppermute | solution.py:309
  76.5 22.8 %collective-permute-start.17 = (bf16[2048,256]{1,0:T(8,128)(2,1)S(1)}, bf16[2048,256]{1,0:T(8,128)(2,1)S(1)}, u32[]{:S(2)}, u32[]{:S(2)}) collective-permute-start(bf16[2048,256]{1,0:T(8,128)(2,1)S(1)} %get-tuple-element.45), channel_id=1, source_target_pairs={{64,192},{80,208},{104,232},{112,240},{65,193},{81,209},{105,233},... | collective-permute-start | bytes 3145736 | tf_op jit(solution)/shard_map/ppermute | solution.py:309
  89.0 51.3 %collective-permute-start.22 = (bf16[11,512,256]{2,1,0:T(8,128)(2,1)S(1)}, bf16[11,512,256]{2,1,0:T(8,128)(2,1)S(1)}, u32[]{:S(2)}, u32[]{:S(2)}) collective-permute-start(bf16[11,512,256]{2,1,0:T(8,128)(2,1)S(1)} %get-tuple-element.51), channel_id=1, source_target_pairs={{0,8},{8,0},{16,24},{24,16},{32,40},{40,32},{48,56},{56,48},{64,72... | collective-permute-start | bytes 8650760 | tf_op jit(solution)/shard_map/ppermute | solution.py:313
  94.4 16.7 %collective-permute-start.14 = (bf16[2048,256]{1,0:T(8,128)(2,1)S(1)}, bf16[2048,256]{1,0:T(8,128)(2,1)S(1)}, u32[]{:S(2)}, u32[]{:S(2)}) collective-permute-start(bf16[2048,256]{1,0:T(8,128)(2,1)S(1)} %get-tuple-element.43.refs_5_), channel_id=1, source_target_pairs={{80,96},{96,112},{128,144},{136,248},{144,160},{152,136},{168,152}... | collective-permute-start | bytes 3145736 | tf_op jit(solution)/shard_map/ppermute | solution.py:309
  98.0 22.4 %collective-permute-start.16 = (bf16[2048,256]{1,0:T(8,128)(2,1)S(1)}, bf16[2048,256]{1,0:T(8,128)(2,1)S(1)}, u32[]{:S(2)}, u32[]{:S(2)}) collective-permute-start(bf16[2048,256]{1,0:T(8,128)(2,1)S(1)} %get-tuple-element.44), channel_id=1, source_target_pairs={{48,176},{64,192},{88,216},{96,224},{112,240},{49,177},{65,193},{8... | collective-permute-start | bytes 3145736 | tf_op jit(solution)/shard_map/ppermute | solution.py:309
  100.0 24.9 %collective-permute-start.18 = (bf16[2048,256]{1,0:T(8,128)(2,1)S(1)}, bf16[2048,256]{1,0:T(8,128)(2,1)S(1)}, u32[]{:S(2)}, u32[]{:S(2)}) collective-permute-start(bf16[2048,256]{1,0:T(8,128)(2,1)S(1)} %get-tuple-element.46.refs_6_), channel_id=1, source_target_pairs={{96,112},{128,144},{136,248},{144,160},{152,136},{160,176},{168,15... | collective-permute-start | bytes 3145736 | tf_op jit(solution)/shard_map/ppermute | solution.py:309
  102.0 23.1 %collective-permute-start.20 = (bf16[2048,256]{1,0:T(8,128)(2,1)S(1)}, bf16[2048,256]{1,0:T(8,128)(2,1)S(1)}, u32[]{:S(2)}, u32[]{:S(2)}) collective-permute-start(bf16[2048,256]{1,0:T(8,128)(2,1)S(1)} %get-tuple-element.49), channel_id=1, source_target_pairs={{72,200},{88,216},{96,224},{120,248},{73,201},{89,217},{97,225},{1... | collective-permute-start | bytes 3145736 | tf_op jit(solution)/shard_map/ppermute | solution.py:309
  122.3 16.7 %collective-permute-start.19 = (bf16[2048,256]{1,0:T(8,128)(2,1)S(1)}, bf16[2048,256]{1,0:T(8,128)(2,1)S(1)}, u32[]{:S(2)}, u32[]{:S(2)}) collective-permute-start(bf16[2048,256]{1,0:T(8,128)(2,1)S(1)} %get-tuple-element.48), channel_id=1, source_target_pairs={{96,112},{136,248},{192,208},{208,224},{224,240},{248,232},{97,113... | collective-permute-start | bytes 3145736 | tf_op jit(solution)/shard_map/ppermute | solution.py:309
  123.6 16.7 %collective-permute-start.21 = (bf16[2048,256]{1,0:T(8,128)(2,1)S(1)}, bf16[2048,256]{1,0:T(8,128)(2,1)S(1)}, u32[]{:S(2)}, u32[]{:S(2)}) collective-permute-start(bf16[2048,256]{1,0:T(8,128)(2,1)S(1)} %get-tuple-element.50), channel_id=1, source_target_pairs={{104,232},{112,240},{105,233},{113,241},{106,234},{114,242},{107,2... | collective-permute-start | bytes 3145736 | tf_op jit(solution)/shard_map/ppermute | solution.py:309
  124.9 15.4 %collective-permute-start.23 = (bf16[4,512,256]{2,1,0:T(8,128)(2,1)S(1)}, bf16[4,512,256]{2,1,0:T(8,128)(2,1)S(1)}, u32[]{:S(2)}, u32[]{:S(2)}) collective-permute-start(bf16[4,512,256]{2,1,0:T(8,128)(2,1)S(1)} %get-tuple-element.52), channel_id=1, source_target_pairs={{0,8},{8,0},{16,24},{24,16},{32,40},{40,32},{48,56},{56,48},{64,72... | collective-permute-start | bytes 3145736 | tf_op jit(solution)/shard_map/ppermute | solution.py:313
  142.8 2.3 collective-permute-start.24
  146.1 66.9 %collective-permute-start.25 = (bf16[8,256,2048]{2,1,0:T(8,128)(2,1)}, bf16[8,256,2048]{2,1,0:T(8,128)(2,1)}, u32[]{:S(2)}, u32[]{:S(2)}) collective-permute-start(bf16[8,256,2048]{2,1,0:T(8,128)(2,1)} %bitcast.6), channel_id=1, source_target_pairs={{0,8},{8,0},{16,24},{24,16},{32,40},{40,32},{48,56},{56,48},{64,72... | collective-permute-start | bytes 25165832 | tf_op jit(solution)/shard_map/ppermute | solution.py:505
  146.3 66.7 %slice-start = ((s8[8388608]{0:T(1024)(128)(4,1)}), s8[4194304]{0:T(1024)(128)(4,1)S(1)}, s32[]{:S(2)}) async-start(s8[8388608]{0:T(1024)(128)(4,1)} %bitcast.7), calls=%async_computation.3 | async-start | bytes 8388608
  150.1 62.8 %slice-start.1 = ((s8[8388608]{0:T(1024)(128)(4,1)}), s8[4194304]{0:T(1024)(128)(4,1)S(1)}, s32[]{:S(2)}) async-start(s8[8388608]{0:T(1024)(128)(4,1)} %bitcast.7), calls=%async_computation.4 | async-start | bytes 8388608
  213.0 30.4 %copy-start.1 = (bf16[512,2048]{1,0:T(8,128)(2,1)S(1)}, bf16[512,2048]{1,0:T(8,128)(2,1)}, u32[]{:S(2)}) copy-start(bf16[512,2048]{1,0:T(8,128)(2,1)} %param.10) | copy-start | bytes 6291460
  (12 other events, 24.0 us)
Sparse Core Ops, SparseCore 0:
  9.3 94.8 all-gather.2

commit v3 on v2

--- a/solution.py
+++ b/solution.py
@@ -159,6 +159,10 @@
     return out
 
 
+def in_hbm(array):
+    return pltpu.with_memory_space_constraint(array, pltpu.HBM)
+
+
 def start_from(refs, numbers, source, first, rows, to, sem):
     for number in numbers:
 
@@ -203,7 +207,10 @@
 
     return pl.pallas_call(
         functools.partial(move_kernel, *ways, *slots),
-        out_shape=[jax.ShapeDtypeStruct(s, arrays[0].dtype) for s in out_shapes],
+        out_shape=[
+            pltpu.HBM(s, arrays[0].dtype) if len(s) == 3 else jax.ShapeDtypeStruct(s, arrays[0].dtype)
+            for s in out_shapes
+        ],
         grid_spec=pltpu.PrefetchScalarGridSpec(
             num_scalar_prefetch=len(scalars),
             grid=(1,),
@@ -387,30 +394,38 @@
     causal = row >= col
     dims = (((1,), (1,)), ((), ()))
 
-    for head in range(q_heads):
-        lanes = pl.ds(head * HEAD_SIZE, HEAD_SIZE)
-        for tile in range(BLOCK_TOKENS // TILE):
-            rows = pl.ds(tile * TILE, TILE)
-            full = (SLOTS - 1) * BLOCK_TOKENS + tile * TILE
-            query = q_ref[rows, lanes]
-            far = lax.dot_general(
-                query, keys[here, pl.ds(0, full), :], dims, preferred_element_type=jnp.float32
+    units = [(head, tile) for head in range(q_heads) for tile in range(BLOCK_TOKENS // TILE)]
+
+    def places(unit):
+        head, tile = unit
+        far = (SLOTS - 1) * BLOCK_TOKENS + tile * TILE
+        return pl.ds(tile * TILE, TILE), pl.ds(head * HEAD_SIZE, HEAD_SIZE), pl.ds(0, far), pl.ds(far, TILE)
+
+    def scores(unit):
+        rows, lanes, *parts = places(unit)
+        query = q_ref[rows, lanes]
+        far, near = (
+            lax.dot_general(query, keys[here, at, :], dims, preferred_element_type=jnp.float32)
+            for at in parts
+        )
+        return far, jnp.where(causal, near, -1e30)
+
+    following = scores(units[0])
+    for number, unit in enumerate(units):
+        now = following
+        if number + 1 < len(units):
+            following = scores(units[number + 1])
+        rows, lanes, *parts = places(unit)
+        highest = functools.reduce(jnp.maximum, [jnp.max(s, axis=1, keepdims=True) for s in now])
+        total = sum(
+            jnp.dot(
+                jnp.exp2((s - highest) * EXP2_SCALE).astype(jnp.bfloat16),
+                values[here, at, :],
+                preferred_element_type=jnp.float32,
             )
-            near = lax.dot_general(
-                query, keys[here, pl.ds(full, TILE), :], dims, preferred_element_type=jnp.float32
-            )
-            near = jnp.where(causal, near, -1e30)
-            highest = jnp.maximum(
-                jnp.max(far, axis=1, keepdims=True), jnp.max(near, axis=1, keepdims=True)
-            )
-            far = jnp.exp2((far - highest) * EXP2_SCALE).astype(jnp.bfloat16)
-            near = jnp.exp2((near - highest) * EXP2_SCALE).astype(jnp.bfloat16)
-            total = jnp.dot(
-                far, values[here, pl.ds(0, full), :], preferred_element_type=jnp.float32
-            ) + jnp.dot(
-                near, values[here, pl.ds(full, TILE), :], preferred_element_type=jnp.float32
-            )
-            o_ref[rows, lanes] = (total[:, :HEAD_SIZE] / total[:, HEAD_SIZE:]).astype(jnp.bfloat16)
+            for s, at in zip(now, parts)
+        )
+        o_ref[rows, lanes] = (total[:, :HEAD_SIZE] / total[:, HEAD_SIZE:]).astype(jnp.bfloat16)
 
 
 def attention(queries, kv, chosen, info, row, place):
@@ -440,35 +455,49 @@
             bytes_accessed=4 * rows * width + 4 * blocks * keys * HEAD_SIZE,
             transcendentals=rows * (width // HEAD_SIZE) * keys,
         ),
-    )(info, row, queries, kv, *chosen)
-
-
-def project_kernel(parts, depth, core, a_ref, mine_ref, other_ref, o_ref):
-    first = pl.ds(pl.multiple_of(core[0] * depth, depth), depth)
-    second = pl.ds(pl.multiple_of((1 - core[0]) * depth, depth), depth)
-    total = jnp.zeros(o_ref.shape[1:], jnp.float32)
-    for part in range(parts):
-        total += jnp.dot(a_ref[part, :, first], mine_ref[part], preferred_element_type=jnp.float32)
-        total += jnp.dot(a_ref[part, :, second], other_ref[part], preferred_element_type=jnp.float32)
-    o_ref[0] = total.astype(jnp.bfloat16)
+    )(info, row, *map(in_hbm, (queries, kv, *chosen)))
+
+
+def project_kernel(depth, core, a_ref, mine_ref, other_ref, o_ref, first, second):
+    parts, rows, _ = a_ref.shape
+
+    @pl.when(pl.program_id(0) == 0)
+    def _():
+        for to, half in ((first, core[0]), (second, 1 - core[0])):
+            lanes = pl.ds(pl.multiple_of(half * depth, depth), depth)
+            for part in range(parts):
+                to[:, pl.ds(part * depth, depth)] = a_ref[part, :, lanes]
+
+    columns = o_ref.shape[2]
+    for number in range(o_ref.shape[0]):
+        at = pl.ds(number * columns, columns)
+        total = sum(
+            jnp.dot(
+                a[...], w[:, :, at].reshape(parts * depth, columns), preferred_element_type=jnp.float32
+            )
+            for a, w in ((first, mine_ref), (second, other_ref))
+        )
+        o_ref[number] = total.astype(jnp.bfloat16)
 
 
 def project(attended, mine, other, core):
     parts, rows, features = attended.shape
     depth = mine.shape[1]
     columns = mine.shape[2] // parts
+    together = 2
     return pl.pallas_call(
-        functools.partial(project_kernel, parts, depth),
+        functools.partial(project_kernel, depth),
         out_shape=jax.ShapeDtypeStruct((parts, rows, columns), jnp.bfloat16),
         grid_spec=pltpu.PrefetchScalarGridSpec(
             num_scalar_prefetch=1,
-            grid=(parts,),
+            grid=(parts // together,),
             in_specs=[
                 pl.BlockSpec((parts, rows, features), lambda i, t: (0, 0, 0)),
-                pl.BlockSpec((parts, depth, columns), lambda i, t: (0, 0, i)),
-                pl.BlockSpec((parts, depth, columns), lambda i, t: (0, 0, i)),
+                pl.BlockSpec((parts, depth, together * columns), lambda i, t: (0, 0, i)),
+                pl.BlockSpec((parts, depth, together * columns), lambda i, t: (0, 0, i)),
             ],
-            out_specs=pl.BlockSpec((1, rows, columns), lambda i, t: (i, 0, 0)),
+            out_specs=pl.BlockSpec((together, rows, columns), lambda i, t: (i, 0, 0)),
+            scratch_shapes=[pltpu.VMEM((rows, parts * depth), jnp.bfloat16)] * 2,
         ),
         compiler_params=pltpu.CompilerParams(
             dimension_semantics=("arbitrary",), vmem_limit_bytes=32 * 1024 * 1024
@@ -478,7 +507,7 @@
             bytes_accessed=2 * parts * parts * features * columns + 4 * parts * rows * features,
             transcendentals=0,
         ),
-    )(core, attended, mine, other)
+    )(core, attended, in_hbm(mine), in_hbm(other))
 
 
 def gather_weight(out_weight, core):

time: 251 us -> 243 us (0.968)
  local copies, waits for them, and re-layouts: 15.4 us -> 7.24 us
    unnamed x36 -> x18, local copies, waits for them, and re-layouts: 12.2 us -> 4.02 us
    pallas_call x10, Pallas kernels: 8.35 us -> 13.7 us  [move(): pl.pallas_call(functools.partial(move_kernel, *ways, *slots), out_shape=[...]
    pallas_call x1, Pallas kernels: 27.9 us -> 22.7 us  [attention(): pl.pallas_call(functools.partial(attention_kernel, width // HEAD_SIZE, le...]
  transfers between devices with their start and end apart: 27 -> 27, of which waited for: 15 -> 15; matrix products, arithmetic and copies ran while one was open for 1% -> 1% of each run, Pallas kernels for 14% -> 15%
where the time goes in v3:
time: 243 us; the launch traced here: 242 us
  waiting for transfers between devices  78.4 us (32%)
  blocking collectives  53.9 us (22%)
  Pallas kernels  45.3 us (19%)
  starting transfers between devices  43.3 us (18%)
  between operations  13.8 us (6%)
  local copies, waits for them, and re-layouts  7.24 us (3%)
    ppermute x20, waiting for transfers between devices, exchange(): arrived[step, way] = lax.ppermute(buffers[way], 'ctx', pairs(step, way))  75.8 us
    ppermute x20, starting transfers between devices, exchange(): arrived[step, way] = lax.ppermute(buffers[way], 'ctx', pairs(step, way))  36.1 us
    all_to_all x1, blocking collectives, per_device(): lax.all_to_all(attended.reshape(head_count, rows // head_count, width), '...  34.6 us
    pallas_call x1, Pallas kernels, attention(): pl.pallas_call(functools.partial(attention_kernel, width // HEAD_SIZE, le...  22.7 us
    all_to_all x1, blocking collectives, per_device(): return lax.all_to_all(mixed, 'head', 0, 0, tiled=True).reshape(rows, -1)  19.3 us
    pallas_call x10, Pallas kernels, move(): pl.pallas_call(functools.partial(move_kernel, *ways, *slots), out_shape=[...  13.7 us
    pallas_call x1, Pallas kernels, project(): pl.pallas_call(functools.partial(project_kernel, depth), out_shape=jax.Sh...  8.91 us
    ppermute x3, starting transfers between devices, exchange(): passed.append(lax.ppermute(give, 'ctx', SWAP))  5.91 us
  transfers between devices with their start and end apart: 27, of which 15 were waited for; matrix products, arithmetic and copies ran while one was open for 1% of the time, Pallas kernels for 15%

profile of v3, /device:TPU:226, one launch (start us, length us, event | category | flops | bytes accessed | tf_op | source)
XLA Modules:
  0.0 242.1 jit_solution(5083534416743627435)
XLA Ops:
  6.6 1.5 copy-done
  16.1 1.3 collective-permute-start.2
  18.1 9.6 %collective-permute-done.4.refs_0_.refs_2_ = bf16[2048,256]{1,0:T(8,128)(2,1)S(1)} collective-permute-done((bf16[2048,256]{1,0:T(8,128)(2,1)}, bf16[2048,256]{1,0:T(8,128)(2,1)S(1)}, u32[]{:S(2)}, u32[]{:S(2)}) %collective-permute-start.4) | collective-permute-done | bytes 1048608 | tf_op jit(solution)/shard_map/ppermute | solution.py:316
  28.4 1.3 collective-permute-start.8
  29.7 1.3 collective-permute-start.9
  31.0 8.0 %collective-permute-done.2.refs_0_.refs_3_.refs_4_ = bf16[2048,256]{1,0:T(8,128)(2,1)S(1)} collective-permute-done((bf16[2048,256]{1,0:T(8,128)(2,1)S(1)}, bf16[2048,256]{1,0:T(8,128)(2,1)S(1)}, u32[]{:S(2)}, u32[]{:S(2)}) %collective-permute-start.2) | collective-permute-done | bytes 1048608 | tf_op jit(solution)/shard_map/ppermute | solution.py:316
  39.6 1.3 collective-permute-start.6
  40.9 1.3 collective-permute-start.7
  42.2 8.0 %collective-permute-done.8.refs_0_.refs_5_.refs_4_ = bf16[2048,256]{1,0:T(8,128)(2,1)S(1)} collective-permute-done((bf16[2048,256]{1,0:T(8,128)(2,1)S(1)}, bf16[2048,256]{1,0:T(8,128)(2,1)S(1)}, u32[]{:S(2)}, u32[]{:S(2)}) %collective-permute-start.8) | collective-permute-done | bytes 1048608 | tf_op jit(solution)/shard_map/ppermute | solution.py:316
  51.7 5.5 %collective-permute-start.12 = (bf16[2048,256]{1,0:T(8,128)(2,1)S(1)}, bf16[2048,256]{1,0:T(8,128)(2,1)S(1)}, u32[]{:S(2)}, u32[]{:S(2)}) collective-permute-start(bf16[2048,256]{1,0:T(8,128)(2,1)S(1)} %get-tuple-element.37.refs_4_), channel_id=1, source_target_pairs={{32,48},{48,64},{64,80},{80,96},{96,112},{104,88},{120,104},{128,1... | collective-permute-start | bytes 3145736 | tf_op jit(solution)/shard_map/ppermute | solution.py:316
  57.2 1.3 collective-permute-start.13
  58.5 2.9 %collective-permute-done.6.refs_0_.refs_6_.refs_1_ = bf16[2048,256]{1,0:T(8,128)(2,1)S(1)} collective-permute-done((bf16[2048,256]{1,0:T(8,128)(2,1)S(1)}, bf16[2048,256]{1,0:T(8,128)(2,1)S(1)}, u32[]{:S(2)}, u32[]{:S(2)}) %collective-permute-start.6) | collective-permute-done | bytes 1048608 | tf_op jit(solution)/shard_map/ppermute | solution.py:316
  63.0 5.5 %collective-permute-start.10 = (bf16[2048,256]{1,0:T(8,128)(2,1)S(1)}, bf16[2048,256]{1,0:T(8,128)(2,1)S(1)}, u32[]{:S(2)}, u32[]{:S(2)}) collective-permute-start(bf16[2048,256]{1,0:T(8,128)(2,1)S(1)} %get-tuple-element.38.refs_2_), channel_id=1, source_target_pairs={{32,48},{48,64},{64,80},{80,96},{96,112},{104,88},{120,104},{128,1... | collective-permute-start | bytes 3145736 | tf_op jit(solution)/shard_map/ppermute | solution.py:316
  68.5 1.3 collective-permute-start.11
  69.8 2.9 %collective-permute-done.12.refs_0_.refs_7_.refs_3_ = bf16[2048,256]{1,0:T(8,128)(2,1)S(1)} collective-permute-done((bf16[2048,256]{1,0:T(8,128)(2,1)S(1)}, bf16[2048,256]{1,0:T(8,128)(2,1)S(1)}, u32[]{:S(2)}, u32[]{:S(2)}) %collective-permute-start.12) | collective-permute-done | bytes 1048608 | tf_op jit(solution)/shard_map/ppermute | solution.py:316
  74.6 1.9 collective-permute-start.15
  77.8 6.1 %collective-permute-done.10.refs_0_.refs_2_ = bf16[2048,256]{1,0:T(8,128)(2,1)S(1)} collective-permute-done((bf16[2048,256]{1,0:T(8,128)(2,1)S(1)}, bf16[2048,256]{1,0:T(8,128)(2,1)S(1)}, u32[]{:S(2)}, u32[]{:S(2)}) %collective-permute-start.10) | collective-permute-done | bytes 1048608 | tf_op jit(solution)/shard_map/ppermute | solution.py:316
  85.2 4.6 %shard_map.70 = (bf16[2048,256]{1,0:T(8,128)(2,1)S(1)}, bf16[2048,256]{1,0:T(8,128)(2,1)S(1)}, bf16[11,512,256]{2,1,0:T(8,128)(2,1)}, bf16[11,512,256]{2,1,0:T(8,128)(2,1)}) custom-call(s32[118]{0:T(128)S(1)} %dynamic-slice_bitcast_fusion.row.row_ref, s32[64]{0:T(128)S(1)} %reshape.173.want, bf16[2048,256]{1,0:T(8,128)(2,1)S(1)} %collective-permute-done.10.refs_0_.refs_2_, ...), custom_call_target="tpu_custom_call" | custom-call | bytes 188743680 | tf_op jit(solution)/shard_map/pallas_call | solution.py:208
  89.8 5.5 %collective-permute-start.22 = (bf16[11,512,256]{2,1,0:T(8,128)(2,1)}, bf16[11,512,256]{2,1,0:T(8,128)(2,1)S(1)}, u32[]{:S(2)}, u32[]{:S(2)}) collective-permute-start(bf16[11,512,256]{2,1,0:T(8,128)(2,1)} %get-tuple-element.51), channel_id=1, source_target_pairs={{0,8},{8,0},{16,24},{24,16},{32,40},{40,32},{48,56},{56,48},{64,72... | collective-permute-start | bytes 8650760 | tf_op jit(solution)/shard_map/ppermute | solution.py:320
  95.3 3.6 %collective-permute-start.14 = (bf16[2048,256]{1,0:T(8,128)(2,1)S(1)}, bf16[2048,256]{1,0:T(8,128)(2,1)S(1)}, u32[]{:S(2)}, u32[]{:S(2)}) collective-permute-start(bf16[2048,256]{1,0:T(8,128)(2,1)S(1)} %get-tuple-element.43.refs_5_), channel_id=1, source_target_pairs={{80,96},{96,112},{128,144},{136,248},{144,160},{152,136},{168,152}... | collective-permute-start | bytes 3145736 | tf_op jit(solution)/shard_map/ppermute | solution.py:316
  100.9 1.9 collective-permute-start.18
  103.6 8.4 %collective-permute-done.14.refs_0_ = bf16[2048,256]{1,0:T(8,128)(2,1)S(1)} collective-permute-done((bf16[2048,256]{1,0:T(8,128)(2,1)S(1)}, bf16[2048,256]{1,0:T(8,128)(2,1)S(1)}, u32[]{:S(2)}, u32[]{:S(2)}) %collective-permute-start.14) | collective-permute-done | bytes 1048608 | tf_op jit(solution)/shard_map/ppermute | solution.py:316
  112.0 10.3 %collective-permute-done.16.refs_4_ = bf16[2048,256]{1,0:T(8,128)(2,1)S(1)} collective-permute-done((bf16[2048,256]{1,0:T(8,128)(2,1)S(1)}, bf16[2048,256]{1,0:T(8,128)(2,1)S(1)}, u32[]{:S(2)}, u32[]{:S(2)}) %collective-permute-start.16) | collective-permute-done | bytes 1048608 | tf_op jit(solution)/shard_map/ppermute | solution.py:316
  122.3 2.2 shard_map.72
  127.2 14.0 %collective-permute-done.19.refs_1_ = bf16[2048,256]{1,0:T(8,128)(2,1)S(1)} collective-permute-done((bf16[2048,256]{1,0:T(8,128)(2,1)S(1)}, bf16[2048,256]{1,0:T(8,128)(2,1)S(1)}, u32[]{:S(2)}, u32[]{:S(2)}) %collective-permute-start.19) | collective-permute-done | bytes 1048608 | tf_op jit(solution)/shard_map/ppermute | solution.py:316
  141.2 1.3 collective-permute-done.21.refs_3_
  142.5 2.6 %shard_map.73 = (bf16[3,512,256]{2,1,0:T(8,128)(2,1)}, bf16[3,512,256]{2,1,0:T(8,128)(2,1)}) custom-call(s32[118]{0:T(128)S(1)} %dynamic-slice_bitcast_fusion.row.row_ref, s32[64]{0:T(128)S(1)} %reshape.173.want, bf16[2048,256]{1,0:T(8,128)(2,1)S(1)} %collective-permute-done.18.refs_0_, bf16[2048,256]{1,0:T(8,128)(2,1)S(1)} %collective-permute-done.19.refs_1_, ...), custom_call_target="tpu_custom_call" | custom-call | bytes 37748736 | tf_op jit(solution)/shard_map/pallas_call | solution.py:208
  145.4 2.5 %collective-permute-done.24.refs_5_ = bf16[3,512,256]{2,1,0:T(8,128)(2,1)S(1)} collective-permute-done((bf16[3,512,256]{2,1,0:T(8,128)(2,1)}, bf16[3,512,256]{2,1,0:T(8,128)(2,1)S(1)}, u32[]{:S(2)}, u32[]{:S(2)}) %collective-permute-start.24) | collective-permute-done | bytes 786464 | tf_op jit(solution)/shard_map/ppermute | solution.py:320
  148.7 22.7 %shard_map.74 = bf16[2048,512]{1,0:T(8,128)(2,1)S(1)} custom-call(s32[12]{0:T(128)S(1)} %reshape.172.info, s32[118]{0:T(128)S(1)} %dynamic-slice_bitcast_fusion.row.row_ref, bf16[2048,512]{1,0:T(8,128)(2,1)} %q_ref.1, bf16[2048,256]{1,0:T(8,128)(2,1)} %constant_dynamic-update-slice_fusion.refs_1_.kv_ref, bf16[11,512,256]{2,1,0:T(8,128)(2,1)} %get-tuple-element.42.refs_0_, ...), custom_call_target="tpu_custom_call" | custom-call | flops 8589934592 | bytes 8388608 | tf_op jit(solution)/shard_map/pallas_call | solution.py:435
  171.4 34.6 %all_to_all.10.a_ref = bf16[8,256,512]{2,1,0:T(8,128)(2,1)S(1)} all-to-all(bf16[8,256,512]{2,1,0:T(8,128)(2,1)S(1)} %bitcast.6), channel_id=1, replica_groups=mesh['ctx'=32,'head'=8] {'head'}, dimensions={0} | all-to-all | bytes 4194304 | tf_op jit(solution)/shard_map/all_to_all | solution.py:536
  206.0 8.9 %shard_map.75 = bf16[8,256,256]{2,1,0:T(8,128)(2,1)S(1)} custom-call(s32[1]{0:T(128)} %bitcast.core, bf16[8,256,512]{2,1,0:T(8,128)(2,1)S(1)} %all_to_all.10.a_ref, bf16[8,256,2048]{2,1,0:T(8,128)(2,1)} %bitcast.8, bf16[8,256,2048]{2,1,0:T(8,128)(2,1)} %collective-permute-done.25.other_ref), custom_call_target="tpu_custom_call" | custom-call | flops 4294967296 | bytes 20971520 | tf_op jit(solution)/shard_map/pallas_call | solution.py:488
  214.9 19.3 %all_to_all.11 = bf16[8,256,256]{2,1,0:T(8,128)(2,1)S(1)} all-to-all(bf16[8,256,256]{2,1,0:T(8,128)(2,1)S(1)} %shard_map.75), channel_id=1, replica_groups=mesh['ctx'=32,'head'=8] {'head'}, dimensions={0} | all-to-all | bytes 2097152 | tf_op jit(solution)/shard_map/all_to_all | solution.py:540
  (68 shorter events, 24.7 us)
Async XLA Ops:
  6.5 2.7 %copy-start.4 = (bf16[2048,128]{1,0:T(8,128)(2,1)S(1)}, bf16[2048,128]{1,0:T(8,128)(2,1)}, u32[]{:S(2)}) copy-start(bf16[2048,128]{1,0:T(8,128)(2,1)} %param.7) | copy-start | bytes 1572868
  6.5 3.5 %copy-start.5 = (bf16[2048,128]{1,0:T(8,128)(2,1)S(1)}, bf16[2048,128]{1,0:T(8,128)(2,1)}, u32[]{:S(2)}) copy-start(bf16[2048,128]{1,0:T(8,128)(2,1)} %param.8) | copy-start | bytes 1572868
  6.5 6.4 %copy-start.6 = (s32[4,3]{1,0:T(4,128)S(1)}, s32[4,3]{1,0:T(4,128)}, u32[]{:S(2)}) copy-start(s32[4,3]{1,0:T(4,128)} %param.9) | copy-start | bytes 148
  6.5 141.3 %all-gather.3.cloned.1.call-start = ((), (), s32[]{:S(2)}) async-start(), calls=%async_computation.2 | async-start | bytes 9437184 | tf_op jit(solution)/shard_map/all_gather | solution.py:521
  10.9 4.6 %collective-permute-start.1 = (bf16[2048,256]{1,0:T(8,128)(2,1)}, bf16[2048,256]{1,0:T(8,128)(2,1)S(1)}, u32[]{:S(2)}, u32[]{:S(2)}) collective-permute-start(bf16[2048,256]{1,0:T(8,128)(2,1)} %constant_dynamic-update-slice_fusion.refs_1_.kv_ref), channel_id=1, source_target_pairs={{0,8},{8,0},{16,24},{24,16},{32,40},{40,32},{48,56},{56,48},{64,72... | collective-permute-start | bytes 3145736 | tf_op jit(solution)/shard_map/ppermute | solution.py:287
  10.9 16.9 %collective-permute-start.4 = (bf16[2048,256]{1,0:T(8,128)(2,1)}, bf16[2048,256]{1,0:T(8,128)(2,1)S(1)}, u32[]{:S(2)}, u32[]{:S(2)}) collective-permute-start(bf16[2048,256]{1,0:T(8,128)(2,1)} %constant_dynamic-update-slice_fusion.refs_1_.kv_ref), channel_id=1, source_target_pairs={{0,16},{8,120},{16,32},{24,8},{32,48},{48,64},{64,80},{80,96},{96,... | collective-permute-start | bytes 3145736 | tf_op jit(solution)/shard_map/ppermute | solution.py:316
  12.2 15.6 %collective-permute-start.5 = (bf16[2048,256]{1,0:T(8,128)(2,1)}, bf16[2048,256]{1,0:T(8,128)(2,1)S(1)}, u32[]{:S(2)}, u32[]{:S(2)}) collective-permute-start(bf16[2048,256]{1,0:T(8,128)(2,1)} %constant_dynamic-update-slice_fusion.refs_1_.kv_ref), channel_id=1, source_target_pairs={{8,136},{24,152},{40,168},{56,184},{72,200},{88,216},{104,232},{12... | collective-permute-start | bytes 3145736 | tf_op jit(solution)/shard_map/ppermute | solution.py:316
  12.9 2.0 collective-permute-start
  16.1 22.9 %collective-permute-start.2 = (bf16[2048,256]{1,0:T(8,128)(2,1)S(1)}, bf16[2048,256]{1,0:T(8,128)(2,1)S(1)}, u32[]{:S(2)}, u32[]{:S(2)}) collective-permute-start(bf16[2048,256]{1,0:T(8,128)(2,1)S(1)} %get-tuple-element.31.refs_2_), channel_id=1, source_target_pairs={{0,16},{8,120},{16,32},{24,8},{32,48},{48,64},{64,80},{80,96},{96,... | collective-permute-start | bytes 3145736 | tf_op jit(solution)/shard_map/ppermute | solution.py:316
  17.4 21.6 %collective-permute-start.3 = (bf16[2048,256]{1,0:T(8,128)(2,1)S(1)}, bf16[2048,256]{1,0:T(8,128)(2,1)S(1)}, u32[]{:S(2)}, u32[]{:S(2)}) collective-permute-start(bf16[2048,256]{1,0:T(8,128)(2,1)S(1)} %get-tuple-element.32), channel_id=1, source_target_pairs={{8,136},{24,152},{40,168},{56,184},{72,200},{88,216},{104,232},{12... | collective-permute-start | bytes 3145736 | tf_op jit(solution)/shard_map/ppermute | solution.py:316
  28.4 21.9 %collective-permute-start.8 = (bf16[2048,256]{1,0:T(8,128)(2,1)S(1)}, bf16[2048,256]{1,0:T(8,128)(2,1)S(1)}, u32[]{:S(2)}, u32[]{:S(2)}) collective-permute-start(bf16[2048,256]{1,0:T(8,128)(2,1)S(1)} %get-tuple-element.33.refs_2_), channel_id=1, source_target_pairs={{8,120},{16,32},{32,48},{48,64},{64,80},{80,96},{96,112},{120,104}... | collective-permute-start | bytes 3145736 | tf_op jit(solution)/shard_map/ppermute | solution.py:316
  29.7 21.4 %collective-permute-start.9 = (bf16[2048,256]{1,0:T(8,128)(2,1)S(1)}, bf16[2048,256]{1,0:T(8,128)(2,1)S(1)}, u32[]{:S(2)}, u32[]{:S(2)}) collective-permute-start(bf16[2048,256]{1,0:T(8,128)(2,1)S(1)} %get-tuple-element.36), channel_id=1, source_target_pairs={{0,128},{16,144},{32,160},{48,176},{64,192},{80,208},{96,224},{112... | collective-permute-start | bytes 3145736 | tf_op jit(solution)/shard_map/ppermute | solution.py:316
  39.6 21.9 %collective-permute-start.6 = (bf16[2048,256]{1,0:T(8,128)(2,1)S(1)}, bf16[2048,256]{1,0:T(8,128)(2,1)S(1)}, u32[]{:S(2)}, u32[]{:S(2)}) collective-permute-start(bf16[2048,256]{1,0:T(8,128)(2,1)S(1)} %get-tuple-element.34.refs_3_), channel_id=1, source_target_pairs={{8,120},{16,32},{32,48},{48,64},{64,80},{80,96},{96,112},{120,104}... | collective-permute-start | bytes 3145736 | tf_op jit(solution)/shard_map/ppermute | solution.py:316
  40.9 21.4 %collective-permute-start.7 = (bf16[2048,256]{1,0:T(8,128)(2,1)S(1)}, bf16[2048,256]{1,0:T(8,128)(2,1)S(1)}, u32[]{:S(2)}, u32[]{:S(2)}) collective-permute-start(bf16[2048,256]{1,0:T(8,128)(2,1)S(1)} %get-tuple-element.35), channel_id=1, source_target_pairs={{0,128},{16,144},{32,160},{48,176},{64,192},{80,208},{96,224},{112... | collective-permute-start | bytes 3145736 | tf_op jit(solution)/shard_map/ppermute | solution.py:316
  51.7 21.0 %collective-permute-start.12 = (bf16[2048,256]{1,0:T(8,128)(2,1)S(1)}, bf16[2048,256]{1,0:T(8,128)(2,1)S(1)}, u32[]{:S(2)}, u32[]{:S(2)}) collective-permute-start(bf16[2048,256]{1,0:T(8,128)(2,1)S(1)} %get-tuple-element.37.refs_4_), channel_id=1, source_target_pairs={{32,48},{48,64},{64,80},{80,96},{96,112},{104,88},{120,104},{128,1... | collective-permute-start | bytes 3145736 | tf_op jit(solution)/shard_map/ppermute | solution.py:316
  57.2 16.7 %collective-permute-start.13 = (bf16[2048,256]{1,0:T(8,128)(2,1)S(1)}, bf16[2048,256]{1,0:T(8,128)(2,1)S(1)}, u32[]{:S(2)}, u32[]{:S(2)}) collective-permute-start(bf16[2048,256]{1,0:T(8,128)(2,1)S(1)} %get-tuple-element.40), channel_id=1, source_target_pairs={{32,160},{48,176},{64,192},{80,208},{96,224},{112,240},{33,161},{4... | collective-permute-start | bytes 3145736 | tf_op jit(solution)/shard_map/ppermute | solution.py:316
  63.0 21.0 %collective-permute-start.10 = (bf16[2048,256]{1,0:T(8,128)(2,1)S(1)}, bf16[2048,256]{1,0:T(8,128)(2,1)S(1)}, u32[]{:S(2)}, u32[]{:S(2)}) collective-permute-start(bf16[2048,256]{1,0:T(8,128)(2,1)S(1)} %get-tuple-element.38.refs_2_), channel_id=1, source_target_pairs={{32,48},{48,64},{64,80},{80,96},{96,112},{104,88},{120,104},{128,1... | collective-permute-start | bytes 3145736 | tf_op jit(solution)/shard_map/ppermute | solution.py:316
  68.5 16.7 %collective-permute-start.11 = (bf16[2048,256]{1,0:T(8,128)(2,1)S(1)}, bf16[2048,256]{1,0:T(8,128)(2,1)S(1)}, u32[]{:S(2)}, u32[]{:S(2)}) collective-permute-start(bf16[2048,256]{1,0:T(8,128)(2,1)S(1)} %get-tuple-element.39), channel_id=1, source_target_pairs={{32,160},{48,176},{64,192},{80,208},{104,232},{112,240},{33,161},{... | collective-permute-start | bytes 3145736 | tf_op jit(solution)/shard_map/ppermute | solution.py:316
  74.6 25.7 %collective-permute-start.15 = (bf16[2048,256]{1,0:T(8,128)(2,1)S(1)}, bf16[2048,256]{1,0:T(8,128)(2,1)S(1)}, u32[]{:S(2)}, u32[]{:S(2)}) collective-permute-start(bf16[2048,256]{1,0:T(8,128)(2,1)S(1)} %get-tuple-element.41.refs_13_), channel_id=1, source_target_pairs={{48,64},{64,80},{80,96},{88,72},{96,112},{104,88},{128,144},{136,2... | collective-permute-start | bytes 3145736 | tf_op jit(solution)/shard_map/ppermute | solution.py:316
  76.5 23.7 %collective-permute-start.17 = (bf16[2048,256]{1,0:T(8,128)(2,1)S(1)}, bf16[2048,256]{1,0:T(8,128)(2,1)S(1)}, u32[]{:S(2)}, u32[]{:S(2)}) collective-permute-start(bf16[2048,256]{1,0:T(8,128)(2,1)S(1)} %get-tuple-element.45), channel_id=1, source_target_pairs={{64,192},{80,208},{104,232},{112,240},{65,193},{81,209},{105,233},... | collective-permute-start | bytes 3145736 | tf_op jit(solution)/shard_map/ppermute | solution.py:316
  89.8 52.7 %collective-permute-start.22 = (bf16[11,512,256]{2,1,0:T(8,128)(2,1)}, bf16[11,512,256]{2,1,0:T(8,128)(2,1)S(1)}, u32[]{:S(2)}, u32[]{:S(2)}) collective-permute-start(bf16[11,512,256]{2,1,0:T(8,128)(2,1)} %get-tuple-element.51), channel_id=1, source_target_pairs={{0,8},{8,0},{16,24},{24,16},{32,40},{40,32},{48,56},{56,48},{64,72... | collective-permute-start | bytes 8650760 | tf_op jit(solution)/shard_map/ppermute | solution.py:320
  95.3 16.7 %collective-permute-start.14 = (bf16[2048,256]{1,0:T(8,128)(2,1)S(1)}, bf16[2048,256]{1,0:T(8,128)(2,1)S(1)}, u32[]{:S(2)}, u32[]{:S(2)}) collective-permute-start(bf16[2048,256]{1,0:T(8,128)(2,1)S(1)} %get-tuple-element.43.refs_5_), channel_id=1, source_target_pairs={{80,96},{96,112},{128,144},{136,248},{144,160},{152,136},{168,152}... | collective-permute-start | bytes 3145736 | tf_op jit(solution)/shard_map/ppermute | solution.py:316
  98.9 23.3 %collective-permute-start.16 = (bf16[2048,256]{1,0:T(8,128)(2,1)S(1)}, bf16[2048,256]{1,0:T(8,128)(2,1)S(1)}, u32[]{:S(2)}, u32[]{:S(2)}) collective-permute-start(bf16[2048,256]{1,0:T(8,128)(2,1)S(1)} %get-tuple-element.44), channel_id=1, source_target_pairs={{48,176},{64,192},{88,216},{96,224},{112,240},{49,177},{65,193},{8... | collective-permute-start | bytes 3145736 | tf_op jit(solution)/shard_map/ppermute | solution.py:316
  100.9 26.1 %collective-permute-start.18 = (bf16[2048,256]{1,0:T(8,128)(2,1)S(1)}, bf16[2048,256]{1,0:T(8,128)(2,1)S(1)}, u32[]{:S(2)}, u32[]{:S(2)}) collective-permute-start(bf16[2048,256]{1,0:T(8,128)(2,1)S(1)} %get-tuple-element.46.refs_6_), channel_id=1, source_target_pairs={{96,112},{128,144},{136,248},{144,160},{152,136},{160,176},{168,15... | collective-permute-start | bytes 3145736 | tf_op jit(solution)/shard_map/ppermute | solution.py:316
  102.9 24.3 %collective-permute-start.20 = (bf16[2048,256]{1,0:T(8,128)(2,1)S(1)}, bf16[2048,256]{1,0:T(8,128)(2,1)S(1)}, u32[]{:S(2)}, u32[]{:S(2)}) collective-permute-start(bf16[2048,256]{1,0:T(8,128)(2,1)S(1)} %get-tuple-element.49), channel_id=1, source_target_pairs={{72,200},{88,216},{96,224},{120,248},{73,201},{89,217},{97,225},{1... | collective-permute-start | bytes 3145736 | tf_op jit(solution)/shard_map/ppermute | solution.py:316
  124.5 16.7 %collective-permute-start.19 = (bf16[2048,256]{1,0:T(8,128)(2,1)S(1)}, bf16[2048,256]{1,0:T(8,128)(2,1)S(1)}, u32[]{:S(2)}, u32[]{:S(2)}) collective-permute-start(bf16[2048,256]{1,0:T(8,128)(2,1)S(1)} %get-tuple-element.48), channel_id=1, source_target_pairs={{96,112},{136,248},{192,208},{208,224},{224,240},{248,232},{97,113... | collective-permute-start | bytes 3145736 | tf_op jit(solution)/shard_map/ppermute | solution.py:316
  125.8 16.7 %collective-permute-start.21 = (bf16[2048,256]{1,0:T(8,128)(2,1)S(1)}, bf16[2048,256]{1,0:T(8,128)(2,1)S(1)}, u32[]{:S(2)}, u32[]{:S(2)}) collective-permute-start(bf16[2048,256]{1,0:T(8,128)(2,1)S(1)} %get-tuple-element.50), channel_id=1, source_target_pairs={{104,232},{112,240},{105,233},{113,241},{106,234},{114,242},{107,2... | collective-permute-start | bytes 3145736 | tf_op jit(solution)/shard_map/ppermute | solution.py:316
  127.1 15.4 %collective-permute-start.23 = (bf16[4,512,256]{2,1,0:T(8,128)(2,1)}, bf16[4,512,256]{2,1,0:T(8,128)(2,1)S(1)}, u32[]{:S(2)}, u32[]{:S(2)}) collective-permute-start(bf16[4,512,256]{2,1,0:T(8,128)(2,1)} %get-tuple-element.52), channel_id=1, source_target_pairs={{0,8},{8,0},{16,24},{24,16},{32,40},{40,32},{48,56},{56,48},{64,72... | collective-permute-start | bytes 3145736 | tf_op jit(solution)/shard_map/ppermute | solution.py:320
  142.5 2.6 %copy-start.2 = (bf16[11,512,256]{2,1,0:T(8,128)(2,1)}, bf16[11,512,256]{2,1,0:T(8,128)(2,1)S(1)}, u32[]{:S(2)}) copy-start(bf16[11,512,256]{2,1,0:T(8,128)(2,1)S(1)} %collective-permute-done.22.refs_4_.refs_3_) | copy-start | bytes 8650756
  145.1 2.8 %collective-permute-start.24 = (bf16[3,512,256]{2,1,0:T(8,128)(2,1)}, bf16[3,512,256]{2,1,0:T(8,128)(2,1)S(1)}, u32[]{:S(2)}, u32[]{:S(2)}) collective-permute-start(bf16[3,512,256]{2,1,0:T(8,128)(2,1)} %get-tuple-element.54), channel_id=1, source_target_pairs={{0,8},{8,0},{16,24},{24,16},{32,40},{40,32},{48,56},{56,48},{64,72... | collective-permute-start | bytes 2359304 | tf_op jit(solution)/shard_map/ppermute | solution.py:320
  147.8 58.2 %collective-permute-start.25 = (bf16[8,256,2048]{2,1,0:T(8,128)(2,1)}, bf16[8,256,2048]{2,1,0:T(8,128)(2,1)}, u32[]{:S(2)}, u32[]{:S(2)}) collective-permute-start(bf16[8,256,2048]{2,1,0:T(8,128)(2,1)} %bitcast.7), channel_id=1, source_target_pairs={{0,8},{8,0},{16,24},{24,16},{32,40},{40,32},{48,56},{56,48},{64,72... | collective-permute-start | bytes 25165832 | tf_op jit(solution)/shard_map/ppermute | solution.py:534
  206.0 29.2 %copy-start.1 = (bf16[512,2048]{1,0:T(8,128)(2,1)S(1)}, bf16[512,2048]{1,0:T(8,128)(2,1)}, u32[]{:S(2)}) copy-start(bf16[512,2048]{1,0:T(8,128)(2,1)} %param.10) | copy-start | bytes 6291460
  (3 other events, 5.1 us)
Sparse Core Ops, SparseCore 0:
  9.3 94.8 all-gather.2

commit v4 on v3

--- a/solution.py
+++ b/solution.py
@@ -121,6 +121,7 @@
     ),
 )
 CHECKPOINTS = (5, 7, 9)
+CHUNKS = 2
 COST = 12
 
 
@@ -321,7 +322,7 @@
     return kept + passed, row, tables.place
 
 
-def attention_kernel(q_heads, sources, place, info, row_ref, q_ref, kv_ref, *refs):
+def attention_kernel(q_heads, sources, place, first, info, row_ref, q_ref, kv_ref, *refs):
     chosen, (o_ref, keys, values, sems) = refs[:sources], refs[sources:]
     step = pl.program_id(0)
     steps = pl.num_programs(0)
@@ -341,10 +342,10 @@
         )
 
     def own_rows(at):
-        return kv_ref.at[pl.ds(pl.multiple_of(at * BLOCK_TOKENS, BLOCK_TOKENS), BLOCK_TOKENS)]
+        return kv_ref.at[pl.ds(pl.multiple_of((first + at) * BLOCK_TOKENS, BLOCK_TOKENS), BLOCK_TOKENS)]
 
     def choice(at, slot):
-        block = info[at * (SLOTS - 1) + slot]
+        block = info[(first + at) * (SLOTS - 1) + slot]
         owner = jnp.maximum(block, 0) // BLOCKS
         return jnp.where(block < 0, -1, row_ref[place + 2 * owner]), row_ref[place + 2 * owner + 1]
 
@@ -428,17 +429,17 @@
         o_ref[rows, lanes] = (total[:, :HEAD_SIZE] / total[:, HEAD_SIZE:]).astype(jnp.bfloat16)
 
 
-def attention(queries, kv, chosen, info, row, place):
-    rows, width = queries.shape
-    blocks = rows // BLOCK_TOKENS
+def attention(queries, kv, chosen, info, row, place, first, blocks):
+    width = queries.shape[1]
+    rows = blocks * BLOCK_TOKENS
     keys = SLOTS * BLOCK_TOKENS
     return pl.pallas_call(
-        functools.partial(attention_kernel, width // HEAD_SIZE, len(chosen), place),
+        functools.partial(attention_kernel, width // HEAD_SIZE, len(chosen), place, first),
         out_shape=jax.ShapeDtypeStruct((rows, width), jnp.bfloat16),
         grid_spec=pltpu.PrefetchScalarGridSpec(
             num_scalar_prefetch=2,
             grid=(blocks,),
-            in_specs=[pl.BlockSpec((BLOCK_TOKENS, width), lambda i, *_: (i, 0))]
+            in_specs=[pl.BlockSpec((BLOCK_TOKENS, width), lambda i, *_: (first + i, 0))]
             + [pl.BlockSpec(memory_space=pltpu.HBM)] * (1 + len(chosen)),
             out_specs=pl.BlockSpec((BLOCK_TOKENS, width), lambda i, *_: (i, 0)),
             scratch_shapes=[
@@ -458,15 +459,18 @@
     )(info, row, *map(in_hbm, (queries, kv, *chosen)))
 
 
-def project_kernel(depth, core, a_ref, mine_ref, other_ref, o_ref, first, second):
-    parts, rows, _ = a_ref.shape
+def project_kernel(depth, core, *refs):
+    *a_refs, mine_ref, other_ref, o_ref, first, second = refs
+    parts, rows, _ = a_refs[0].shape
 
     @pl.when(pl.program_id(0) == 0)
     def _():
         for to, half in ((first, core[0]), (second, 1 - core[0])):
             lanes = pl.ds(pl.multiple_of(half * depth, depth), depth)
-            for part in range(parts):
-                to[:, pl.ds(part * depth, depth)] = a_ref[part, :, lanes]
+            for chunk, a_ref in enumerate(a_refs):
+                for part in range(parts):
+                    at = pl.ds(chunk * rows, rows), pl.ds(part * depth, depth)
+                    to[at] = a_ref[part, :, lanes]
 
     columns = o_ref.shape[2]
     for number in range(o_ref.shape[0]):
@@ -481,7 +485,8 @@
 
 
 def project(attended, mine, other, core):
-    parts, rows, features = attended.shape
+    parts, part_rows, features = attended[0].shape
+    rows = part_rows * len(attended)
     depth = mine.shape[1]
     columns = mine.shape[2] // parts
     together = 2
@@ -492,7 +497,7 @@
             num_scalar_prefetch=1,
             grid=(parts // together,),
             in_specs=[
-                pl.BlockSpec((parts, rows, features), lambda i, t: (0, 0, 0)),
+                *[pl.BlockSpec((parts, part_rows, features), lambda i, t: (0, 0, 0))] * len(attended),
                 pl.BlockSpec((parts, depth, together * columns), lambda i, t: (0, 0, i)),
                 pl.BlockSpec((parts, depth, together * columns), lambda i, t: (0, 0, i)),
             ],
@@ -507,7 +512,7 @@
             bytes_accessed=2 * parts * parts * features * columns + 4 * parts * rows * features,
             transcendentals=0,
         ),
-    )(core, attended, in_hbm(mine), in_hbm(other))
+    )(core, *attended, in_hbm(mine), in_hbm(other))
 
 
 def gather_weight(out_weight, core):
@@ -532,12 +537,18 @@
     chosen, row, place = exchange(kv, selected, other_selected, index)
     mine, chosen[-1] = lax.optimization_barrier((mine, chosen[-1]))
     other = lax.ppermute(mine, "ctx", SWAP)
-    attended = attention(queries, kv, chosen, selected.reshape(-1), row, place)
-    tokens = lax.all_to_all(
-        attended.reshape(head_count, rows // head_count, width), "head", 0, 0, tiled=True
-    )
-    mixed = project(tokens, mine, other, core[None])
-    return lax.all_to_all(mixed, "head", 0, 0, tiled=True).reshape(rows, -1)
+    tokens = []
+    share = rows // CHUNKS // head_count
+    for chunk in range(CHUNKS):
+        blocks = BLOCKS // CHUNKS
+        attended = attention(
+            queries, kv, chosen, selected.reshape(-1), row, place, chunk * blocks, blocks
+        )
+        tokens.append(
+            lax.all_to_all(attended.reshape(head_count, share, width), "head", 0, 0, tiled=True)
+        )
+    mixed = lax.all_to_all(project(tokens, mine, other, core[None]), "head", 0, 0, tiled=True)
+    return mixed.reshape(head_count, CHUNKS, share, -1).swapaxes(0, 1).reshape(rows, -1)
 
 
 def solution(mesh):

time: 243 us -> 243 us (level)
  blocking collectives: 53.9 us -> 40.8 us
  starting transfers between devices: 43.3 us -> 49.5 us
  Pallas kernels: 45.3 us -> 48.7 us
  waiting for transfers between devices: 78.4 us -> 81.6 us
    all_to_all x2, blocking collectives: 53.9 us -> 40.8 us  [the longest x1 21.6 us: per_device(): lax.all_to_all(attended.reshape(head_count, share, width), 'head', 0, 0,...]
    all_to_all x0 -> x1, starting transfers between devices: none -> 6.15 us  [per_device(): lax.all_to_all(attended.reshape(head_count, share, width), 'head', 0, 0,...]
    pallas_call x1 -> x2, Pallas kernels: 22.7 us -> 26.1 us  [attention(): pl.pallas_call(functools.partial(attention_kernel, width // HEAD_SIZE, le...]
    all_to_all x0 -> x1, waiting for transfers between devices: none -> 3.19 us  [per_device(): lax.all_to_all(attended.reshape(head_count, share, width), 'head', 0, 0,...]
  transfers between devices with their start and end apart: 27 -> 28, of which waited for: 15 -> 16; matrix products, arithmetic and copies ran while one was open for 1% -> 1% of each run, Pallas kernels for 15% -> 16%
where the time goes in v4:
time: 243 us; the launch traced here: 242 us
  waiting for transfers between devices  81.6 us (34%)
  starting transfers between devices  49.5 us (20%)
  Pallas kernels  48.7 us (20%)
  blocking collectives  40.8 us (17%)
  between operations  13.8 us (6%)
  local copies, waits for them, and re-layouts  7.3 us (3%)
    ppermute x20, waiting for transfers between devices, exchange(): arrived[step, way] = lax.ppermute(buffers[way], 'ctx', pairs(step, way))  75.9 us
    ppermute x20, starting transfers between devices, exchange(): arrived[step, way] = lax.ppermute(buffers[way], 'ctx', pairs(step, way))  36.1 us
    pallas_call x2, Pallas kernels, attention(): pl.pallas_call(functools.partial(attention_kernel, width // HEAD_SIZE, le...  26.1 us
    all_to_all x1, blocking collectives, per_device(): lax.all_to_all(attended.reshape(head_count, share, width), 'head', 0, 0,...  21.6 us
    all_to_all x1, blocking collectives, per_device(): lax.all_to_all(project(tokens, mine, other, core[None]), 'head', 0, 0, ti...  19.2 us
    pallas_call x10, Pallas kernels, move(): pl.pallas_call(functools.partial(move_kernel, *ways, *slots), out_shape=[...  13.7 us
    pallas_call x1, Pallas kernels, project(): pl.pallas_call(functools.partial(project_kernel, depth), out_shape=jax.Sh...  8.88 us
    all_to_all x1, starting transfers between devices, per_device(): lax.all_to_all(attended.reshape(head_count, share, width), 'head', 0, 0,...  6.15 us
  transfers between devices with their start and end apart: 28, of which 16 were waited for; matrix products, arithmetic and copies ran while one was open for 1% of the time, Pallas kernels for 16%

profile of v4, /device:TPU:226, one launch (start us, length us, event | category | flops | bytes accessed | tf_op | source)
XLA Modules:
  0.0 241.8 jit_solution(11527176070490535240)
XLA Ops:
  6.6 1.5 copy-done
  16.1 1.3 collective-permute-start.2
  18.1 9.6 %collective-permute-done.4.refs_0_.refs_2_ = bf16[2048,256]{1,0:T(8,128)(2,1)S(1)} collective-permute-done((bf16[2048,256]{1,0:T(8,128)(2,1)}, bf16[2048,256]{1,0:T(8,128)(2,1)S(1)}, u32[]{:S(2)}, u32[]{:S(2)}) %collective-permute-start.4) | collective-permute-done | bytes 1048608 | tf_op jit(solution)/shard_map/ppermute | solution.py:317
  28.4 1.3 collective-permute-start.8
  29.7 1.3 collective-permute-start.9
  31.0 8.0 %collective-permute-done.2.refs_0_.refs_3_.refs_4_ = bf16[2048,256]{1,0:T(8,128)(2,1)S(1)} collective-permute-done((bf16[2048,256]{1,0:T(8,128)(2,1)S(1)}, bf16[2048,256]{1,0:T(8,128)(2,1)S(1)}, u32[]{:S(2)}, u32[]{:S(2)}) %collective-permute-start.2) | collective-permute-done | bytes 1048608 | tf_op jit(solution)/shard_map/ppermute | solution.py:317
  39.6 1.3 collective-permute-start.6
  42.2 8.0 %collective-permute-done.8.refs_0_.refs_5_.refs_4_ = bf16[2048,256]{1,0:T(8,128)(2,1)S(1)} collective-permute-done((bf16[2048,256]{1,0:T(8,128)(2,1)S(1)}, bf16[2048,256]{1,0:T(8,128)(2,1)S(1)}, u32[]{:S(2)}, u32[]{:S(2)}) %collective-permute-start.8) | collective-permute-done | bytes 1048608 | tf_op jit(solution)/shard_map/ppermute | solution.py:317
  51.7 5.5 %collective-permute-start.12 = (bf16[2048,256]{1,0:T(8,128)(2,1)S(1)}, bf16[2048,256]{1,0:T(8,128)(2,1)S(1)}, u32[]{:S(2)}, u32[]{:S(2)}) collective-permute-start(bf16[2048,256]{1,0:T(8,128)(2,1)S(1)} %get-tuple-element.37.refs_4_), channel_id=1, source_target_pairs={{32,48},{48,64},{64,80},{80,96},{96,112},{104,88},{120,104},{128,1... | collective-permute-start | bytes 3145736 | tf_op jit(solution)/shard_map/ppermute | solution.py:317
  58.5 2.9 %collective-permute-done.6.refs_0_.refs_6_.refs_1_ = bf16[2048,256]{1,0:T(8,128)(2,1)S(1)} collective-permute-done((bf16[2048,256]{1,0:T(8,128)(2,1)S(1)}, bf16[2048,256]{1,0:T(8,128)(2,1)S(1)}, u32[]{:S(2)}, u32[]{:S(2)}) %collective-permute-start.6) | collective-permute-done | bytes 1048608 | tf_op jit(solution)/shard_map/ppermute | solution.py:317
  63.0 5.5 %collective-permute-start.10 = (bf16[2048,256]{1,0:T(8,128)(2,1)S(1)}, bf16[2048,256]{1,0:T(8,128)(2,1)S(1)}, u32[]{:S(2)}, u32[]{:S(2)}) collective-permute-start(bf16[2048,256]{1,0:T(8,128)(2,1)S(1)} %get-tuple-element.38.refs_2_), channel_id=1, source_target_pairs={{32,48},{48,64},{64,80},{80,96},{96,112},{104,88},{120,104},{128,1... | collective-permute-start | bytes 3145736 | tf_op jit(solution)/shard_map/ppermute | solution.py:317
  69.8 2.9 %collective-permute-done.12.refs_0_.refs_7_.refs_3_ = bf16[2048,256]{1,0:T(8,128)(2,1)S(1)} collective-permute-done((bf16[2048,256]{1,0:T(8,128)(2,1)S(1)}, bf16[2048,256]{1,0:T(8,128)(2,1)S(1)}, u32[]{:S(2)}, u32[]{:S(2)}) %collective-permute-start.12) | collective-permute-done | bytes 1048608 | tf_op jit(solution)/shard_map/ppermute | solution.py:317
  74.6 1.9 collective-permute-start.15
  77.8 6.1 %collective-permute-done.10.refs_0_.refs_2_ = bf16[2048,256]{1,0:T(8,128)(2,1)S(1)} collective-permute-done((bf16[2048,256]{1,0:T(8,128)(2,1)S(1)}, bf16[2048,256]{1,0:T(8,128)(2,1)S(1)}, u32[]{:S(2)}, u32[]{:S(2)}) %collective-permute-start.10) | collective-permute-done | bytes 1048608 | tf_op jit(solution)/shard_map/ppermute | solution.py:317
  85.2 4.7 %shard_map.70 = (bf16[2048,256]{1,0:T(8,128)(2,1)S(1)}, bf16[2048,256]{1,0:T(8,128)(2,1)S(1)}, bf16[11,512,256]{2,1,0:T(8,128)(2,1)}, bf16[11,512,256]{2,1,0:T(8,128)(2,1)}) custom-call(s32[118]{0:T(128)S(1)} %dynamic-slice_bitcast_fusion.row.row_ref, s32[64]{0:T(128)S(1)} %reshape.180.want, bf16[2048,256]{1,0:T(8,128)(2,1)S(1)} %collective-permute-done.10.refs_0_.refs_2_, ...), custom_call_target="tpu_custom_call" | custom-call | bytes 188743680 | tf_op jit(solution)/shard_map/pallas_call | solution.py:209
  89.8 5.5 %collective-permute-start.22 = (bf16[11,512,256]{2,1,0:T(8,128)(2,1)}, bf16[11,512,256]{2,1,0:T(8,128)(2,1)S(1)}, u32[]{:S(2)}, u32[]{:S(2)}) collective-permute-start(bf16[11,512,256]{2,1,0:T(8,128)(2,1)} %get-tuple-element.51), channel_id=1, source_target_pairs={{0,8},{8,0},{16,24},{24,16},{32,40},{40,32},{48,56},{56,48},{64,72... | collective-permute-start | bytes 8650760 | tf_op jit(solution)/shard_map/ppermute | solution.py:321
  95.3 3.6 %collective-permute-start.14 = (bf16[2048,256]{1,0:T(8,128)(2,1)S(1)}, bf16[2048,256]{1,0:T(8,128)(2,1)S(1)}, u32[]{:S(2)}, u32[]{:S(2)}) collective-permute-start(bf16[2048,256]{1,0:T(8,128)(2,1)S(1)} %get-tuple-element.43.refs_5_), channel_id=1, source_target_pairs={{80,96},{96,112},{128,144},{136,248},{144,160},{152,136},{168,152}... | collective-permute-start | bytes 3145736 | tf_op jit(solution)/shard_map/ppermute | solution.py:317
  101.0 1.9 collective-permute-start.18
  103.6 8.4 %collective-permute-done.14.refs_0_ = bf16[2048,256]{1,0:T(8,128)(2,1)S(1)} collective-permute-done((bf16[2048,256]{1,0:T(8,128)(2,1)S(1)}, bf16[2048,256]{1,0:T(8,128)(2,1)S(1)}, u32[]{:S(2)}, u32[]{:S(2)}) %collective-permute-start.14) | collective-permute-done | bytes 1048608 | tf_op jit(solution)/shard_map/ppermute | solution.py:317
  112.0 10.3 %collective-permute-done.16.refs_4_ = bf16[2048,256]{1,0:T(8,128)(2,1)S(1)} collective-permute-done((bf16[2048,256]{1,0:T(8,128)(2,1)S(1)}, bf16[2048,256]{1,0:T(8,128)(2,1)S(1)}, u32[]{:S(2)}, u32[]{:S(2)}) %collective-permute-start.16) | collective-permute-done | bytes 1048608 | tf_op jit(solution)/shard_map/ppermute | solution.py:317
  122.4 2.2 shard_map.72
  127.2 14.0 %collective-permute-done.19.refs_1_ = bf16[2048,256]{1,0:T(8,128)(2,1)S(1)} collective-permute-done((bf16[2048,256]{1,0:T(8,128)(2,1)S(1)}, bf16[2048,256]{1,0:T(8,128)(2,1)S(1)}, u32[]{:S(2)}, u32[]{:S(2)}) %collective-permute-start.19) | collective-permute-done | bytes 1048608 | tf_op jit(solution)/shard_map/ppermute | solution.py:317
  141.2 1.3 collective-permute-done.21.refs_3_
  142.5 2.5 %shard_map.73 = (bf16[3,512,256]{2,1,0:T(8,128)(2,1)}, bf16[3,512,256]{2,1,0:T(8,128)(2,1)}) custom-call(s32[118]{0:T(128)S(1)} %dynamic-slice_bitcast_fusion.row.row_ref, s32[64]{0:T(128)S(1)} %reshape.180.want, bf16[2048,256]{1,0:T(8,128)(2,1)S(1)} %collective-permute-done.18.refs_0_, bf16[2048,256]{1,0:T(8,128)(2,1)S(1)} %collective-permute-done.19.refs_1_, ...), custom_call_target="tpu_custom_call" | custom-call | bytes 37748736 | tf_op jit(solution)/shard_map/pallas_call | solution.py:209
  145.3 2.5 %collective-permute-done.24.refs_5_ = bf16[3,512,256]{2,1,0:T(8,128)(2,1)S(1)} collective-permute-done((bf16[3,512,256]{2,1,0:T(8,128)(2,1)}, bf16[3,512,256]{2,1,0:T(8,128)(2,1)S(1)}, u32[]{:S(2)}, u32[]{:S(2)}) %collective-permute-start.24) | collective-permute-done | bytes 786464 | tf_op jit(solution)/shard_map/ppermute | solution.py:321
  148.7 13.5 %shard_map.74 = bf16[1024,512]{1,0:T(8,128)(2,1)} custom-call(s32[12]{0:T(128)S(1)} %reshape.179.info, s32[118]{0:T(128)S(1)} %dynamic-slice_bitcast_fusion.row.row_ref, bf16[2048,512]{1,0:T(8,128)(2,1)} %q_ref.3, bf16[2048,256]{1,0:T(8,128)(2,1)} %constant_dynamic-update-slice_fusion.refs_1_.kv_ref, bf16[11,512,256]{2,1,0:T(8,128)(2,1)} %get-tuple-element.42.refs_0_, ...), custom_call_target="tpu_custom_call" | custom-call | flops 4294967296 | bytes 4194304 | tf_op jit(solution)/shard_map/pallas_call | solution.py:436
  162.2 6.2 %all-to-all-start = ((bf16[8,128,512]{2,1,0:T(8,128)(2,1)}), bf16[8,128,512]{2,1,0:T(8,128)(2,1)S(1)}, u32[]{:S(2)}, u32[]{:S(2)}) async-start(bf16[8,128,512]{2,1,0:T(8,128)(2,1)} %bitcast.3), calls=%async_computation | async-start | bytes 2097152 | tf_op jit(solution)/shard_map/all_to_all | solution.py:548
  168.3 12.7 %shard_map.75 = bf16[1024,512]{1,0:T(8,128)(2,1)S(1)} custom-call(s32[12]{0:T(128)S(1)} %reshape.179.info, s32[118]{0:T(128)S(1)} %dynamic-slice_bitcast_fusion.row.row_ref, bf16[2048,512]{1,0:T(8,128)(2,1)} %q_ref.3, bf16[2048,256]{1,0:T(8,128)(2,1)} %constant_dynamic-update-slice_fusion.refs_1_.kv_ref, bf16[11,512,256]{2,1,0:T(8,128)(2,1)} %get-tuple-element.42.refs_0_, ...), custom_call_target="tpu_custom_call" | custom-call | flops 4294967296 | bytes 4194304 | tf_op jit(solution)/shard_map/pallas_call | solution.py:436
  181.0 3.2 %all-to-all-done.refs_0_ = bf16[8,128,512]{2,1,0:T(8,128)(2,1)S(1)} async-done(((bf16[8,128,512]{2,1,0:T(8,128)(2,1)}), bf16[8,128,512]{2,1,0:T(8,128)(2,1)S(1)}, u32[]{:S(2)}, u32[]{:S(2)}) %all-to-all-start) | async-done | bytes 1048608 | tf_op jit(solution)/shard_map/all_to_all | solution.py:548
  184.2 21.6 %all_to_all.15.refs_1_ = bf16[8,128,512]{2,1,0:T(8,128)(2,1)S(1)} all-to-all(bf16[8,128,512]{2,1,0:T(8,128)(2,1)S(1)} %bitcast.10), channel_id=1, replica_groups=mesh['ctx'=32,'head'=8] {'head'}, dimensions={0} | all-to-all | bytes 2097152 | tf_op jit(solution)/shard_map/all_to_all | solution.py:548
  205.8 8.9 %shard_map.76 = bf16[8,256,256]{2,1,0:T(8,128)(2,1)S(1)} custom-call(s32[1]{0:T(128)} %bitcast.core, bf16[8,128,512]{2,1,0:T(8,128)(2,1)S(1)} %all-to-all-done.refs_0_, bf16[8,128,512]{2,1,0:T(8,128)(2,1)S(1)} %all_to_all.15.refs_1_, bf16[8,256,2048]{2,1,0:T(8,128)(2,1)} %bitcast.12, bf16[8,256,2048]{2,1,0:T(8,128)(2,1)} %collective-permute-done.25.refs_3_), custom_call_target="tpu_custom_call" | custom-call | flops 4294967296 | bytes 20971520 | tf_op jit(solution)/shard_map/pallas_call | solution.py:493
  214.7 19.2 %all_to_all.16 = bf16[8,256,256]{2,1,0:T(8,128)(2,1)S(1)} all-to-all(bf16[8,256,256]{2,1,0:T(8,128)(2,1)S(1)} %shard_map.76), channel_id=1, replica_groups=mesh['ctx'=32,'head'=8] {'head'}, dimensions={0} | all-to-all | bytes 2097152 | tf_op jit(solution)/shard_map/all_to_all | solution.py:550
  (71 shorter events, 28.7 us)
Async XLA Ops:
  6.5 2.7 %copy-start.4 = (bf16[2048,128]{1,0:T(8,128)(2,1)S(1)}, bf16[2048,128]{1,0:T(8,128)(2,1)}, u32[]{:S(2)}) copy-start(bf16[2048,128]{1,0:T(8,128)(2,1)} %param.7) | copy-start | bytes 1572868
  6.5 3.5 %copy-start.5 = (bf16[2048,128]{1,0:T(8,128)(2,1)S(1)}, bf16[2048,128]{1,0:T(8,128)(2,1)}, u32[]{:S(2)}) copy-start(bf16[2048,128]{1,0:T(8,128)(2,1)} %param.8) | copy-start | bytes 1572868
  6.5 6.4 %copy-start.6 = (s32[4,3]{1,0:T(4,128)S(1)}, s32[4,3]{1,0:T(4,128)}, u32[]{:S(2)}) copy-start(s32[4,3]{1,0:T(4,128)} %param.9) | copy-start | bytes 148
  6.5 141.3 %all-gather.3.cloned.1.call-start = ((), (), s32[]{:S(2)}) async-start(), calls=%async_computation.3 | async-start | bytes 9437184 | tf_op jit(solution)/shard_map/all_gather | solution.py:526
  10.9 4.6 %collective-permute-start.1 = (bf16[2048,256]{1,0:T(8,128)(2,1)}, bf16[2048,256]{1,0:T(8,128)(2,1)S(1)}, u32[]{:S(2)}, u32[]{:S(2)}) collective-permute-start(bf16[2048,256]{1,0:T(8,128)(2,1)} %constant_dynamic-update-slice_fusion.refs_1_.kv_ref), channel_id=1, source_target_pairs={{0,8},{8,0},{16,24},{24,16},{32,40},{40,32},{48,56},{56,48},{64,72... | collective-permute-start | bytes 3145736 | tf_op jit(solution)/shard_map/ppermute | solution.py:288
  10.9 16.9 %collective-permute-start.4 = (bf16[2048,256]{1,0:T(8,128)(2,1)}, bf16[2048,256]{1,0:T(8,128)(2,1)S(1)}, u32[]{:S(2)}, u32[]{:S(2)}) collective-permute-start(bf16[2048,256]{1,0:T(8,128)(2,1)} %constant_dynamic-update-slice_fusion.refs_1_.kv_ref), channel_id=1, source_target_pairs={{0,16},{8,120},{16,32},{24,8},{32,48},{48,64},{64,80},{80,96},{96,... | collective-permute-start | bytes 3145736 | tf_op jit(solution)/shard_map/ppermute | solution.py:317
  12.2 15.6 %collective-permute-start.5 = (bf16[2048,256]{1,0:T(8,128)(2,1)}, bf16[2048,256]{1,0:T(8,128)(2,1)S(1)}, u32[]{:S(2)}, u32[]{:S(2)}) collective-permute-start(bf16[2048,256]{1,0:T(8,128)(2,1)} %constant_dynamic-update-slice_fusion.refs_1_.kv_ref), channel_id=1, source_target_pairs={{8,136},{24,152},{40,168},{56,184},{72,200},{88,216},{104,232},{12... | collective-permute-start | bytes 3145736 | tf_op jit(solution)/shard_map/ppermute | solution.py:317
  12.9 2.0 collective-permute-start
  16.1 22.9 %collective-permute-start.2 = (bf16[2048,256]{1,0:T(8,128)(2,1)S(1)}, bf16[2048,256]{1,0:T(8,128)(2,1)S(1)}, u32[]{:S(2)}, u32[]{:S(2)}) collective-permute-start(bf16[2048,256]{1,0:T(8,128)(2,1)S(1)} %get-tuple-element.31.refs_2_), channel_id=1, source_target_pairs={{0,16},{8,120},{16,32},{24,8},{32,48},{48,64},{64,80},{80,96},{96,... | collective-permute-start | bytes 3145736 | tf_op jit(solution)/shard_map/ppermute | solution.py:317
  17.4 21.6 %collective-permute-start.3 = (bf16[2048,256]{1,0:T(8,128)(2,1)S(1)}, bf16[2048,256]{1,0:T(8,128)(2,1)S(1)}, u32[]{:S(2)}, u32[]{:S(2)}) collective-permute-start(bf16[2048,256]{1,0:T(8,128)(2,1)S(1)} %get-tuple-element.32), channel_id=1, source_target_pairs={{8,136},{24,152},{40,168},{56,184},{72,200},{88,216},{104,232},{12... | collective-permute-start | bytes 3145736 | tf_op jit(solution)/shard_map/ppermute | solution.py:317
  28.4 21.9 %collective-permute-start.8 = (bf16[2048,256]{1,0:T(8,128)(2,1)S(1)}, bf16[2048,256]{1,0:T(8,128)(2,1)S(1)}, u32[]{:S(2)}, u32[]{:S(2)}) collective-permute-start(bf16[2048,256]{1,0:T(8,128)(2,1)S(1)} %get-tuple-element.33.refs_2_), channel_id=1, source_target_pairs={{8,120},{16,32},{32,48},{48,64},{64,80},{80,96},{96,112},{120,104}... | collective-permute-start | bytes 3145736 | tf_op jit(solution)/shard_map/ppermute | solution.py:317
  29.7 21.4 %collective-permute-start.9 = (bf16[2048,256]{1,0:T(8,128)(2,1)S(1)}, bf16[2048,256]{1,0:T(8,128)(2,1)S(1)}, u32[]{:S(2)}, u32[]{:S(2)}) collective-permute-start(bf16[2048,256]{1,0:T(8,128)(2,1)S(1)} %get-tuple-element.36), channel_id=1, source_target_pairs={{0,128},{16,144},{32,160},{48,176},{64,192},{80,208},{96,224},{112... | collective-permute-start | bytes 3145736 | tf_op jit(solution)/shard_map/ppermute | solution.py:317
  39.6 21.9 %collective-permute-start.6 = (bf16[2048,256]{1,0:T(8,128)(2,1)S(1)}, bf16[2048,256]{1,0:T(8,128)(2,1)S(1)}, u32[]{:S(2)}, u32[]{:S(2)}) collective-permute-start(bf16[2048,256]{1,0:T(8,128)(2,1)S(1)} %get-tuple-element.34.refs_3_), channel_id=1, source_target_pairs={{8,120},{16,32},{32,48},{48,64},{64,80},{80,96},{96,112},{120,104}... | collective-permute-start | bytes 3145736 | tf_op jit(solution)/shard_map/ppermute | solution.py:317
  40.9 21.4 %collective-permute-start.7 = (bf16[2048,256]{1,0:T(8,128)(2,1)S(1)}, bf16[2048,256]{1,0:T(8,128)(2,1)S(1)}, u32[]{:S(2)}, u32[]{:S(2)}) collective-permute-start(bf16[2048,256]{1,0:T(8,128)(2,1)S(1)} %get-tuple-element.35), channel_id=1, source_target_pairs={{0,128},{16,144},{32,160},{48,176},{64,192},{80,208},{96,224},{112... | collective-permute-start | bytes 3145736 | tf_op jit(solution)/shard_map/ppermute | solution.py:317
  51.7 21.0 %collective-permute-start.12 = (bf16[2048,256]{1,0:T(8,128)(2,1)S(1)}, bf16[2048,256]{1,0:T(8,128)(2,1)S(1)}, u32[]{:S(2)}, u32[]{:S(2)}) collective-permute-start(bf16[2048,256]{1,0:T(8,128)(2,1)S(1)} %get-tuple-element.37.refs_4_), channel_id=1, source_target_pairs={{32,48},{48,64},{64,80},{80,96},{96,112},{104,88},{120,104},{128,1... | collective-permute-start | bytes 3145736 | tf_op jit(solution)/shard_map/ppermute | solution.py:317
  57.2 16.7 %collective-permute-start.13 = (bf16[2048,256]{1,0:T(8,128)(2,1)S(1)}, bf16[2048,256]{1,0:T(8,128)(2,1)S(1)}, u32[]{:S(2)}, u32[]{:S(2)}) collective-permute-start(bf16[2048,256]{1,0:T(8,128)(2,1)S(1)} %get-tuple-element.40), channel_id=1, source_target_pairs={{32,160},{48,176},{64,192},{80,208},{96,224},{112,240},{33,161},{4... | collective-permute-start | bytes 3145736 | tf_op jit(solution)/shard_map/ppermute | solution.py:317
  63.0 21.0 %collective-permute-start.10 = (bf16[2048,256]{1,0:T(8,128)(2,1)S(1)}, bf16[2048,256]{1,0:T(8,128)(2,1)S(1)}, u32[]{:S(2)}, u32[]{:S(2)}) collective-permute-start(bf16[2048,256]{1,0:T(8,128)(2,1)S(1)} %get-tuple-element.38.refs_2_), channel_id=1, source_target_pairs={{32,48},{48,64},{64,80},{80,96},{96,112},{104,88},{120,104},{128,1... | collective-permute-start | bytes 3145736 | tf_op jit(solution)/shard_map/ppermute | solution.py:317
  68.5 16.7 %collective-permute-start.11 = (bf16[2048,256]{1,0:T(8,128)(2,1)S(1)}, bf16[2048,256]{1,0:T(8,128)(2,1)S(1)}, u32[]{:S(2)}, u32[]{:S(2)}) collective-permute-start(bf16[2048,256]{1,0:T(8,128)(2,1)S(1)} %get-tuple-element.39), channel_id=1, source_target_pairs={{32,160},{48,176},{64,192},{80,208},{104,232},{112,240},{33,161},{... | collective-permute-start | bytes 3145736 | tf_op jit(solution)/shard_map/ppermute | solution.py:317
  74.6 25.7 %collective-permute-start.15 = (bf16[2048,256]{1,0:T(8,128)(2,1)S(1)}, bf16[2048,256]{1,0:T(8,128)(2,1)S(1)}, u32[]{:S(2)}, u32[]{:S(2)}) collective-permute-start(bf16[2048,256]{1,0:T(8,128)(2,1)S(1)} %get-tuple-element.41.refs_13_), channel_id=1, source_target_pairs={{48,64},{64,80},{80,96},{88,72},{96,112},{104,88},{128,144},{136,2... | collective-permute-start | bytes 3145736 | tf_op jit(solution)/shard_map/ppermute | solution.py:317
  76.5 23.8 %collective-permute-start.17 = (bf16[2048,256]{1,0:T(8,128)(2,1)S(1)}, bf16[2048,256]{1,0:T(8,128)(2,1)S(1)}, u32[]{:S(2)}, u32[]{:S(2)}) collective-permute-start(bf16[2048,256]{1,0:T(8,128)(2,1)S(1)} %get-tuple-element.45), channel_id=1, source_target_pairs={{64,192},{80,208},{104,232},{112,240},{65,193},{81,209},{105,233},... | collective-permute-start | bytes 3145736 | tf_op jit(solution)/shard_map/ppermute | solution.py:317
  89.8 52.7 %collective-permute-start.22 = (bf16[11,512,256]{2,1,0:T(8,128)(2,1)}, bf16[11,512,256]{2,1,0:T(8,128)(2,1)S(1)}, u32[]{:S(2)}, u32[]{:S(2)}) collective-permute-start(bf16[11,512,256]{2,1,0:T(8,128)(2,1)} %get-tuple-element.51), channel_id=1, source_target_pairs={{0,8},{8,0},{16,24},{24,16},{32,40},{40,32},{48,56},{56,48},{64,72... | collective-permute-start | bytes 8650760 | tf_op jit(solution)/shard_map/ppermute | solution.py:321
  95.3 16.7 %collective-permute-start.14 = (bf16[2048,256]{1,0:T(8,128)(2,1)S(1)}, bf16[2048,256]{1,0:T(8,128)(2,1)S(1)}, u32[]{:S(2)}, u32[]{:S(2)}) collective-permute-start(bf16[2048,256]{1,0:T(8,128)(2,1)S(1)} %get-tuple-element.43.refs_5_), channel_id=1, source_target_pairs={{80,96},{96,112},{128,144},{136,248},{144,160},{152,136},{168,152}... | collective-permute-start | bytes 3145736 | tf_op jit(solution)/shard_map/ppermute | solution.py:317
  99.0 23.4 %collective-permute-start.16 = (bf16[2048,256]{1,0:T(8,128)(2,1)S(1)}, bf16[2048,256]{1,0:T(8,128)(2,1)S(1)}, u32[]{:S(2)}, u32[]{:S(2)}) collective-permute-start(bf16[2048,256]{1,0:T(8,128)(2,1)S(1)} %get-tuple-element.44), channel_id=1, source_target_pairs={{48,176},{64,192},{88,216},{96,224},{112,240},{49,177},{65,193},{8... | collective-permute-start | bytes 3145736 | tf_op jit(solution)/shard_map/ppermute | solution.py:317
  101.0 26.2 %collective-permute-start.18 = (bf16[2048,256]{1,0:T(8,128)(2,1)S(1)}, bf16[2048,256]{1,0:T(8,128)(2,1)S(1)}, u32[]{:S(2)}, u32[]{:S(2)}) collective-permute-start(bf16[2048,256]{1,0:T(8,128)(2,1)S(1)} %get-tuple-element.46.refs_6_), channel_id=1, source_target_pairs={{96,112},{128,144},{136,248},{144,160},{152,136},{160,176},{168,15... | collective-permute-start | bytes 3145736 | tf_op jit(solution)/shard_map/ppermute | solution.py:317
  102.9 24.3 %collective-permute-start.20 = (bf16[2048,256]{1,0:T(8,128)(2,1)S(1)}, bf16[2048,256]{1,0:T(8,128)(2,1)S(1)}, u32[]{:S(2)}, u32[]{:S(2)}) collective-permute-start(bf16[2048,256]{1,0:T(8,128)(2,1)S(1)} %get-tuple-element.49), channel_id=1, source_target_pairs={{72,200},{88,216},{96,224},{120,248},{73,201},{89,217},{97,225},{1... | collective-permute-start | bytes 3145736 | tf_op jit(solution)/shard_map/ppermute | solution.py:317
  124.5 16.7 %collective-permute-start.19 = (bf16[2048,256]{1,0:T(8,128)(2,1)S(1)}, bf16[2048,256]{1,0:T(8,128)(2,1)S(1)}, u32[]{:S(2)}, u32[]{:S(2)}) collective-permute-start(bf16[2048,256]{1,0:T(8,128)(2,1)S(1)} %get-tuple-element.48), channel_id=1, source_target_pairs={{96,112},{136,248},{192,208},{208,224},{224,240},{248,232},{97,113... | collective-permute-start | bytes 3145736 | tf_op jit(solution)/shard_map/ppermute | solution.py:317
  125.8 16.7 %collective-permute-start.21 = (bf16[2048,256]{1,0:T(8,128)(2,1)S(1)}, bf16[2048,256]{1,0:T(8,128)(2,1)S(1)}, u32[]{:S(2)}, u32[]{:S(2)}) collective-permute-start(bf16[2048,256]{1,0:T(8,128)(2,1)S(1)} %get-tuple-element.50), channel_id=1, source_target_pairs={{104,232},{112,240},{105,233},{113,241},{106,234},{114,242},{107,2... | collective-permute-start | bytes 3145736 | tf_op jit(solution)/shard_map/ppermute | solution.py:317
  127.1 15.4 %collective-permute-start.23 = (bf16[4,512,256]{2,1,0:T(8,128)(2,1)}, bf16[4,512,256]{2,1,0:T(8,128)(2,1)S(1)}, u32[]{:S(2)}, u32[]{:S(2)}) collective-permute-start(bf16[4,512,256]{2,1,0:T(8,128)(2,1)} %get-tuple-element.52), channel_id=1, source_target_pairs={{0,8},{8,0},{16,24},{24,16},{32,40},{40,32},{48,56},{56,48},{64,72... | collective-permute-start | bytes 3145736 | tf_op jit(solution)/shard_map/ppermute | solution.py:321
  145.1 2.8 %collective-permute-start.24 = (bf16[3,512,256]{2,1,0:T(8,128)(2,1)}, bf16[3,512,256]{2,1,0:T(8,128)(2,1)S(1)}, u32[]{:S(2)}, u32[]{:S(2)}) collective-permute-start(bf16[3,512,256]{2,1,0:T(8,128)(2,1)} %get-tuple-element.54), channel_id=1, source_target_pairs={{0,8},{8,0},{16,24},{24,16},{32,40},{40,32},{48,56},{56,48},{64,72... | collective-permute-start | bytes 2359304 | tf_op jit(solution)/shard_map/ppermute | solution.py:321
  147.8 58.0 %collective-permute-start.25 = (bf16[8,256,2048]{2,1,0:T(8,128)(2,1)}, bf16[8,256,2048]{2,1,0:T(8,128)(2,1)}, u32[]{:S(2)}, u32[]{:S(2)}) collective-permute-start(bf16[8,256,2048]{2,1,0:T(8,128)(2,1)} %bitcast.11), channel_id=1, source_target_pairs={{0,8},{8,0},{16,24},{24,16},{32,40},{40,32},{48,56},{56,48},{64,72... | collective-permute-start | bytes 25165832 | tf_op jit(solution)/shard_map/ppermute | solution.py:539
  162.2 22.0 %all-to-all-start = ((bf16[8,128,512]{2,1,0:T(8,128)(2,1)}), bf16[8,128,512]{2,1,0:T(8,128)(2,1)S(1)}, u32[]{:S(2)}, u32[]{:S(2)}) async-start(bf16[8,128,512]{2,1,0:T(8,128)(2,1)} %bitcast.3), calls=%async_computation | async-start | bytes 2097152 | tf_op jit(solution)/shard_map/all_to_all | solution.py:548
  205.8 29.2 %copy-start.1 = (bf16[512,2048]{1,0:T(8,128)(2,1)S(1)}, bf16[512,2048]{1,0:T(8,128)(2,1)}, u32[]{:S(2)}) copy-start(bf16[512,2048]{1,0:T(8,128)(2,1)} %param.10) | copy-start | bytes 6291460
  (4 other events, 7.5 us)
Sparse Core Ops, SparseCore 0:
  9.3 94.8 all-gather.2

commit v5 on v3

--- a/solution.py
+++ b/solution.py
@@ -21,106 +21,96 @@
 SCHEDULE = (
     (
         (
-            0, 1, 2, 3, 4, -1, 6, -1, 8, -1, 10, -1, 12, -1, 14, -1,
-            16, 17, 18, 19, 20, -1, 22, -1, 24, -1, 26, -1, 28, -1, -1, -1,
-        ),
-        (
-            -1, 1, -1, 3, -1, 5, -1, 7, -1, 9, -1, 11, -1, 13, -1, 15,
-            -1, -1, -1, -1, -1, -1, -1, -1, -1, -1, -1, -1, -1, -1, -1, -1,
-        ),
-    ),
-    (
-        (
-            1, 0, 3, 2, 5, -1, 7, -1, 9, -1, 11, -1, 13, -1, 15, -1,
-            17, 16, 19, 18, 21, -1, 23, -1, 25, -1, 27, -1, 29, -1, -1, -1,
-        ),
-        (
-            -1, 0, -1, 2, -1, 4, -1, 6, -1, 8, -1, 10, -1, 12, -1, 14,
-            -1, -1, -1, -1, -1, -1, -1, -1, -1, -1, -1, -1, -1, -1, -1, -1,
-        ),
-    ),
-    (
-        (
-            -1, 3, 0, -1, 2, -1, 4, -1, 6, -1, 8, -1, 10, -1, -1, 1,
-            -1, 1, 16, 3, 18, 5, 20, 7, 22, 9, 24, 11, 26, 13, -1, 15,
-        ),
-        (
-            14, -1, 0, -1, 2, -1, 4, -1, 6, -1, 8, -1, 10, -1, 12, -1,
+            0, 1, 2, 3, 4, 5, 6, -1, 8, -1, 10, -1, 12, -1, -1, 15,
+            16, 17, 18, 19, 20, 21, 22, -1, 24, -1, 26, -1, -1, -1, -1, -1,
+        ),
+        (
+            -1, 1, -1, 3, -1, -1, -1, 7, -1, 9, -1, 11, -1, 13, 14, -1,
+            -1, -1, -1, -1, -1, -1, -1, -1, -1, -1, -1, -1, -1, -1, -1, -1,
+        ),
+    ),
+    (
+        (
+            1, 0, 3, 2, 5, -1, 7, -1, 9, -1, 11, -1, 13, -1, -1, 14,
+            17, 16, 19, 18, 21, -1, 23, -1, 25, -1, 27, -1, -1, -1, -1, -1,
+        ),
+        (
+            -1, 0, -1, -1, -1, 4, -1, 6, -1, 8, -1, 10, -1, 12, 15, -1,
+            -1, -1, -1, -1, -1, -1, -1, -1, -1, -1, -1, -1, -1, -1, -1, -1,
+        ),
+    ),
+    (
+        (
+            -1, 3, 0, 5, 2, -1, 4, -1, 6, -1, 8, -1, 10, -1, -1, 1,
+            -1, 19, 16, 21, 18, -1, 20, 7, 22, 9, 24, 11, 1018, 13, 14, 17,
+        ),
+        (
+            -1, 3, -1, 226, 226, -1, 36, -1, 38, -1, 40, -1, -1, 15, 12, -1,
             -1, -1, -1, -1, -1, -1, -1, -1, -1, -1, -1, -1, -1, -1, -1, -1,
         ),
     ),
     (
         (
             -1, 2, 1, -1, 3, -1, 5, -1, 7, -1, 9, -1, 11, -1, -1, 0,
-            -1, 18, 17, 2, 19, 4, 21, 6, 23, 8, 25, 10, 27, 12, -1, 14,
-        ),
-        (
-            15, -1, 1, -1, 3, -1, 5, -1, 7, -1, 9, -1, 11, -1, 13, -1,
-            -1, -1, -1, -1, -1, -1, -1, -1, -1, -1, -1, -1, -1, -1, -1, -1,
-        ),
-    ),
-    (
-        (
-            -1, -1, -1, -1, 0, -1, 2, -1, 4, -1, 6, -1, 8, 1, -1, 3,
-            14, 19, -1, 5, 16, 7, 18, 9, 20, 11, 22, 13, 24, 15, 12, 1,
-        ),
-        (
-            -1, -1, -1, -1, 0, -1, 2, -1, 4, -1, 6, -1, 8, -1, 10, -1,
-            -1, -1, -1, -1, -1, -1, -1, -1, -1, -1, -1, -1, -1, -1, -1, -1,
-        ),
-    ),
-    (
-        (
-            -1, -1, -1, -1, 1, -1, 3, -1, 5, -1, 7, -1, 9, 0, -1, 2,
-            15, 0, -1, 4, 17, 6, 19, 8, 21, 10, 23, 12, 25, 14, 13, 16,
-        ),
-        (
-            -1, -1, -1, -1, 1, -1, 3, -1, 5, -1, 7, -1, -1, 0, 11, -1,
-            -1, -1, -1, -1, -1, -1, -1, -1, -1, -1, -1, -1, -1, -1, -1, -1,
-        ),
-    ),
-    (
-        (
-            -1, -1, -1, -1, -1, -1, 0, -1, 2, -1, 4, 1, 6, 3, -1, -1,
-            12, 5, 14, 7, 0, 9, 16, 11, 18, 13, 20, 15, 22, 1, 10, 19,
-        ),
-        (
-            -1, -1, -1, -1, -1, -1, -1, -1, 2, -1, 4, -1, -1, 3, 8, -1,
-            -1, -1, -1, -1, -1, -1, -1, -1, -1, -1, -1, -1, -1, -1, -1, -1,
-        ),
-    ),
-    (
-        (
-            -1, -1, -1, -1, -1, -1, -1, -1, -1, -1, 5, -1, 7, -1, -1, -1,
-            13, 4, 15, 6, -1, 8, 17, 10, 5, 12, 21, 14, 23, 16, 11, 17,
-        ),
-        (
-            -1, -1, -1, -1, -1, -1, 1, -1, 3, -1, -1, 0, 7, -1, 9, -1,
-            -1, -1, -1, -1, -1, -1, -1, -1, -1, -1, -1, -1, -1, -1, -1, -1,
-        ),
-    ),
-    (
-        (
-            -1, -1, -1, -1, -1, -1, -1, -1, -1, -1, -1, -1, 4, -1, -1, -1,
-            10, 2, 12, 9, 14, 11, 0, 13, 2, 15, 18, -1, 20, 19, 8, 5,
-        ),
-        (
-            -1, -1, -1, -1, -1, -1, -1, -1, -1, 1, -1, 3, 6, -1, -1, 3,
-            -1, -1, -1, -1, -1, -1, -1, -1, -1, -1, -1, -1, -1, -1, -1, -1,
-        ),
-    ),
-    (
-        (
-            -1, -1, -1, -1, -1, -1, -1, -1, -1, -1, -1, -1, 5, -1, -1, -1,
-            -1, 6, -1, -1, -1, -1, -1, -1, 17, -1, 9, -1, 21, -1, -1, 4,
-        ),
-        (
-            -1, -1, -1, -1, -1, -1, -1, -1, -1, -1, -1, -1, -1, 2, 7, -1,
+            -1, 18, 17, -1, 19, 4, 21, 6, 23, 8, 25, 10, 987, 12, 15, 16,
+        ),
+        (
+            -1, 2, 96, -1, 35, -1, 37, -1, 39, -1, 41, -1, 426, -1, 13, -1,
+            -1, -1, -1, -1, -1, -1, -1, -1, -1, -1, -1, -1, -1, -1, -1, -1,
+        ),
+    ),
+    (
+        (
+            -1, 5, -1, -1, 0, -1, 2, -1, 4, -1, 6, -1, 8, 1, -1, 3,
+            14, 736, -1, -1, 16, 7, 18, 9, 20, 11, 22, 13, 56, 15, 12, 19,
+        ),
+        (
+            -1, 5, -1, -1, 32, -1, 34, -1, 4, -1, -1, -1, -1, 14, 10, -1,
+            -1, -1, -1, -1, -1, -1, -1, -1, -1, -1, -1, -1, -1, -1, -1, -1,
+        ),
+    ),
+    (
+        (
+            -1, -1, -1, -1, 33, -1, 35, -1, 37, -1, 7, -1, 9, 0, -1, 2,
+            15, 129, -1, 4, 17, 6, 51, 8, 21, 10, 23, 12, 57, 624, 13, 50,
+        ),
+        (
+            -1, -1, -1, -1, 1, -1, 3, -1, 5, -1, 294, -1, 360, -1, 11, -1,
+            -1, -1, -1, -1, -1, -1, -1, -1, -1, -1, -1, -1, -1, -1, -1, -1,
+        ),
+    ),
+    (
+        (
+            -1, -1, -1, -1, -1, -1, 0, -1, 34, -1, 4, 33, 6, 3, -1, 37,
+            12, 5, 14, 7, -1, 9, 48, 11, 4, 13, 20, 15, 54, 14, 10, -1,
+        ),
+        (
+            -1, -1, -1, -1, -1, -1, 32, -1, 2, -1, -1, 1, -1, 160, 8, -1,
+            -1, -1, -1, -1, -1, -1, -1, -1, -1, -1, -1, -1, -1, -1, -1, -1,
+        ),
+    ),
+    (
+        (
+            -1, -1, -1, -1, -1, -1, -1, -1, -1, -1, -1, -1, 39, -1, -1, -1,
+            45, 195, 15, 38, 33, 40, 611, 42, 645, 44, 53, -1, 55, 51, 43, -1,
+        ),
+        (
+            -1, -1, -1, -1, -1, -1, -1, -1, -1, -1, -1, 32, -1, 129, 41, -1,
+            -1, -1, -1, -1, -1, -1, -1, -1, -1, -1, -1, -1, -1, -1, -1, -1,
+        ),
+    ),
+    (
+        (
+            -1, -1, -1, -1, -1, -1, -1, -1, -1, -1, -1, -1, 36, -1, -1, -1,
+            42, 7, 44, 41, 46, 43, -1, 45, 34, 47, 36, 513, 52, -1, 40, 37,
+        ),
+        (
+            -1, -1, -1, -1, -1, -1, -1, -1, 32, -1, -1, 35, 294, -1, 38, -1,
             -1, -1, -1, -1, -1, -1, -1, -1, -1, -1, -1, -1, -1, -1, -1, -1,
         ),
     ),
 )
-CHECKPOINTS = (5, 7, 9)
+CHECKPOINTS = (4, 6, 7, 8)
 COST = 12
 
 
@@ -131,17 +121,28 @@
     return side * (CORES // 2) + (place + (2 if core % 2 == 0 else -2)) % (CORES // 2)
 
 
+def owners_of(item):
+    if item < CORES:
+        return [item] if item >= 0 else [], []
+    second, first = divmod(item - CORES, CORES)
+    return [], [first] + ([second - 1] if second else [])
+
+
 def plan():
     found = [{core: "own", core ^ 1: "other"} for core in range(CORES)]
+    parts = [{} for _ in range(CORES)]
     for step, sends in enumerate(SCHEDULE):
         for way, row in enumerate(sends):
-            for core, owner in enumerate(row):
-                if owner >= 0:
+            for core, item in enumerate(row):
+                whole, wanted = owners_of(item)
+                for owner in whole:
                     found[target(way, core)].setdefault(owner, (step, way))
-    return found
-
-
-def batches(found):
+                for position, owner in enumerate(wanted):
+                    parts[target(way, core)].setdefault(owner, (step, way, position))
+    return found, parts
+
+
+def batches(found, parts):
     out = []
     for number, last in enumerate(CHECKPOINTS):
         first = -2 if number == 0 else CHECKPOINTS[number - 1]
@@ -149,11 +150,11 @@
             [
                 [
                     owner
-                    for owner, place in sorted(held.items())
+                    for owner, place in sorted((parts[core] | found[core]).items())
                     if (owner // 2 < core // 2 or owner == core ^ 1)
                     and first < (-1 if isinstance(place, str) else place[0]) <= last
                 ]
-                for core, held in enumerate(found)
+                for core in range(CORES)
             ]
         )
     return out
@@ -182,16 +183,27 @@
     outs = len(ways) + (2 if slots else 0)
     ins, outs, sems = refs[: -outs - 1], refs[-outs - 1 : -1], refs[-1]
 
-    def block_of(slot, which):
-        owner = row[slot_base + 2 * slot]
-        block = jnp.where(owner >= 0, want[which * CORES + jnp.maximum(owner, 0)], -1)
-        source = jnp.where(block >= 0, row[slot_base + 2 * slot + 1], -1)
-        return source, jnp.maximum(block, 0) * BLOCK_TOKENS
-
-    jobs = [(numbers, row[way_base + i], 0, ROWS, outs[i]) for i, numbers in enumerate(ways)]
+    def wanted(who, owner):
+        return jnp.where(owner >= 0, want[who * CORES + jnp.maximum(owner, 0)], -1)
+
+    jobs = []
+    for way, (whole, *parts) in enumerate(ways):
+        base = way_base + 5 * way
+        if whole:
+            jobs.append((whole, row[base], 0, ROWS, outs[way]))
+        for position, numbers in enumerate(parts):
+            for core in range(2 if numbers else 0):
+                block = wanted(2 + 2 * way + core, row[base + 1 + 2 * position])
+                to = outs[way].at[pl.ds((2 * position + core) * BLOCK_TOKENS, BLOCK_TOKENS)]
+                source = jnp.where(block >= 0, row[base + 2 + 2 * position], -1)
+                jobs.append((numbers, source, jnp.maximum(block, 0) * BLOCK_TOKENS, BLOCK_TOKENS, to))
     for slot, numbers in enumerate(slots):
+        base = slot_base + 4 * slot
         for which in range(2):
-            source, first = block_of(slot, which)
+            block = wanted(which, row[base])
+            at = row[base + 2 + which]
+            first = jnp.where(at >= 0, at, jnp.maximum(block, 0) * BLOCK_TOKENS)
+            source = jnp.where(block >= 0, row[base + 1], -1)
             jobs.append((numbers, source, first, BLOCK_TOKENS, outs[len(ways) + which].at[slot]))
     for i, (numbers, source, first, rows, to) in enumerate(jobs):
         start_from(ins, numbers, source, first, rows, to, sems.at[i])
@@ -216,7 +228,7 @@
             grid=(1,),
             in_specs=[pl.BlockSpec(memory_space=pltpu.HBM)] * (len(arrays) + len(after)),
             out_specs=[whole(s) for s in out_shapes],
-            scratch_shapes=[pltpu.SemaphoreType.DMA((len(ways[0]) + 2 * len(slots[0]),))],
+            scratch_shapes=[pltpu.SemaphoreType.DMA((5 * len(ways[0]) + 2 * len(slots[0]),))],
         ),
         compiler_params=pltpu.CompilerParams(vmem_limit_bytes=24 * 1024 * 1024),
         cost_estimate=pl.CostEstimate(
@@ -229,8 +241,8 @@
 
 class Plan:
     def __init__(self):
-        found = plan()
-        groups = batches(found)
+        found, parts = plan()
+        groups = batches(found, parts)
         columns = []
         self.ways, self.slots, self.sources = {}, {}, {}
 
@@ -246,14 +258,19 @@
 
         for step in range(1, len(SCHEDULE)):
             sources, numbers = self.sources.setdefault(step, []), []
-            table = np.full((CORES, 2), -1, np.int32)
+            table = np.full((CORES, 2, 5), -1, np.int32)
             for way in range(2):
-                used = set()
-                for core, owner in enumerate(SCHEDULE[step][way]):
-                    if owner >= 0:
-                        table[core, way] = number_of(found[core][owner], sources)
-                        used.add(int(table[core, way]))
-                numbers.append(tuple(sorted(used)))
+                used = [set(), set(), set()]
+                for core, item in enumerate(SCHEDULE[step][way]):
+                    whole, wanted = owners_of(item)
+                    for owner in whole:
+                        table[core, way, 0] = number_of(found[core][owner], sources)
+                        used[0].add(int(table[core, way, 0]))
+                    for i, owner in enumerate(wanted):
+                        number = number_of(found[core][owner], sources)
+                        table[core, way, 1 + 2 * i : 3 + 2 * i] = owner, number
+                        used[1 + i].add(number)
+                numbers.append(tuple(tuple(sorted(n)) for n in used))
             self.ways[step] = (tuple(numbers), add(table))
 
         held = np.full((CORES, CORES, 2), -1, np.int32)
@@ -261,12 +278,19 @@
             depth = max(len(owners) for owners in group)
             step = CHECKPOINTS[batch] + 2
             sources, numbers = self.sources.setdefault(step, []), [set() for _ in range(depth)]
-            table = np.full((CORES, depth, 2), -1, np.int32)
+            table = np.full((CORES, depth, 4), -1, np.int32)
             for core, owners in enumerate(group):
                 for slot, owner in enumerate(owners):
                     held[core, owner] = (batch, slot)
-                    table[core, slot] = owner, number_of(found[core][owner], sources)
-                    numbers[slot].add(int(table[core, slot, 1]))
+                    if owner in found[core]:
+                        number = number_of(found[core][owner], sources)
+                        table[core, slot, :2] = owner, number
+                    else:
+                        *place, position = parts[core][owner]
+                        number = number_of(tuple(place), sources)
+                        rows = [(2 * position + c) * BLOCK_TOKENS for c in (core % 2, 1 - core % 2)]
+                        table[core, slot] = owner, number, *rows
+                    numbers[slot].add(number)
             self.slots[step] = (tuple(tuple(sorted(n)) for n in numbers), add(table))
         place = held.copy()
         for core in range(CORES):
@@ -289,7 +313,12 @@
     def pairs(step, way):
         return [(a, target(way, a)) for a, owner in enumerate(SCHEDULE[step][way]) if owner >= 0]
 
-    choices = jnp.stack([selected.reshape(-1), other_selected.reshape(-1)])[:, None, :]
+    mine, other = selected.reshape(1, -1), other_selected.reshape(1, -1)
+    chip = jnp.where(index % 2 == 0, jnp.concatenate([mine, other]), jnp.concatenate([other, mine]))
+    along, across = (
+        lax.ppermute(chip, "ctx", [(target(way, i), i) for i in range(CORES >> way)]) for way in range(2)
+    )
+    choices = jnp.concatenate([mine, other, along, across])[:, None, :]
     owner = jnp.arange(CORES, dtype=jnp.int32)[None, :, None]
     named = (choices >= 0) & (choices // BLOCKS == owner)
     want = jnp.max(jnp.where(named, choices % BLOCKS, -1), axis=2).reshape(-1)
@@ -304,10 +333,10 @@
             buffers = move(
                 ways,
                 slots,
-                [row, want],
+                [row, want if step > 1 else row],
                 [arrived[key] for key in tables.sources[step]],
                 kv.shape[1],
-                after=buffers[:1] if ways[0] else passed,
+                after=buffers[:1] if step <= len(SCHEDULE) else passed,
             )
         else:
             continue

time: 243 us -> 225 us (0.926)
  waiting for transfers between devices: 78.4 us -> 56.9 us
  Pallas kernels: 45.3 us -> 50.5 us
  starting transfers between devices: 43.3 us -> 40.7 us
    ppermute x20 -> x18, waiting for transfers between devices: 75.8 us -> 54.3 us  [exchange(): arrived[step, way] = lax.ppermute(buffers[way], 'ctx', pairs(step, way))]
    ppermute x0 -> x2, starting transfers between devices: none -> 6.33 us  [exchange(): lax.ppermute(chip, 'ctx', [(target(way, i), i) for i in range(CORES >> wa...]
    ppermute x20 -> x18, starting transfers between devices: 36.1 us -> 30.2 us  [exchange(): arrived[step, way] = lax.ppermute(buffers[way], 'ctx', pairs(step, way))]
    pallas_call x10, Pallas kernels: 13.7 us -> 18.8 us  [move(): pl.pallas_call(functools.partial(move_kernel, *ways, *slots), out_shape=[...]
    ppermute x3 -> x4, starting transfers between devices: 5.91 us -> 3.53 us  [exchange(): passed.append(lax.ppermute(give, 'ctx', SWAP))]
  transfers between devices with their start and end apart: 27 -> 28, of which waited for: 15 -> 15; matrix products, arithmetic and copies ran while one was open for 1% -> 1% of each run, Pallas kernels for 15% -> 19%
where the time goes in v5:
time: 225 us; the launch traced here: 223 us
  waiting for transfers between devices  56.9 us (25%)
  blocking collectives  53.7 us (24%)
  Pallas kernels  50.5 us (22%)
  starting transfers between devices  40.7 us (18%)
  between operations  13.8 us (6%)
  local copies, waits for them, and re-layouts  7.05 us (3%)
    ppermute x18, waiting for transfers between devices, exchange(): arrived[step, way] = lax.ppermute(buffers[way], 'ctx', pairs(step, way))  54.3 us
    all_to_all x1, blocking collectives, per_device(): lax.all_to_all(attended.reshape(head_count, rows // head_count, width), '...  34.3 us
    ppermute x18, starting transfers between devices, exchange(): arrived[step, way] = lax.ppermute(buffers[way], 'ctx', pairs(step, way))  30.2 us
    pallas_call x1, Pallas kernels, attention(): pl.pallas_call(functools.partial(attention_kernel, width // HEAD_SIZE, le...  22.7 us
    all_to_all x1, blocking collectives, per_device(): return lax.all_to_all(mixed, 'head', 0, 0, tiled=True).reshape(rows, -1)  19.3 us
    pallas_call x10, Pallas kernels, move(): pl.pallas_call(functools.partial(move_kernel, *ways, *slots), out_shape=[...  18.8 us
    pallas_call x1, Pallas kernels, project(): pl.pallas_call(functools.partial(project_kernel, depth), out_shape=jax.Sh...  8.91 us
    ppermute x2, starting transfers between devices, exchange(): lax.ppermute(chip, 'ctx', [(target(way, i), i) for i in range(CORES >> wa...  6.33 us
  transfers between devices with their start and end apart: 28, of which 15 were waited for; matrix products, arithmetic and copies ran while one was open for 1% of the time, Pallas kernels for 19%

profile of v5, /device:TPU:226, one launch (start us, length us, event | category | flops | bytes accessed | tf_op | source)
XLA Modules:
  0.0 222.7 jit_solution(5982881006901566867)
XLA Ops:
  15.2 5.3 %collective-permute-start.2 = (s32[2,12]{1,0:T(2,128)S(1)}, s32[2,12]{1,0:T(2,128)S(1)}, u32[]{:S(2)}, u32[]{:S(2)}) collective-permute-start(s32[2,12]{1,0:T(2,128)S(1)} %add_select_fusion.2), channel_id=1, source_target_pairs={{128,0},{136,8},{144,16},{152,24},{160,32},{168,40},{176,48},{184,... | collective-permute-start | bytes 296 | tf_op jit(solution)/shard_map/ppermute | solution.py:319
  21.6 2.0 shard_map.64
  25.9 3.7 %collective-permute-done.4.refs_1_.refs_8_ = bf16[2048,256]{1,0:T(8,128)(2,1)} collective-permute-done((bf16[2048,256]{1,0:T(8,128)(2,1)}, bf16[2048,256]{1,0:T(8,128)(2,1)}, u32[]{:S(2)}, u32[]{:S(2)}) %collective-permute-start.4) | collective-permute-done | bytes 1048608 | tf_op jit(solution)/shard_map/ppermute | solution.py:345
  29.5 1.9 shard_map.65
  31.4 2.1 collective-permute-start.6
  34.8 5.8 %collective-permute-done.7.refs_1_.refs_7_ = bf16[2048,256]{1,0:T(8,128)(2,1)S(1)} collective-permute-done((bf16[2048,256]{1,0:T(8,128)(2,1)}, bf16[2048,256]{1,0:T(8,128)(2,1)S(1)}, u32[]{:S(2)}, u32[]{:S(2)}) %collective-permute-start.7) | collective-permute-done | bytes 1048608 | tf_op jit(solution)/shard_map/ppermute | solution.py:345
  41.5 4.3 %collective-permute-start.12 = (bf16[2048,256]{1,0:T(8,128)(2,1)S(1)}, bf16[2048,256]{1,0:T(8,128)(2,1)S(1)}, u32[]{:S(2)}, u32[]{:S(2)}) collective-permute-start(bf16[2048,256]{1,0:T(8,128)(2,1)S(1)} %get-tuple-element.35.refs_4_), channel_id=1, source_target_pairs={{8,120},{16,32},{32,48},{48,64},{64,80},{80,96},{96,112},{120,104}... | collective-permute-start | bytes 3145736 | tf_op jit(solution)/shard_map/ppermute | solution.py:345
  48.1 3.8 %collective-permute-done.8.refs_2_.refs_10_.refs_1_ = bf16[2048,256]{1,0:T(8,128)(2,1)S(1)} collective-permute-done((bf16[2048,256]{1,0:T(8,128)(2,1)S(1)}, bf16[2048,256]{1,0:T(8,128)(2,1)S(1)}, u32[]{:S(2)}, u32[]{:S(2)}) %collective-permute-start.8) | collective-permute-done | bytes 1048608 | tf_op jit(solution)/shard_map/ppermute | solution.py:345
  52.7 1.9 collective-permute-start.10
  55.9 3.4 %collective-permute-done.12.refs_0_.refs_2_ = bf16[2048,256]{1,0:T(8,128)(2,1)S(1)} collective-permute-done((bf16[2048,256]{1,0:T(8,128)(2,1)S(1)}, bf16[2048,256]{1,0:T(8,128)(2,1)S(1)}, u32[]{:S(2)}, u32[]{:S(2)}) %collective-permute-start.12) | collective-permute-done | bytes 1048608 | tf_op jit(solution)/shard_map/ppermute | solution.py:345
  59.4 3.8 %collective-permute-done.13.refs_2_.refs_9_ = bf16[2048,256]{1,0:T(8,128)(2,1)S(1)} collective-permute-done((bf16[2048,256]{1,0:T(8,128)(2,1)S(1)}, bf16[2048,256]{1,0:T(8,128)(2,1)S(1)}, u32[]{:S(2)}, u32[]{:S(2)}) %collective-permute-start.13) | collective-permute-done | bytes 1048608 | tf_op jit(solution)/shard_map/ppermute | solution.py:345
  64.0 1.9 collective-permute-start.16
  67.2 3.4 %collective-permute-done.10.refs_0_.refs_3_.refs_2_ = bf16[2048,256]{1,0:T(8,128)(2,1)S(1)} collective-permute-done((bf16[2048,256]{1,0:T(8,128)(2,1)S(1)}, bf16[2048,256]{1,0:T(8,128)(2,1)S(1)}, u32[]{:S(2)}, u32[]{:S(2)}) %collective-permute-start.10) | collective-permute-done | bytes 1048608 | tf_op jit(solution)/shard_map/ppermute | solution.py:345
  70.6 3.8 %collective-permute-done.11.refs_1_ = bf16[2048,256]{1,0:T(8,128)(2,1)S(1)} collective-permute-done((bf16[2048,256]{1,0:T(8,128)(2,1)S(1)}, bf16[2048,256]{1,0:T(8,128)(2,1)S(1)}, u32[]{:S(2)}, u32[]{:S(2)}) %collective-permute-start.11) | collective-permute-done | bytes 1048608 | tf_op jit(solution)/shard_map/ppermute | solution.py:345
  74.4 5.0 %shard_map.69 = (bf16[2048,256]{1,0:T(8,128)(2,1)S(1)}, bf16[2048,256]{1,0:T(8,128)(2,1)S(1)}, bf16[11,512,256]{2,1,0:T(8,128)(2,1)}, bf16[11,512,256]{2,1,0:T(8,128)(2,1)}) custom-call(s32[224]{0:T(256)S(1)} %bitcast.12, s32[192]{0:T(256)S(1)} %reshape.277.want, bf16[2048,256]{1,0:T(8,128)(2,1)S(1)} %collective-permute-done.10.refs_0_.refs_3_.refs_2_, ...), custom_call_target="tpu_custom_call" | custom-call | bytes 188743680 | tf_op jit(solution)/shard_map/pallas_call | solution.py:220
  79.3 3.0 %collective-permute-start.22 = (bf16[11,512,256]{2,1,0:T(8,128)(2,1)}, bf16[11,512,256]{2,1,0:T(8,128)(2,1)S(1)}, u32[]{:S(2)}, u32[]{:S(2)}) collective-permute-start(bf16[11,512,256]{2,1,0:T(8,128)(2,1)} %get-tuple-element.50), channel_id=1, source_target_pairs={{0,8},{8,0},{16,24},{24,16},{32,40},{40,32},{48,56},{56,48},{64,72... | collective-permute-start | bytes 8650760 | tf_op jit(solution)/shard_map/ppermute | solution.py:349
  82.4 1.9 collective-permute-start.14
  86.4 1.9 collective-permute-start.18
  89.7 9.4 %collective-permute-done.14.refs_0_ = bf16[2048,256]{1,0:T(8,128)(2,1)S(1)} collective-permute-done((bf16[2048,256]{1,0:T(8,128)(2,1)S(1)}, bf16[2048,256]{1,0:T(8,128)(2,1)S(1)}, u32[]{:S(2)}, u32[]{:S(2)}) %collective-permute-start.14) | collective-permute-done | bytes 1048608 | tf_op jit(solution)/shard_map/ppermute | solution.py:345
  99.0 1.9 collective-permute-done.15.refs_1_
  101.0 2.5 %shard_map.71 = (bf16[2048,256]{1,0:T(8,128)(2,1)S(1)}, bf16[2048,256]{1,0:T(8,128)(2,1)S(1)}, bf16[4,512,256]{2,1,0:T(8,128)(2,1)}, bf16[4,512,256]{2,1,0:T(8,128)(2,1)}) custom-call(s32[224]{0:T(256)S(1)} %bitcast.14, s32[192]{0:T(256)S(1)} %reshape.277.want, bf16[2048,256]{1,0:T(8,128)(2,1)S(1)} %collective-permute-done.14.refs_0_, ...), custom_call_target="tpu_custom_call" | custom-call | bytes 100663296 | tf_op jit(solution)/shard_map/pallas_call | solution.py:220
  103.4 1.9 collective-permute-start.20
  106.8 3.4 %collective-permute-done.18.refs_0_ = bf16[2048,256]{1,0:T(8,128)(2,1)S(1)} collective-permute-done((bf16[2048,256]{1,0:T(8,128)(2,1)S(1)}, bf16[2048,256]{1,0:T(8,128)(2,1)S(1)}, u32[]{:S(2)}, u32[]{:S(2)}) %collective-permute-start.18) | collective-permute-done | bytes 1048608 | tf_op jit(solution)/shard_map/ppermute | solution.py:345
  112.2 1.7 shard_map.72
  114.0 7.5 %collective-permute-done.20.refs_0_ = bf16[2048,256]{1,0:T(8,128)(2,1)S(1)} collective-permute-done((bf16[2048,256]{1,0:T(8,128)(2,1)S(1)}, bf16[2048,256]{1,0:T(8,128)(2,1)S(1)}, u32[]{:S(2)}, u32[]{:S(2)}) %collective-permute-start.20) | collective-permute-done | bytes 1048608 | tf_op jit(solution)/shard_map/ppermute | solution.py:345
  121.5 1.9 collective-permute-done.21.refs_1_
  123.5 2.6 %shard_map.73 = (bf16[3,512,256]{2,1,0:T(8,128)(2,1)}, bf16[3,512,256]{2,1,0:T(8,128)(2,1)}) custom-call(s32[224]{0:T(256)S(1)} %bitcast.16, s32[192]{0:T(256)S(1)} %reshape.277.want, bf16[2048,256]{1,0:T(8,128)(2,1)S(1)} %collective-permute-done.20.refs_0_, bf16[2048,256]{1,0:T(8,128)(2,1)S(1)} %collective-permute-done.21.refs_1_, ...), custom_call_target="tpu_custom_call" | custom-call | bytes 37748736 | tf_op jit(solution)/shard_map/pallas_call | solution.py:220
  126.2 2.5 %collective-permute-done.25.refs_7_ = bf16[3,512,256]{2,1,0:T(8,128)(2,1)S(1)} collective-permute-done((bf16[3,512,256]{2,1,0:T(8,128)(2,1)}, bf16[3,512,256]{2,1,0:T(8,128)(2,1)S(1)}, u32[]{:S(2)}, u32[]{:S(2)}) %collective-permute-start.25) | collective-permute-done | bytes 786464 | tf_op jit(solution)/shard_map/ppermute | solution.py:349
  129.6 22.7 %shard_map.74 = bf16[2048,512]{1,0:T(8,128)(2,1)S(1)} custom-call(s32[12]{0:T(128)S(1)} %reshape.276.info, s32[224]{0:T(256)S(1)} %bitcast.17, bf16[2048,512]{1,0:T(8,128)(2,1)} %q_ref.1, bf16[2048,256]{1,0:T(8,128)(2,1)} %constant_dynamic-update-slice_fusion.refs_1_.refs_2_.kv_ref, bf16[11,512,256]{2,1,0:T(8,128)(2,1)} %get-tuple-element.40.refs_0_, ...), custom_call_target="tpu_custom_call" | custom-call | flops 8589934592 | bytes 8388608 | tf_op jit(solution)/shard_map/pallas_call | solution.py:464
  152.3 34.3 %all_to_all.10.a_ref = bf16[8,256,512]{2,1,0:T(8,128)(2,1)S(1)} all-to-all(bf16[8,256,512]{2,1,0:T(8,128)(2,1)S(1)} %bitcast.5), channel_id=1, replica_groups=mesh['ctx'=32,'head'=8] {'head'}, dimensions={0} | all-to-all | bytes 4194304 | tf_op jit(solution)/shard_map/all_to_all | solution.py:565
  186.6 8.9 %shard_map.75 = bf16[8,256,256]{2,1,0:T(8,128)(2,1)S(1)} custom-call(s32[1]{0:T(128)} %bitcast.core, bf16[8,256,512]{2,1,0:T(8,128)(2,1)S(1)} %all_to_all.10.a_ref, bf16[8,256,2048]{2,1,0:T(8,128)(2,1)} %bitcast.19, bf16[8,256,2048]{2,1,0:T(8,128)(2,1)} %collective-permute-done.26.other_ref), custom_call_target="tpu_custom_call" | custom-call | flops 4294967296 | bytes 20971520 | tf_op jit(solution)/shard_map/pallas_call | solution.py:517
  195.6 19.3 %all_to_all.11 = bf16[8,256,256]{2,1,0:T(8,128)(2,1)S(1)} all-to-all(bf16[8,256,256]{2,1,0:T(8,128)(2,1)S(1)} %shard_map.75), channel_id=1, replica_groups=mesh['ctx'=32,'head'=8] {'head'}, dimensions={0} | all-to-all | bytes 2097152 | tf_op jit(solution)/shard_map/all_to_all | solution.py:569
  (70 shorter events, 29.4 us)
Async XLA Ops:
  6.5 3.5 %copy-start.6 = (bf16[2048,128]{1,0:T(8,128)(2,1)S(1)}, bf16[2048,128]{1,0:T(8,128)(2,1)}, u32[]{:S(2)}) copy-start(bf16[2048,128]{1,0:T(8,128)(2,1)} %param.8) | copy-start | bytes 1572868
  6.5 7.3 %copy-start.7 = (s32[4,3]{1,0:T(4,128)S(1)}, s32[4,3]{1,0:T(4,128)}, u32[]{:S(2)}) copy-start(s32[4,3]{1,0:T(4,128)} %param.9) | copy-start | bytes 148
  6.5 122.2 %all-gather.3.cloned.1.call-start = ((), (), s32[]{:S(2)}) async-start(), calls=%async_computation.2 | async-start | bytes 9437184 | tf_op jit(solution)/shard_map/all_gather | solution.py:550
  10.9 10.7 %collective-permute-start.5 = (bf16[2048,256]{1,0:T(8,128)(2,1)}, bf16[2048,256]{1,0:T(8,128)(2,1)S(1)}, u32[]{:S(2)}, u32[]{:S(2)}) collective-permute-start(bf16[2048,256]{1,0:T(8,128)(2,1)} %constant_dynamic-update-slice_fusion.refs_1_.refs_2_.kv_ref), channel_id=1, source_target_pairs={{0,8},{8,0},{16,24},{24,16},{32,40},{40,32},{48,56},{56,48},{64,72... | collective-permute-start | bytes 3145736 | tf_op jit(solution)/shard_map/ppermute | solution.py:311
  10.9 15.0 %collective-permute-start.3 = (bf16[2048,256]{1,0:T(8,128)(2,1)}, bf16[2048,256]{1,0:T(8,128)(2,1)}, u32[]{:S(2)}, u32[]{:S(2)}) collective-permute-start(bf16[2048,256]{1,0:T(8,128)(2,1)} %constant_dynamic-update-slice_fusion.refs_1_.refs_2_.kv_ref), channel_id=1, source_target_pairs={{0,16},{8,120},{16,32},{24,8},{32,48},{40,24},{48,64},{64,80},{80,... | collective-permute-start | bytes 3145736 | tf_op jit(solution)/shard_map/ppermute | solution.py:345
  12.5 17.0 %collective-permute-start.4 = (bf16[2048,256]{1,0:T(8,128)(2,1)}, bf16[2048,256]{1,0:T(8,128)(2,1)}, u32[]{:S(2)}, u32[]{:S(2)}) collective-permute-start(bf16[2048,256]{1,0:T(8,128)(2,1)} %constant_dynamic-update-slice_fusion.refs_1_.refs_2_.kv_ref), channel_id=1, source_target_pairs={{8,136},{24,152},{56,184},{72,200},{88,216},{104,232},{112,240},{9... | collective-permute-start | bytes 3145736 | tf_op jit(solution)/shard_map/ppermute | solution.py:345
  13.8 1.3 collective-permute-start
  15.2 9.6 %collective-permute-start.2 = (s32[2,12]{1,0:T(2,128)S(1)}, s32[2,12]{1,0:T(2,128)S(1)}, u32[]{:S(2)}, u32[]{:S(2)}) collective-permute-start(s32[2,12]{1,0:T(2,128)S(1)} %add_select_fusion.2), channel_id=1, source_target_pairs={{128,0},{136,8},{144,16},{152,24},{160,32},{168,40},{176,48},{184,... | collective-permute-start | bytes 296 | tf_op jit(solution)/shard_map/ppermute | solution.py:319
  20.6 5.0 %collective-permute-start.1 = (s32[2,12]{1,0:T(2,128)S(1)}, s32[2,12]{1,0:T(2,128)S(1)}, u32[]{:S(2)}, u32[]{:S(2)}) collective-permute-start(s32[2,12]{1,0:T(2,128)S(1)} %add_select_fusion.2), channel_id=1, source_target_pairs={{16,0},{120,8},{32,16},{8,24},{48,32},{24,40},{64,48},{40,56},{80,... | collective-permute-start | bytes 296 | tf_op jit(solution)/shard_map/ppermute | solution.py:319
  23.6 17.1 %collective-permute-start.7 = (bf16[2048,256]{1,0:T(8,128)(2,1)}, bf16[2048,256]{1,0:T(8,128)(2,1)S(1)}, u32[]{:S(2)}, u32[]{:S(2)}) collective-permute-start(bf16[2048,256]{1,0:T(8,128)(2,1)} %get-tuple-element.33), channel_id=1, source_target_pairs={{8,136},{40,168},{56,184},{72,200},{88,216},{104,232},{112,240},{9... | collective-permute-start | bytes 3145736 | tf_op jit(solution)/shard_map/ppermute | solution.py:345
  24.9 15.8 %collective-permute-start.9 = (bf16[2048,256]{1,0:T(8,128)(2,1)}, bf16[2048,256]{1,0:T(8,128)(2,1)S(1)}, u32[]{:S(2)}, u32[]{:S(2)}) collective-permute-start(bf16[2048,256]{1,0:T(8,128)(2,1)} %get-tuple-element.31.refs_3_), channel_id=1, source_target_pairs={{0,16},{8,120},{16,32},{24,8},{32,48},{48,64},{64,80},{80,96},{96,... | collective-permute-start | bytes 3145736 | tf_op jit(solution)/shard_map/ppermute | solution.py:345
  31.4 16.7 %collective-permute-start.6 = (bf16[2048,256]{1,0:T(8,128)(2,1)S(1)}, bf16[2048,256]{1,0:T(8,128)(2,1)S(1)}, u32[]{:S(2)}, u32[]{:S(2)}) collective-permute-start(bf16[2048,256]{1,0:T(8,128)(2,1)S(1)} %get-tuple-element.32.refs_4_), channel_id=1, source_target_pairs={{8,120},{16,32},{24,8},{32,48},{48,64},{64,80},{80,96},{96,112},{1... | collective-permute-start | bytes 3145736 | tf_op jit(solution)/shard_map/ppermute | solution.py:345
  33.5 18.4 %collective-permute-start.8 = (bf16[2048,256]{1,0:T(8,128)(2,1)S(1)}, bf16[2048,256]{1,0:T(8,128)(2,1)S(1)}, u32[]{:S(2)}, u32[]{:S(2)}) collective-permute-start(bf16[2048,256]{1,0:T(8,128)(2,1)S(1)} %get-tuple-element.34), channel_id=1, source_target_pairs={{8,136},{24,152},{32,160},{48,176},{64,192},{80,208},{104,232},{11... | collective-permute-start | bytes 3145736 | tf_op jit(solution)/shard_map/ppermute | solution.py:345
  41.5 17.9 %collective-permute-start.12 = (bf16[2048,256]{1,0:T(8,128)(2,1)S(1)}, bf16[2048,256]{1,0:T(8,128)(2,1)S(1)}, u32[]{:S(2)}, u32[]{:S(2)}) collective-permute-start(bf16[2048,256]{1,0:T(8,128)(2,1)S(1)} %get-tuple-element.35.refs_4_), channel_id=1, source_target_pairs={{8,120},{16,32},{32,48},{48,64},{64,80},{80,96},{96,112},{120,104}... | collective-permute-start | bytes 3145736 | tf_op jit(solution)/shard_map/ppermute | solution.py:345
  45.8 17.3 %collective-permute-start.13 = (bf16[2048,256]{1,0:T(8,128)(2,1)S(1)}, bf16[2048,256]{1,0:T(8,128)(2,1)S(1)}, u32[]{:S(2)}, u32[]{:S(2)}) collective-permute-start(bf16[2048,256]{1,0:T(8,128)(2,1)S(1)} %get-tuple-element.38), channel_id=1, source_target_pairs={{8,136},{16,144},{32,160},{48,176},{64,192},{80,208},{96,224},{112... | collective-permute-start | bytes 3145736 | tf_op jit(solution)/shard_map/ppermute | solution.py:345
  52.7 17.9 %collective-permute-start.10 = (bf16[2048,256]{1,0:T(8,128)(2,1)S(1)}, bf16[2048,256]{1,0:T(8,128)(2,1)S(1)}, u32[]{:S(2)}, u32[]{:S(2)}) collective-permute-start(bf16[2048,256]{1,0:T(8,128)(2,1)S(1)} %get-tuple-element.36.refs_4_), channel_id=1, source_target_pairs={{8,120},{32,48},{48,64},{64,80},{80,96},{96,112},{104,88},{120,104... | collective-permute-start | bytes 3145736 | tf_op jit(solution)/shard_map/ppermute | solution.py:345
  54.6 19.7 %collective-permute-start.11 = (bf16[2048,256]{1,0:T(8,128)(2,1)S(1)}, bf16[2048,256]{1,0:T(8,128)(2,1)S(1)}, u32[]{:S(2)}, u32[]{:S(2)}) collective-permute-start(bf16[2048,256]{1,0:T(8,128)(2,1)S(1)} %get-tuple-element.37), channel_id=1, source_target_pairs={{8,136},{32,160},{48,176},{64,192},{104,232},{112,240},{9,137},{33... | collective-permute-start | bytes 3145736 | tf_op jit(solution)/shard_map/ppermute | solution.py:345
  64.0 21.6 %collective-permute-start.16 = (bf16[2048,256]{1,0:T(8,128)(2,1)S(1)}, bf16[2048,256]{1,0:T(8,128)(2,1)S(1)}, u32[]{:S(2)}, u32[]{:S(2)}) collective-permute-start(bf16[2048,256]{1,0:T(8,128)(2,1)S(1)} %get-tuple-element.39.refs_11_), channel_id=1, source_target_pairs={{32,48},{48,64},{64,80},{80,96},{96,112},{104,88},{120,104},{128,1... | collective-permute-start | bytes 3145736 | tf_op jit(solution)/shard_map/ppermute | solution.py:345
  65.9 19.7 %collective-permute-start.17 = (bf16[2048,256]{1,0:T(8,128)(2,1)S(1)}, bf16[2048,256]{1,0:T(8,128)(2,1)S(1)}, u32[]{:S(2)}, u32[]{:S(2)}) collective-permute-start(bf16[2048,256]{1,0:T(8,128)(2,1)S(1)} %get-tuple-element.43), channel_id=1, source_target_pairs={{32,160},{48,176},{64,192},{80,208},{96,224},{112,240},{33,161},{4... | collective-permute-start | bytes 3145736 | tf_op jit(solution)/shard_map/ppermute | solution.py:345
  79.3 44.1 %collective-permute-start.22 = (bf16[11,512,256]{2,1,0:T(8,128)(2,1)}, bf16[11,512,256]{2,1,0:T(8,128)(2,1)S(1)}, u32[]{:S(2)}, u32[]{:S(2)}) collective-permute-start(bf16[11,512,256]{2,1,0:T(8,128)(2,1)} %get-tuple-element.50), channel_id=1, source_target_pairs={{0,8},{8,0},{16,24},{24,16},{32,40},{40,32},{48,56},{56,48},{64,72... | collective-permute-start | bytes 8650760 | tf_op jit(solution)/shard_map/ppermute | solution.py:349
  82.4 16.7 %collective-permute-start.14 = (bf16[2048,256]{1,0:T(8,128)(2,1)S(1)}, bf16[2048,256]{1,0:T(8,128)(2,1)S(1)}, u32[]{:S(2)}, u32[]{:S(2)}) collective-permute-start(bf16[2048,256]{1,0:T(8,128)(2,1)S(1)} %get-tuple-element.41.refs_5_), channel_id=1, source_target_pairs={{48,64},{64,80},{80,96},{88,72},{96,112},{104,88},{120,104},{128,1... | collective-permute-start | bytes 3145736 | tf_op jit(solution)/shard_map/ppermute | solution.py:345
  84.3 16.7 %collective-permute-start.15 = (bf16[2048,256]{1,0:T(8,128)(2,1)S(1)}, bf16[2048,256]{1,0:T(8,128)(2,1)S(1)}, u32[]{:S(2)}, u32[]{:S(2)}) collective-permute-start(bf16[2048,256]{1,0:T(8,128)(2,1)S(1)} %get-tuple-element.42), channel_id=1, source_target_pairs={{48,176},{64,192},{88,216},{104,232},{112,240},{49,177},{65,193},{... | collective-permute-start | bytes 3145736 | tf_op jit(solution)/shard_map/ppermute | solution.py:345
  86.4 23.8 %collective-permute-start.18 = (bf16[2048,256]{1,0:T(8,128)(2,1)S(1)}, bf16[2048,256]{1,0:T(8,128)(2,1)S(1)}, u32[]{:S(2)}, u32[]{:S(2)}) collective-permute-start(bf16[2048,256]{1,0:T(8,128)(2,1)S(1)} %get-tuple-element.44.refs_5_), channel_id=1, source_target_pairs={{96,112},{128,144},{136,248},{144,160},{152,136},{160,176},{168,15... | collective-permute-start | bytes 3145736 | tf_op jit(solution)/shard_map/ppermute | solution.py:345
  88.4 23.8 %collective-permute-start.19 = (bf16[2048,256]{1,0:T(8,128)(2,1)S(1)}, bf16[2048,256]{1,0:T(8,128)(2,1)S(1)}, u32[]{:S(2)}, u32[]{:S(2)}) collective-permute-start(bf16[2048,256]{1,0:T(8,128)(2,1)S(1)} %get-tuple-element.46), channel_id=1, source_target_pairs={{88,216},{104,232},{112,240},{89,217},{105,233},{113,241},{90,218}... | collective-permute-start | bytes 3145736 | tf_op jit(solution)/shard_map/ppermute | solution.py:345
  103.4 18.1 %collective-permute-start.20 = (bf16[2048,256]{1,0:T(8,128)(2,1)S(1)}, bf16[2048,256]{1,0:T(8,128)(2,1)S(1)}, u32[]{:S(2)}, u32[]{:S(2)}) collective-permute-start(bf16[2048,256]{1,0:T(8,128)(2,1)S(1)} %get-tuple-element.47.refs_2_), channel_id=1, source_target_pairs={{96,112},{128,144},{136,248},{144,160},{152,136},{160,176},{168,15... | collective-permute-start | bytes 3145736 | tf_op jit(solution)/shard_map/ppermute | solution.py:345
  105.4 18.1 %collective-permute-start.21 = (bf16[2048,256]{1,0:T(8,128)(2,1)S(1)}, bf16[2048,256]{1,0:T(8,128)(2,1)S(1)}, u32[]{:S(2)}, u32[]{:S(2)}) collective-permute-start(bf16[2048,256]{1,0:T(8,128)(2,1)S(1)} %get-tuple-element.49), channel_id=1, source_target_pairs={{64,192},{88,216},{96,224},{112,240},{65,193},{89,217},{97,225},{1... | collective-permute-start | bytes 3145736 | tf_op jit(solution)/shard_map/ppermute | solution.py:345
  110.3 13.2 %collective-permute-start.23 = (bf16[4,512,256]{2,1,0:T(8,128)(2,1)}, bf16[4,512,256]{2,1,0:T(8,128)(2,1)S(1)}, u32[]{:S(2)}, u32[]{:S(2)}) collective-permute-start(bf16[4,512,256]{2,1,0:T(8,128)(2,1)} %get-tuple-element.51), channel_id=1, source_target_pairs={{0,8},{8,0},{16,24},{24,16},{32,40},{40,32},{48,56},{56,48},{64,72... | collective-permute-start | bytes 3145736 | tf_op jit(solution)/shard_map/ppermute | solution.py:349
  113.9 9.5 %collective-permute-start.24 = (bf16[2,512,256]{2,1,0:T(8,128)(2,1)}, bf16[2,512,256]{2,1,0:T(8,128)(2,1)S(1)}, u32[]{:S(2)}, u32[]{:S(2)}) collective-permute-start(bf16[2,512,256]{2,1,0:T(8,128)(2,1)} %get-tuple-element.52), channel_id=1, source_target_pairs={{0,8},{8,0},{16,24},{24,16},{32,40},{40,32},{48,56},{56,48},{64,72... | collective-permute-start | bytes 1572872 | tf_op jit(solution)/shard_map/ppermute | solution.py:349
  123.5 2.7 %copy-start.2 = (bf16[11,512,256]{2,1,0:T(8,128)(2,1)}, bf16[11,512,256]{2,1,0:T(8,128)(2,1)S(1)}, u32[]{:S(2)}) copy-start(bf16[11,512,256]{2,1,0:T(8,128)(2,1)S(1)} %collective-permute-done.22.refs_2_.refs_4_) | copy-start | bytes 8650756
  126.2 2.5 %collective-permute-start.25 = (bf16[3,512,256]{2,1,0:T(8,128)(2,1)}, bf16[3,512,256]{2,1,0:T(8,128)(2,1)S(1)}, u32[]{:S(2)}, u32[]{:S(2)}) collective-permute-start(bf16[3,512,256]{2,1,0:T(8,128)(2,1)} %get-tuple-element.54), channel_id=1, source_target_pairs={{0,8},{8,0},{16,24},{24,16},{32,40},{40,32},{48,56},{56,48},{64,72... | collective-permute-start | bytes 2359304 | tf_op jit(solution)/shard_map/ppermute | solution.py:349
  128.7 57.9 %collective-permute-start.26 = (bf16[8,256,2048]{2,1,0:T(8,128)(2,1)}, bf16[8,256,2048]{2,1,0:T(8,128)(2,1)}, u32[]{:S(2)}, u32[]{:S(2)}) collective-permute-start(bf16[8,256,2048]{2,1,0:T(8,128)(2,1)} %bitcast.18), channel_id=1, source_target_pairs={{0,8},{8,0},{16,24},{24,16},{32,40},{40,32},{48,56},{56,48},{64,72... | collective-permute-start | bytes 25165832 | tf_op jit(solution)/shard_map/ppermute | solution.py:563
  186.6 29.2 %copy-start.1 = (bf16[512,2048]{1,0:T(8,128)(2,1)S(1)}, bf16[512,2048]{1,0:T(8,128)(2,1)}, u32[]{:S(2)}) copy-start(bf16[512,2048]{1,0:T(8,128)(2,1)} %param.10) | copy-start | bytes 6291460
  (5 other events, 10.4 us)
Sparse Core Ops, SparseCore 0:
  9.3 94.8 all-gather.2

commit v6 on v5

--- a/solution.py
+++ b/solution.py
@@ -110,7 +110,7 @@
         ),
     ),
 )
-CHECKPOINTS = (4, 6, 7, 8)
+CHECKPOINTS = (3, 5, 7, 8)
 COST = 12
 
 
@@ -214,14 +214,16 @@
 def move(ways, slots, scalars, arrays, width, after=()):
     out_shapes = [(ROWS, width)] * len(ways[0]) + [(len(slots[0]), BLOCK_TOKENS, width)] * (2 if slots[0] else 0)
 
+    kept = len(ways[0])
+
     def whole(shape):
         return pl.BlockSpec(shape, lambda *_: (0,) * len(shape))
 
     return pl.pallas_call(
         functools.partial(move_kernel, *ways, *slots),
         out_shape=[
-            pltpu.HBM(s, arrays[0].dtype) if len(s) == 3 else jax.ShapeDtypeStruct(s, arrays[0].dtype)
-            for s in out_shapes
+            pltpu.HBM(s, arrays[0].dtype) if i == kept else jax.ShapeDtypeStruct(s, arrays[0].dtype)
+            for i, s in enumerate(out_shapes)
         ],
         grid_spec=pltpu.PrefetchScalarGridSpec(
             num_scalar_prefetch=len(scalars),
@@ -513,7 +515,7 @@
     parts, rows, features = attended.shape
     depth = mine.shape[1]
     columns = mine.shape[2] // parts
-    together = 2
+    together = 4
     return pl.pallas_call(
         functools.partial(project_kernel, depth),
         out_shape=jax.ShapeDtypeStruct((parts, rows, columns), jnp.bfloat16),
@@ -539,9 +541,43 @@
     )(core, attended, in_hbm(mine), in_hbm(other))
 
 
+def join_kernel(key_ref, value_ref, o_ref):
+    o_ref[:, :HEAD_SIZE] = key_ref[...]
+    o_ref[:, HEAD_SIZE:] = value_ref[...]
+
+
+def join(keys, values):
+    rows = keys.shape[0]
+    part = pl.BlockSpec((BLOCK_TOKENS, HEAD_SIZE), lambda i: (i, 0))
+    return pl.pallas_call(
+        join_kernel,
+        out_shape=jax.ShapeDtypeStruct((rows, 2 * HEAD_SIZE), keys.dtype),
+        grid=(rows // BLOCK_TOKENS,),
+        in_specs=[part, part],
+        out_specs=pl.BlockSpec((BLOCK_TOKENS, 2 * HEAD_SIZE), lambda i: (i, 0)),
+    )(keys, values)
+
+
+def half_kernel(core, w_ref, o_ref):
+    o_ref[...] = w_ref[...]
+
+
+def half_of(weight, core):
+    rows, columns = weight.shape
+    return pl.pallas_call(
+        half_kernel,
+        out_shape=jax.ShapeDtypeStruct((rows // 2, columns), weight.dtype),
+        grid_spec=pltpu.PrefetchScalarGridSpec(
+            num_scalar_prefetch=1,
+            grid=(1,),
+            in_specs=[pl.BlockSpec((rows // 2, columns), lambda i, core: (core[0], 0))],
+            out_specs=pl.BlockSpec((rows // 2, columns), lambda i, core: (0, 0)),
+        ),
+    )(core, in_hbm(weight))
+
+
 def gather_weight(out_weight, core):
-    half = out_weight.shape[0] // 2
-    mine = lax.dynamic_slice_in_dim(out_weight, core * half, half, 0)
+    mine = half_of(out_weight, core[None])
     groups = [
         [((side ^ x_hi) * (CORES // 2) + rest) * 8 + x_hi * 4 + y for x_hi in range(2) for y in range(4)]
         for side in range(2)
@@ -555,7 +591,7 @@
     index = lax.axis_index("ctx")
     core = index % 2
     rows, width = queries.shape
-    kv = jnp.concatenate([key_state_matrix, value_state_matrix], axis=1)
+    kv = join(key_state_matrix, value_state_matrix)
     other_selected = lax.ppermute(selected, "ctx", SWAP)
     mine = gather_weight(out_weight, core)
     chosen, row, place = exchange(kv, selected, other_selected, index)

time: 225 us -> 232 us (1.031)
  waiting for transfers between devices: 56.9 us -> 62.6 us
  Pallas kernels: 50.5 us -> 55.8 us
  starting transfers between devices: 40.7 us -> 37.9 us
    pallas_call x0 -> x2, Pallas kernels: none -> 5.74 us  [the longest x1 3.47 us: join(): pl.pallas_call(join_kernel, out_shape=jax.ShapeDtypeStruct((rows, 2 * HEA...]
    ppermute x2, waiting for transfers between devices: 0.01 us -> 4.73 us  [exchange(): lax.ppermute(chip, 'ctx', [(target(way, i), i) for i in range(CORES >> wa...]
    ppermute x4, starting transfers between devices: 3.53 us -> 0.65 us  [exchange(): passed.append(lax.ppermute(give, 'ctx', SWAP))]
    unnamed x20 -> x21, local copies, waits for them, and re-layouts: 4.13 us -> 5.36 us
  transfers between devices with their start and end apart: 28 -> 28, of which waited for: 15 -> 16; matrix products, arithmetic and copies ran while one was open for 1% -> 1% of each run, Pallas kernels for 19% -> 20%
where the time goes in v6:
time: 232 us; the launch traced here: 231 us
  waiting for transfers between devices  62.6 us (27%)
  Pallas kernels  55.8 us (24%)
  blocking collectives  53.8 us (23%)
  starting transfers between devices  37.9 us (16%)
  between operations  13.8 us (6%)
  local copies, waits for them, and re-layouts  6.4 us (3%)
    ppermute x18, waiting for transfers between devices, exchange(): arrived[step, way] = lax.ppermute(buffers[way], 'ctx', pairs(step, way))  54.8 us
    all_to_all x1, blocking collectives, per_device(): lax.all_to_all(attended.reshape(head_count, rows // head_count, width), '...  34.5 us
    ppermute x18, starting transfers between devices, exchange(): arrived[step, way] = lax.ppermute(buffers[way], 'ctx', pairs(step, way))  28.5 us
    pallas_call x1, Pallas kernels, attention(): pl.pallas_call(functools.partial(attention_kernel, width // HEAD_SIZE, le...  24.9 us
    all_to_all x1, blocking collectives, per_device(): return lax.all_to_all(mixed, 'head', 0, 0, tiled=True).reshape(rows, -1)  19.3 us
    pallas_call x10, Pallas kernels, move(): pl.pallas_call(functools.partial(move_kernel, *ways, *slots), out_shape=[...  16.7 us
    pallas_call x1, Pallas kernels, project(): pl.pallas_call(functools.partial(project_kernel, depth), out_shape=jax.Sh...  8.42 us
    ppermute x2, starting transfers between devices, exchange(): lax.ppermute(chip, 'ctx', [(target(way, i), i) for i in range(CORES >> wa...  8.04 us
  transfers between devices with their start and end apart: 28, of which 16 were waited for; matrix products, arithmetic and copies ran while one was open for 1% of the time, Pallas kernels for 20%

profile of v6, /device:TPU:226, one launch (start us, length us, event | category | flops | bytes accessed | tf_op | source)
XLA Modules:
  0.0 230.5 jit_solution(10117813609523478759)
XLA Ops:
  6.5 2.3 shard_map.75
  8.8 3.5 %shard_map.64.refs_1_.refs_2_.kv_ref = bf16[2048,256]{1,0:T(8,128)(2,1)} custom-call(bf16[2048,128]{1,0:T(8,128)(2,1)} %key_ref.1, bf16[2048,128]{1,0:T(8,128)(2,1)} %value_ref.1), custom_call_target="tpu_custom_call" | custom-call | tf_op jit(solution)/shard_map/pallas_call | solution.py:552
  17.2 2.0 shard_map.65
  23.9 6.6 %collective-permute-start.2 = (s32[2,12]{1,0:T(2,128)S(1)}, s32[2,12]{1,0:T(2,128)S(1)}, u32[]{:S(2)}, u32[]{:S(2)}) collective-permute-start(s32[2,12]{1,0:T(2,128)S(1)} %add_select_fusion.2), channel_id=1, source_target_pairs={{128,0},{136,8},{144,16},{152,24},{160,32},{168,40},{176,48},{184,... | collective-permute-start | bytes 296 | tf_op jit(solution)/shard_map/ppermute | solution.py:321
  33.2 3.4 %collective-permute-done.1 = s32[2,12]{1,0:T(2,128)S(1)} collective-permute-done((s32[2,12]{1,0:T(2,128)S(1)}, s32[2,12]{1,0:T(2,128)S(1)}, u32[]{:S(2)}, u32[]{:S(2)}) %collective-permute-start.1) | collective-permute-done | bytes 128 | tf_op jit(solution)/shard_map/ppermute | solution.py:321
  40.1 2.8 %collective-permute-start.10 = (bf16[2048,256]{1,0:T(8,128)(2,1)S(1)}, bf16[2048,256]{1,0:T(8,128)(2,1)S(1)}, u32[]{:S(2)}, u32[]{:S(2)}) collective-permute-start(bf16[2048,256]{1,0:T(8,128)(2,1)S(1)} %get-tuple-element.33.refs_4_), channel_id=1, source_target_pairs={{8,120},{16,32},{24,8},{32,48},{48,64},{64,80},{80,96},{96,112},{1... | collective-permute-start | bytes 3145736 | tf_op jit(solution)/shard_map/ppermute | solution.py:347
  45.0 1.9 collective-permute-start.8
  48.4 8.4 %collective-permute-done.10.refs_0_.refs_3_.refs_4_ = bf16[2048,256]{1,0:T(8,128)(2,1)S(1)} collective-permute-done((bf16[2048,256]{1,0:T(8,128)(2,1)S(1)}, bf16[2048,256]{1,0:T(8,128)(2,1)S(1)}, u32[]{:S(2)}, u32[]{:S(2)}) %collective-permute-start.10) | collective-permute-done | bytes 1048608 | tf_op jit(solution)/shard_map/ppermute | solution.py:347
  56.8 2.8 %collective-permute-done.11.refs_2_.refs_8_.refs_1_ = bf16[2048,256]{1,0:T(8,128)(2,1)S(1)} collective-permute-done((bf16[2048,256]{1,0:T(8,128)(2,1)S(1)}, bf16[2048,256]{1,0:T(8,128)(2,1)S(1)}, u32[]{:S(2)}, u32[]{:S(2)}) %collective-permute-start.11) | collective-permute-done | bytes 1048608 | tf_op jit(solution)/shard_map/ppermute | solution.py:347
  60.3 1.9 collective-permute-start.14
  63.6 4.4 %collective-permute-done.8.refs_0_.refs_2_ = bf16[2048,256]{1,0:T(8,128)(2,1)S(1)} collective-permute-done((bf16[2048,256]{1,0:T(8,128)(2,1)S(1)}, bf16[2048,256]{1,0:T(8,128)(2,1)S(1)}, u32[]{:S(2)}, u32[]{:S(2)}) %collective-permute-start.8) | collective-permute-done | bytes 1048608 | tf_op jit(solution)/shard_map/ppermute | solution.py:347
  68.0 2.8 %collective-permute-done.9.refs_2_ = bf16[2048,256]{1,0:T(8,128)(2,1)S(1)} collective-permute-done((bf16[2048,256]{1,0:T(8,128)(2,1)S(1)}, bf16[2048,256]{1,0:T(8,128)(2,1)S(1)}, u32[]{:S(2)}, u32[]{:S(2)}) %collective-permute-start.9) | collective-permute-done | bytes 1048608 | tf_op jit(solution)/shard_map/ppermute | solution.py:347
  70.8 3.2 %shard_map.69 = (bf16[2048,256]{1,0:T(8,128)(2,1)S(1)}, bf16[2048,256]{1,0:T(8,128)(2,1)S(1)}, bf16[9,512,256]{2,1,0:T(8,128)(2,1)}, bf16[9,512,256]{2,1,0:T(8,128)(2,1)S(1)}) custom-call(s32[224]{0:T(256)S(1)} %bitcast.11, s32[192]{0:T(256)S(1)} %reshape.277.want, bf16[2048,256]{1,0:T(8,128)(2,1)S(1)} %collective-permute-done.8.refs_0_.refs_2_, ...), custom_call_target="tpu_custom_call" | custom-call | bytes 163577856 | tf_op jit(solution)/shard_map/pallas_call | solution.py:222
  74.0 1.9 collective-permute-start.12
  79.2 2.8 %collective-permute-done.15.refs_1_.refs_5_ = bf16[2048,256]{1,0:T(8,128)(2,1)S(1)} collective-permute-done((bf16[2048,256]{1,0:T(8,128)(2,1)S(1)}, bf16[2048,256]{1,0:T(8,128)(2,1)S(1)}, u32[]{:S(2)}, u32[]{:S(2)}) %collective-permute-start.15) | collective-permute-done | bytes 1048608 | tf_op jit(solution)/shard_map/ppermute | solution.py:347
  82.8 1.9 collective-permute-start.16
  86.0 4.7 %collective-permute-done.12.refs_0_.refs_3_ = bf16[2048,256]{1,0:T(8,128)(2,1)S(1)} collective-permute-done((bf16[2048,256]{1,0:T(8,128)(2,1)S(1)}, bf16[2048,256]{1,0:T(8,128)(2,1)S(1)}, u32[]{:S(2)}, u32[]{:S(2)}) %collective-permute-start.12) | collective-permute-done | bytes 1048608 | tf_op jit(solution)/shard_map/ppermute | solution.py:347
  90.7 2.5 %collective-permute-done.13.refs_2_ = bf16[2048,256]{1,0:T(8,128)(2,1)S(1)} collective-permute-done((bf16[2048,256]{1,0:T(8,128)(2,1)S(1)}, bf16[2048,256]{1,0:T(8,128)(2,1)S(1)}, u32[]{:S(2)}, u32[]{:S(2)}) %collective-permute-start.13) | collective-permute-done | bytes 1048608 | tf_op jit(solution)/shard_map/ppermute | solution.py:347
  93.2 2.2 shard_map.71
  95.4 1.9 collective-permute-start.17
  98.7 3.3 %collective-permute-done.16.refs_0_ = bf16[2048,256]{1,0:T(8,128)(2,1)S(1)} collective-permute-done((bf16[2048,256]{1,0:T(8,128)(2,1)S(1)}, bf16[2048,256]{1,0:T(8,128)(2,1)S(1)}, u32[]{:S(2)}, u32[]{:S(2)}) %collective-permute-start.16) | collective-permute-done | bytes 1048608 | tf_op jit(solution)/shard_map/ppermute | solution.py:347
  101.9 2.5 %collective-permute-done.18.refs_1_.refs_2_ = bf16[2048,256]{1,0:T(8,128)(2,1)S(1)} collective-permute-done((bf16[2048,256]{1,0:T(8,128)(2,1)S(1)}, bf16[2048,256]{1,0:T(8,128)(2,1)S(1)}, u32[]{:S(2)}, u32[]{:S(2)}) %collective-permute-start.18) | collective-permute-done | bytes 1048608 | tf_op jit(solution)/shard_map/ppermute | solution.py:347
  105.2 1.9 collective-permute-start.20
  108.5 10.1 %collective-permute-done.17.refs_1_ = bf16[2048,256]{1,0:T(8,128)(2,1)S(1)} collective-permute-done((bf16[2048,256]{1,0:T(8,128)(2,1)S(1)}, bf16[2048,256]{1,0:T(8,128)(2,1)S(1)}, u32[]{:S(2)}, u32[]{:S(2)}) %collective-permute-start.17) | collective-permute-done | bytes 1048608 | tf_op jit(solution)/shard_map/ppermute | solution.py:347
  118.6 2.1 shard_map.73
  121.2 8.6 %collective-permute-done.20.refs_0_ = bf16[2048,256]{1,0:T(8,128)(2,1)S(1)} collective-permute-done((bf16[2048,256]{1,0:T(8,128)(2,1)S(1)}, bf16[2048,256]{1,0:T(8,128)(2,1)S(1)}, u32[]{:S(2)}, u32[]{:S(2)}) %collective-permute-start.20) | collective-permute-done | bytes 1048608 | tf_op jit(solution)/shard_map/ppermute | solution.py:347
  129.9 2.2 shard_map.74
  132.4 2.3 collective-permute-done.25.refs_7_
  135.5 24.9 %shard_map.76 = bf16[2048,512]{1,0:T(8,128)(2,1)S(1)} custom-call(s32[12]{0:T(128)S(1)} %reshape.276.info, s32[224]{0:T(256)S(1)} %bitcast.17, bf16[2048,512]{1,0:T(8,128)(2,1)} %q_ref.1, bf16[2048,256]{1,0:T(8,128)(2,1)} %shard_map.64.refs_1_.refs_2_.kv_ref, bf16[9,512,256]{2,1,0:T(8,128)(2,1)} %get-tuple-element.38.refs_0_, ...), custom_call_target="tpu_custom_call" | custom-call | flops 8589934592 | bytes 8388608 | tf_op jit(solution)/shard_map/pallas_call | solution.py:466
  160.4 34.5 %all_to_all.10.a_ref = bf16[8,256,512]{2,1,0:T(8,128)(2,1)S(1)} all-to-all(bf16[8,256,512]{2,1,0:T(8,128)(2,1)S(1)} %bitcast.5), channel_id=1, replica_groups=mesh['ctx'=32,'head'=8] {'head'}, dimensions={0} | all-to-all | bytes 4194304 | tf_op jit(solution)/shard_map/all_to_all | solution.py:601
  195.0 8.4 %shard_map.77 = bf16[8,256,256]{2,1,0:T(8,128)(2,1)S(1)} custom-call(s32[1]{0:T(128)} %bitcast.core, bf16[8,256,512]{2,1,0:T(8,128)(2,1)S(1)} %all_to_all.10.a_ref, bf16[8,256,2048]{2,1,0:T(8,128)(2,1)} %bitcast.19, bf16[8,256,2048]{2,1,0:T(8,128)(2,1)} %collective-permute-done.26.other_ref), custom_call_target="tpu_custom_call" | custom-call | flops 4294967296 | bytes 20971520 | tf_op jit(solution)/shard_map/pallas_call | solution.py:519
  203.4 19.3 %all_to_all.11 = bf16[8,256,256]{2,1,0:T(8,128)(2,1)S(1)} all-to-all(bf16[8,256,256]{2,1,0:T(8,128)(2,1)S(1)} %shard_map.77), channel_id=1, replica_groups=mesh['ctx'=32,'head'=8] {'head'}, dimensions={0} | all-to-all | bytes 2097152 | tf_op jit(solution)/shard_map/all_to_all | solution.py:605
  (71 shorter events, 32.7 us)
Async XLA Ops:
  6.5 128.1 %all-gather.3.cloned.1.call-start = ((), (), s32[]{:S(2)}) async-start(), calls=%async_computation.2 | async-start | bytes 9437184 | tf_op jit(solution)/shard_map/all_gather | solution.py:586
  8.8 13.5 %copy-start.8 = (s32[4,3]{1,0:T(4,128)S(1)}, s32[4,3]{1,0:T(4,128)}, u32[]{:S(2)}) copy-start(s32[4,3]{1,0:T(4,128)} %param.9) | copy-start | bytes 148
  12.3 3.6 %collective-permute-start.3 = (bf16[2048,256]{1,0:T(8,128)(2,1)}, bf16[2048,256]{1,0:T(8,128)(2,1)S(1)}, u32[]{:S(2)}, u32[]{:S(2)}) collective-permute-start(bf16[2048,256]{1,0:T(8,128)(2,1)} %shard_map.64.refs_1_.refs_2_.kv_ref), channel_id=1, source_target_pairs={{0,8},{8,0},{16,24},{24,16},{32,40},{40,32},{48,56},{56,48},{64,72... | collective-permute-start | bytes 3145736 | tf_op jit(solution)/shard_map/ppermute | solution.py:313
  12.3 24.6 %collective-permute-start.6 = (bf16[2048,256]{1,0:T(8,128)(2,1)}, bf16[2048,256]{1,0:T(8,128)(2,1)}, u32[]{:S(2)}, u32[]{:S(2)}) collective-permute-start(bf16[2048,256]{1,0:T(8,128)(2,1)} %shard_map.64.refs_1_.refs_2_.kv_ref), channel_id=1, source_target_pairs={{0,16},{8,120},{16,32},{24,8},{32,48},{40,24},{48,64},{64,80},{80,... | collective-permute-start | bytes 3145736 | tf_op jit(solution)/shard_map/ppermute | solution.py:347
  13.9 23.0 %collective-permute-start.7 = (bf16[2048,256]{1,0:T(8,128)(2,1)}, bf16[2048,256]{1,0:T(8,128)(2,1)}, u32[]{:S(2)}, u32[]{:S(2)}) collective-permute-start(bf16[2048,256]{1,0:T(8,128)(2,1)} %shard_map.64.refs_1_.refs_2_.kv_ref), channel_id=1, source_target_pairs={{8,136},{24,152},{56,184},{72,200},{88,216},{104,232},{112,240},{9... | collective-permute-start | bytes 3145736 | tf_op jit(solution)/shard_map/ppermute | solution.py:347
  20.2 23.9 %copy-start.1 = (bf16[2048,256]{1,0:T(8,128)(2,1)S(1)}, bf16[2048,256]{1,0:T(8,128)(2,1)}, u32[]{:S(2)}) copy-start(bf16[2048,256]{1,0:T(8,128)(2,1)} %shard_map.64.refs_1_.refs_2_.kv_ref) | copy-start | bytes 3145732
  20.2 23.9 %collective-permute-start.4 = (bf16[2048,256]{1,0:T(8,128)(2,1)}, bf16[2048,256]{1,0:T(8,128)(2,1)S(1)}, u32[]{:S(2)}, u32[]{:S(2)}) collective-permute-start(bf16[2048,256]{1,0:T(8,128)(2,1)} %get-tuple-element.31.refs_3_), channel_id=1, source_target_pairs={{0,16},{8,120},{16,32},{24,8},{32,48},{48,64},{64,80},{80,96},{96,... | collective-permute-start | bytes 3145736 | tf_op jit(solution)/shard_map/ppermute | solution.py:347
  21.1 23.1 %collective-permute-start.5 = (bf16[2048,256]{1,0:T(8,128)(2,1)}, bf16[2048,256]{1,0:T(8,128)(2,1)S(1)}, u32[]{:S(2)}, u32[]{:S(2)}) collective-permute-start(bf16[2048,256]{1,0:T(8,128)(2,1)} %get-tuple-element.32), channel_id=1, source_target_pairs={{8,136},{40,168},{56,184},{72,200},{88,216},{104,232},{112,240},{9... | collective-permute-start | bytes 3145736 | tf_op jit(solution)/shard_map/ppermute | solution.py:347
  22.4 1.4 collective-permute-start
  23.9 7.9 %collective-permute-start.2 = (s32[2,12]{1,0:T(2,128)S(1)}, s32[2,12]{1,0:T(2,128)S(1)}, u32[]{:S(2)}, u32[]{:S(2)}) collective-permute-start(s32[2,12]{1,0:T(2,128)S(1)} %add_select_fusion.2), channel_id=1, source_target_pairs={{128,0},{136,8},{144,16},{152,24},{160,32},{168,40},{176,48},{184,... | collective-permute-start | bytes 296 | tf_op jit(solution)/shard_map/ppermute | solution.py:321
  31.8 4.9 %collective-permute-start.1 = (s32[2,12]{1,0:T(2,128)S(1)}, s32[2,12]{1,0:T(2,128)S(1)}, u32[]{:S(2)}, u32[]{:S(2)}) collective-permute-start(s32[2,12]{1,0:T(2,128)S(1)} %add_select_fusion.2), channel_id=1, source_target_pairs={{16,0},{120,8},{32,16},{8,24},{48,32},{24,40},{64,48},{40,56},{80,... | collective-permute-start | bytes 296 | tf_op jit(solution)/shard_map/ppermute | solution.py:321
  40.1 16.7 %collective-permute-start.10 = (bf16[2048,256]{1,0:T(8,128)(2,1)S(1)}, bf16[2048,256]{1,0:T(8,128)(2,1)S(1)}, u32[]{:S(2)}, u32[]{:S(2)}) collective-permute-start(bf16[2048,256]{1,0:T(8,128)(2,1)S(1)} %get-tuple-element.33.refs_4_), channel_id=1, source_target_pairs={{8,120},{16,32},{24,8},{32,48},{48,64},{64,80},{80,96},{96,112},{1... | collective-permute-start | bytes 3145736 | tf_op jit(solution)/shard_map/ppermute | solution.py:347
  42.8 16.7 %collective-permute-start.11 = (bf16[2048,256]{1,0:T(8,128)(2,1)S(1)}, bf16[2048,256]{1,0:T(8,128)(2,1)S(1)}, u32[]{:S(2)}, u32[]{:S(2)}) collective-permute-start(bf16[2048,256]{1,0:T(8,128)(2,1)S(1)} %get-tuple-element.36), channel_id=1, source_target_pairs={{8,136},{24,152},{32,160},{48,176},{64,192},{80,208},{104,232},{11... | collective-permute-start | bytes 3145736 | tf_op jit(solution)/shard_map/ppermute | solution.py:347
  45.0 23.0 %collective-permute-start.8 = (bf16[2048,256]{1,0:T(8,128)(2,1)S(1)}, bf16[2048,256]{1,0:T(8,128)(2,1)S(1)}, u32[]{:S(2)}, u32[]{:S(2)}) collective-permute-start(bf16[2048,256]{1,0:T(8,128)(2,1)S(1)} %get-tuple-element.34.refs_4_), channel_id=1, source_target_pairs={{8,120},{16,32},{32,48},{48,64},{64,80},{80,96},{96,112},{120,104}... | collective-permute-start | bytes 3145736 | tf_op jit(solution)/shard_map/ppermute | solution.py:347
  46.9 23.8 %copy-start.4 = (bf16[2048,256]{1,0:T(8,128)(2,1)S(1)}, bf16[2048,256]{1,0:T(8,128)(2,1)}, u32[]{:S(2)}) copy-start(bf16[2048,256]{1,0:T(8,128)(2,1)} %copy-done.2) | copy-start | bytes 3145732
  46.9 23.8 %collective-permute-start.9 = (bf16[2048,256]{1,0:T(8,128)(2,1)S(1)}, bf16[2048,256]{1,0:T(8,128)(2,1)S(1)}, u32[]{:S(2)}, u32[]{:S(2)}) collective-permute-start(bf16[2048,256]{1,0:T(8,128)(2,1)S(1)} %get-tuple-element.35), channel_id=1, source_target_pairs={{8,136},{16,144},{32,160},{48,176},{64,192},{80,208},{96,224},{112... | collective-permute-start | bytes 3145736 | tf_op jit(solution)/shard_map/ppermute | solution.py:347
  60.3 18.9 %collective-permute-start.14 = (bf16[2048,256]{1,0:T(8,128)(2,1)S(1)}, bf16[2048,256]{1,0:T(8,128)(2,1)S(1)}, u32[]{:S(2)}, u32[]{:S(2)}) collective-permute-start(bf16[2048,256]{1,0:T(8,128)(2,1)S(1)} %get-tuple-element.37.refs_9_), channel_id=1, source_target_pairs={{8,120},{32,48},{48,64},{64,80},{80,96},{96,112},{104,88},{120,104... | collective-permute-start | bytes 3145736 | tf_op jit(solution)/shard_map/ppermute | solution.py:347
  62.3 19.7 %collective-permute-start.15 = (bf16[2048,256]{1,0:T(8,128)(2,1)S(1)}, bf16[2048,256]{1,0:T(8,128)(2,1)S(1)}, u32[]{:S(2)}, u32[]{:S(2)}) collective-permute-start(bf16[2048,256]{1,0:T(8,128)(2,1)S(1)} %get-tuple-element.41), channel_id=1, source_target_pairs={{8,136},{32,160},{48,176},{64,192},{104,232},{112,240},{9,137},{33... | collective-permute-start | bytes 3145736 | tf_op jit(solution)/shard_map/ppermute | solution.py:347
  74.0 16.7 %collective-permute-start.12 = (bf16[2048,256]{1,0:T(8,128)(2,1)S(1)}, bf16[2048,256]{1,0:T(8,128)(2,1)S(1)}, u32[]{:S(2)}, u32[]{:S(2)}) collective-permute-start(bf16[2048,256]{1,0:T(8,128)(2,1)S(1)} %get-tuple-element.39.refs_3_), channel_id=1, source_target_pairs={{32,48},{48,64},{64,80},{80,96},{96,112},{104,88},{120,104},{128,1... | collective-permute-start | bytes 3145736 | tf_op jit(solution)/shard_map/ppermute | solution.py:347
  75.9 17.3 %collective-permute-start.13 = (bf16[2048,256]{1,0:T(8,128)(2,1)S(1)}, bf16[2048,256]{1,0:T(8,128)(2,1)S(1)}, u32[]{:S(2)}, u32[]{:S(2)}) collective-permute-start(bf16[2048,256]{1,0:T(8,128)(2,1)S(1)} %get-tuple-element.40), channel_id=1, source_target_pairs={{32,160},{48,176},{64,192},{80,208},{96,224},{112,240},{33,161},{4... | collective-permute-start | bytes 3145736 | tf_op jit(solution)/shard_map/ppermute | solution.py:347
  77.2 52.7 %collective-permute-start.22 = (bf16[9,512,256]{2,1,0:T(8,128)(2,1)S(1)}, bf16[9,512,256]{2,1,0:T(8,128)(2,1)S(1)}, u32[]{:S(2)}, u32[]{:S(2)}) collective-permute-start(bf16[9,512,256]{2,1,0:T(8,128)(2,1)S(1)} %get-tuple-element.50), channel_id=1, source_target_pairs={{0,8},{8,0},{16,24},{24,16},{32,40},{40,32},{48,56},{56,48},{64,72... | collective-permute-start | bytes 7077896 | tf_op jit(solution)/shard_map/ppermute | solution.py:351
  82.8 19.1 %collective-permute-start.16 = (bf16[2048,256]{1,0:T(8,128)(2,1)S(1)}, bf16[2048,256]{1,0:T(8,128)(2,1)S(1)}, u32[]{:S(2)}, u32[]{:S(2)}) collective-permute-start(bf16[2048,256]{1,0:T(8,128)(2,1)S(1)} %get-tuple-element.42.refs_6_), channel_id=1, source_target_pairs={{48,64},{64,80},{80,96},{88,72},{96,112},{104,88},{120,104},{128,1... | collective-permute-start | bytes 3145736 | tf_op jit(solution)/shard_map/ppermute | solution.py:347
  84.7 19.7 %collective-permute-start.18 = (bf16[2048,256]{1,0:T(8,128)(2,1)S(1)}, bf16[2048,256]{1,0:T(8,128)(2,1)S(1)}, u32[]{:S(2)}, u32[]{:S(2)}) collective-permute-start(bf16[2048,256]{1,0:T(8,128)(2,1)S(1)} %get-tuple-element.45), channel_id=1, source_target_pairs={{48,176},{64,192},{88,216},{104,232},{112,240},{49,177},{65,193},{... | collective-permute-start | bytes 3145736 | tf_op jit(solution)/shard_map/ppermute | solution.py:347
  95.4 23.2 %collective-permute-start.17 = (bf16[2048,256]{1,0:T(8,128)(2,1)S(1)}, bf16[2048,256]{1,0:T(8,128)(2,1)S(1)}, u32[]{:S(2)}, u32[]{:S(2)}) collective-permute-start(bf16[2048,256]{1,0:T(8,128)(2,1)S(1)} %get-tuple-element.44.refs_4_), channel_id=1, source_target_pairs={{96,112},{128,144},{136,248},{144,160},{152,136},{160,176},{168,15... | collective-permute-start | bytes 3145736 | tf_op jit(solution)/shard_map/ppermute | solution.py:347
  97.4 21.3 %collective-permute-start.19 = (bf16[2048,256]{1,0:T(8,128)(2,1)S(1)}, bf16[2048,256]{1,0:T(8,128)(2,1)S(1)}, u32[]{:S(2)}, u32[]{:S(2)}) collective-permute-start(bf16[2048,256]{1,0:T(8,128)(2,1)S(1)} %get-tuple-element.46), channel_id=1, source_target_pairs={{88,216},{104,232},{112,240},{89,217},{105,233},{113,241},{90,218}... | collective-permute-start | bytes 3145736 | tf_op jit(solution)/shard_map/ppermute | solution.py:347
  105.2 24.6 %collective-permute-start.20 = (bf16[2048,256]{1,0:T(8,128)(2,1)S(1)}, bf16[2048,256]{1,0:T(8,128)(2,1)S(1)}, u32[]{:S(2)}, u32[]{:S(2)}) collective-permute-start(bf16[2048,256]{1,0:T(8,128)(2,1)S(1)} %get-tuple-element.47.refs_4_), channel_id=1, source_target_pairs={{96,112},{128,144},{136,248},{144,160},{152,136},{160,176},{168,15... | collective-permute-start | bytes 3145736 | tf_op jit(solution)/shard_map/ppermute | solution.py:347
  107.2 22.7 %collective-permute-start.21 = (bf16[2048,256]{1,0:T(8,128)(2,1)S(1)}, bf16[2048,256]{1,0:T(8,128)(2,1)S(1)}, u32[]{:S(2)}, u32[]{:S(2)}) collective-permute-start(bf16[2048,256]{1,0:T(8,128)(2,1)S(1)} %get-tuple-element.49), channel_id=1, source_target_pairs={{64,192},{88,216},{96,224},{112,240},{65,193},{89,217},{97,225},{1... | collective-permute-start | bytes 3145736 | tf_op jit(solution)/shard_map/ppermute | solution.py:347
  118.6 11.2 %collective-permute-start.23 = (bf16[4,512,256]{2,1,0:T(8,128)(2,1)S(1)}, bf16[4,512,256]{2,1,0:T(8,128)(2,1)S(1)}, u32[]{:S(2)}, u32[]{:S(2)}) collective-permute-start(bf16[4,512,256]{2,1,0:T(8,128)(2,1)S(1)} %get-tuple-element.51), channel_id=1, source_target_pairs={{0,8},{8,0},{16,24},{24,16},{32,40},{40,32},{48,56},{56,48},{64,72... | collective-permute-start | bytes 3145736 | tf_op jit(solution)/shard_map/ppermute | solution.py:351
  120.7 9.2 %collective-permute-start.24 = (bf16[4,512,256]{2,1,0:T(8,128)(2,1)S(1)}, bf16[4,512,256]{2,1,0:T(8,128)(2,1)S(1)}, u32[]{:S(2)}, u32[]{:S(2)}) collective-permute-start(bf16[4,512,256]{2,1,0:T(8,128)(2,1)S(1)} %get-tuple-element.52), channel_id=1, source_target_pairs={{0,8},{8,0},{16,24},{24,16},{32,40},{40,32},{48,56},{56,48},{64,72... | collective-permute-start | bytes 3145736 | tf_op jit(solution)/shard_map/ppermute | solution.py:351
  129.9 2.5 %copy-start.7 = (bf16[4,512,256]{2,1,0:T(8,128)(2,1)}, bf16[4,512,256]{2,1,0:T(8,128)(2,1)S(1)}, u32[]{:S(2)}) copy-start(bf16[4,512,256]{2,1,0:T(8,128)(2,1)S(1)} %collective-permute-done.24.refs_4_.refs_6_) | copy-start | bytes 3145732
  132.3 2.3 collective-permute-start.25
  134.6 60.3 %collective-permute-start.26 = (bf16[8,256,2048]{2,1,0:T(8,128)(2,1)}, bf16[8,256,2048]{2,1,0:T(8,128)(2,1)}, u32[]{:S(2)}, u32[]{:S(2)}) collective-permute-start(bf16[8,256,2048]{2,1,0:T(8,128)(2,1)} %bitcast.18), channel_id=1, source_target_pairs={{0,8},{8,0},{16,24},{24,16},{32,40},{40,32},{48,56},{56,48},{64,72... | collective-permute-start | bytes 25165832 | tf_op jit(solution)/shard_map/ppermute | solution.py:599
  (6 other events, 8.8 us)
Sparse Core Ops, SparseCore 0:
  9.1 94.8 all-gather.2

commit v7 on v5

--- a/solution.py
+++ b/solution.py
@@ -22,90 +22,90 @@
     (
         (
             0, 1, 2, 3, 4, 5, 6, -1, 8, -1, 10, -1, 12, -1, -1, 15,
-            16, 17, 18, 19, 20, 21, 22, -1, 24, -1, 26, -1, -1, -1, -1, -1,
-        ),
-        (
-            -1, 1, -1, 3, -1, -1, -1, 7, -1, 9, -1, 11, -1, 13, 14, -1,
+            16, 17, 18, 19, 20, 21, 22, -1, 24, -1, 26, -1, 28, -1, -1, -1,
+        ),
+        (
+            -1, 1, 2, -1, -1, 5, -1, 7, -1, 9, -1, 11, -1, 13, 14, -1,
             -1, -1, -1, -1, -1, -1, -1, -1, -1, -1, -1, -1, -1, -1, -1, -1,
         ),
     ),
     (
         (
             1, 0, 3, 2, 5, -1, 7, -1, 9, -1, 11, -1, 13, -1, -1, 14,
-            17, 16, 19, 18, 21, -1, 23, -1, 25, -1, 27, -1, -1, -1, -1, -1,
-        ),
-        (
-            -1, 0, -1, -1, -1, 4, -1, 6, -1, 8, -1, 10, -1, 12, 15, -1,
+            17, 16, 19, 18, 21, -1, 23, -1, 25, -1, 27, -1, 29, -1, -1, -1,
+        ),
+        (
+            -1, 0, 3, -1, -1, 4, -1, 6, -1, 8, -1, 10, -1, 12, 15, -1,
             -1, -1, -1, -1, -1, -1, -1, -1, -1, -1, -1, -1, -1, -1, -1, -1,
         ),
     ),
     (
         (
             -1, 3, 0, 5, 2, -1, 4, -1, 6, -1, 8, -1, 10, -1, -1, 1,
-            -1, 19, 16, 21, 18, -1, 20, 7, 22, 9, 24, 11, 1018, 13, 14, 17,
-        ),
-        (
-            -1, 3, -1, 226, 226, -1, 36, -1, 38, -1, 40, -1, -1, 15, 12, -1,
+            -1, 19, 16, 21, 18, 5, 20, 7, 22, 9, 24, 11, 26, 13, 14, 17,
+        ),
+        (
+            -1, 3, -1, -1, -1, -1, 4, -1, 6, -1, 8, -1, -1, 15, 12, -1,
             -1, -1, -1, -1, -1, -1, -1, -1, -1, -1, -1, -1, -1, -1, -1, -1,
         ),
     ),
     (
         (
             -1, 2, 1, -1, 3, -1, 5, -1, 7, -1, 9, -1, 11, -1, -1, 0,
-            -1, 18, 17, -1, 19, 4, 21, 6, 23, 8, 25, 10, 987, 12, 15, 16,
-        ),
-        (
-            -1, 2, 96, -1, 35, -1, 37, -1, 39, -1, 41, -1, 426, -1, 13, -1,
+            -1, 18, 17, -1, 19, 4, 21, 6, 23, 8, 25, 10, -1, 12, 15, 16,
+        ),
+        (
+            -1, 2, -1, -1, -1, -1, -1, -1, -1, -1, 9, -1, -1, 14, 13, -1,
             -1, -1, -1, -1, -1, -1, -1, -1, -1, -1, -1, -1, -1, -1, -1, -1,
         ),
     ),
     (
         (
             -1, 5, -1, -1, 0, -1, 2, -1, 4, -1, 6, -1, 8, 1, -1, 3,
-            14, 736, -1, -1, 16, 7, 18, 9, 20, 11, 22, 13, 56, 15, 12, 19,
-        ),
-        (
-            -1, 5, -1, -1, 32, -1, 34, -1, 4, -1, -1, -1, -1, 14, 10, -1,
+            14, 160, 35, 5, 16, 7, 18, 9, 20, 11, 22, 13, 952, 15, 12, 19,
+        ),
+        (
+            -1, -1, 96, -1, 128, -1, 226, -1, 292, -1, 6, -1, 426, -1, 10, -1,
             -1, -1, -1, -1, -1, -1, -1, -1, -1, -1, -1, -1, -1, -1, -1, -1,
         ),
     ),
     (
         (
             -1, -1, -1, -1, 33, -1, 35, -1, 37, -1, 7, -1, 9, 0, -1, 2,
-            15, 129, -1, 4, 17, 6, 51, 8, 21, 10, 23, 12, 57, 624, 13, 50,
-        ),
-        (
-            -1, -1, -1, -1, 1, -1, 3, -1, 5, -1, 294, -1, 360, -1, 11, -1,
-            -1, -1, -1, -1, -1, -1, -1, -1, -1, -1, -1, -1, -1, -1, -1, -1,
-        ),
-    ),
-    (
-        (
-            -1, -1, -1, -1, -1, -1, 0, -1, 34, -1, 4, 33, 6, 3, -1, 37,
-            12, 5, 14, 7, -1, 9, 48, 11, 4, 13, 20, 15, 54, 14, 10, -1,
-        ),
-        (
-            -1, -1, -1, -1, -1, -1, 32, -1, 2, -1, -1, 1, -1, 160, 8, -1,
+            15, 129, -1, 4, 17, 6, 51, 8, 21, 10, 23, 12, 57, 14, 13, 50,
+        ),
+        (
+            -1, -1, -1, -1, 1, -1, 3, -1, 5, -1, 39, -1, -1, 96, 11, -1,
+            -1, -1, -1, -1, -1, -1, -1, -1, -1, -1, -1, -1, -1, -1, -1, -1,
+        ),
+    ),
+    (
+        (
+            -1, -1, -1, -1, -1, -1, 32, -1, 34, -1, 4, 1, 6, 3, -1, 37,
+            12, 5, 14, 7, -1, 9, 48, 11, 50, 13, 20, 15, 54, 624, 10, -1,
+        ),
+        (
+            -1, -1, -1, -1, -1, -1, 0, -1, 2, -1, 36, -1, 360, -1, 8, -1,
             -1, -1, -1, -1, -1, -1, -1, -1, -1, -1, -1, -1, -1, -1, -1, -1,
         ),
     ),
     (
         (
             -1, -1, -1, -1, -1, -1, -1, -1, -1, -1, -1, -1, 39, -1, -1, -1,
-            45, 195, 15, 38, 33, 40, 611, 42, 645, 44, 53, -1, 55, 51, 43, -1,
-        ),
-        (
-            -1, -1, -1, -1, -1, -1, -1, -1, -1, -1, -1, 32, -1, 129, 41, -1,
+            45, 740, 47, 38, 33, 40, 611, 42, 37, 44, 742, 46, 55, 51, 43, -1,
+        ),
+        (
+            -1, -1, -1, -1, -1, -1, -1, -1, -1, -1, -1, 96, -1, 162, 41, -1,
             -1, -1, -1, -1, -1, -1, -1, -1, -1, -1, -1, -1, -1, -1, -1, -1,
         ),
     ),
     (
         (
             -1, -1, -1, -1, -1, -1, -1, -1, -1, -1, -1, -1, 36, -1, -1, -1,
-            42, 7, 44, 41, 46, 43, -1, 45, 34, 47, 36, 513, 52, -1, 40, 37,
-        ),
-        (
-            -1, -1, -1, -1, -1, -1, -1, -1, 32, -1, -1, 35, 294, -1, 38, -1,
+            42, 39, 44, 41, 46, 43, 32, 45, 34, 47, -1, -1, 52, -1, 40, 37,
+        ),
+        (
+            -1, -1, -1, -1, -1, -1, -1, -1, -1, 33, -1, 35, 292, -1, 38, -1,
             -1, -1, -1, -1, -1, -1, -1, -1, -1, -1, -1, -1, -1, -1, -1, -1,
         ),
     ),
@@ -333,7 +333,7 @@
             buffers = move(
                 ways,
                 slots,
-                [row, want if step > 1 else row],
+                [row, want if slots[0] or any(any(parts) for _, *parts in ways[0]) else row],
                 [arrived[key] for key in tables.sources[step]],
                 kv.shape[1],
                 after=buffers[:1] if step <= len(SCHEDULE) else passed,
@@ -513,7 +513,7 @@
     parts, rows, features = attended.shape
     depth = mine.shape[1]
     columns = mine.shape[2] // parts
-    together = 2
+    together = 4
     return pl.pallas_call(
         functools.partial(project_kernel, depth),
         out_shape=jax.ShapeDtypeStruct((parts, rows, columns), jnp.bfloat16),

time: 225 us -> 231 us (1.027); the launches traced: 223 us -> 226 us
  Pallas kernels: 50.5 us -> 54.8 us
  starting transfers between devices: 40.7 us -> 37.4 us
  waiting for transfers between devices: 56.9 us -> 59.4 us
    pallas_call x10, Pallas kernels: 18.8 us -> 23.5 us  [move(): pl.pallas_call(functools.partial(move_kernel, *ways, *slots), out_shape=[...]
    ppermute x4, starting transfers between devices: 3.53 us -> 0.73 us  [exchange(): passed.append(lax.ppermute(give, 'ctx', SWAP))]
  transfers between devices with their start and end apart: 28 -> 28, of which waited for: 15 -> 15; matrix products, arithmetic and copies ran while one was open for 1% -> 1% of each run, Pallas kernels for 19% -> 20%
where the time goes in v7:
time: 231 us; the launch traced here: 226 us
  waiting for transfers between devices  59.4 us (26%)
  Pallas kernels  54.8 us (24%)
  blocking collectives  53.8 us (23%)
  starting transfers between devices  37.4 us (16%)
  between operations  13.8 us (6%)
  local copies, waits for them, and re-layouts  7.01 us (3%)
    ppermute x18, waiting for transfers between devices, exchange(): arrived[step, way] = lax.ppermute(buffers[way], 'ctx', pairs(step, way))  56.2 us
    all_to_all x1, blocking collectives, per_device(): lax.all_to_all(attended.reshape(head_count, rows // head_count, width), '...  34.5 us
    ppermute x18, starting transfers between devices, exchange(): arrived[step, way] = lax.ppermute(buffers[way], 'ctx', pairs(step, way))  30.7 us
    pallas_call x10, Pallas kernels, move(): pl.pallas_call(functools.partial(move_kernel, *ways, *slots), out_shape=[...  23.5 us
    pallas_call x1, Pallas kernels, attention(): pl.pallas_call(functools.partial(attention_kernel, width // HEAD_SIZE, le...  22.7 us
    all_to_all x1, blocking collectives, per_device(): return lax.all_to_all(mixed, 'head', 0, 0, tiled=True).reshape(rows, -1)  19.3 us
    pallas_call x1, Pallas kernels, project(): pl.pallas_call(functools.partial(project_kernel, depth), out_shape=jax.Sh...  8.55 us
    ppermute x2, starting transfers between devices, exchange(): lax.ppermute(chip, 'ctx', [(target(way, i), i) for i in range(CORES >> wa...  5.69 us
  transfers between devices with their start and end apart: 28, of which 15 were waited for; matrix products, arithmetic and copies ran while one was open for 1% of the time, Pallas kernels for 20%

profile of v7, /device:TPU:226, one launch (start us, length us, event | category | flops | bytes accessed | tf_op | source)
XLA Modules:
  0.0 226.4 jit_solution(5683632267190958123)
XLA Ops:
  6.6 1.6 copy-done
  14.3 2.0 shard_map.64
  18.9 9.0 %collective-permute-done.3.refs_0_.refs_4_.refs_5_ = bf16[2048,256]{1,0:T(8,128)(2,1)S(1)} collective-permute-done((bf16[2048,256]{1,0:T(8,128)(2,1)}, bf16[2048,256]{1,0:T(8,128)(2,1)S(1)}, u32[]{:S(2)}, u32[]{:S(2)}) %collective-permute-start.3) | collective-permute-done | bytes 1048608 | tf_op jit(solution)/shard_map/ppermute | solution.py:345
  29.2 2.1 shard_map.65
  31.3 1.9 collective-permute-start.6
  35.9 5.4 %collective-permute-start.2 = (s32[2,12]{1,0:T(2,128)S(1)}, s32[2,12]{1,0:T(2,128)S(1)}, u32[]{:S(2)}, u32[]{:S(2)}) collective-permute-start(s32[2,12]{1,0:T(2,128)S(1)} %add_select_fusion.2), channel_id=1, source_target_pairs={{128,0},{136,8},{144,16},{152,24},{160,32},{168,40},{176,48},{184,... | collective-permute-start | bytes 296 | tf_op jit(solution)/shard_map/ppermute | solution.py:319
  41.6 3.2 %shard_map.66 = (bf16[2048,256]{1,0:T(8,128)(2,1)}, bf16[2048,256]{1,0:T(8,128)(2,1)}) custom-call(s32[224]{0:T(256)S(1)} %bitcast.10, s32[224]{0:T(256)S(1)} %bitcast.11, bf16[2048,256]{1,0:T(8,128)(2,1)} %collective-permute-done.9.refs_0_.refs_3_.refs_6_, bf16[2048,256]{1,0:T(8,128)(2,1)} %collective-permute-done.7.refs_1_.refs_7_, ...), custom_call_target="tpu_custom_call" | custom-call | bytes 50331648 | tf_op jit(solution)/shard_map/pallas_call | solution.py:220
  44.8 4.7 %collective-permute-start.11 = (bf16[2048,256]{1,0:T(8,128)(2,1)}, bf16[2048,256]{1,0:T(8,128)(2,1)}, u32[]{:S(2)}, u32[]{:S(2)}) collective-permute-start(bf16[2048,256]{1,0:T(8,128)(2,1)} %get-tuple-element.35.refs_5_), channel_id=1, source_target_pairs={{8,120},{16,32},{32,48},{48,64},{64,80},{80,96},{96,112},{120,104}... | collective-permute-start | bytes 3145736 | tf_op jit(solution)/shard_map/ppermute | solution.py:345
  51.8 1.9 shard_map.67
  53.7 2.1 collective-permute-start.10
  57.1 4.1 %collective-permute-done.11.refs_0_.refs_1_ = bf16[2048,256]{1,0:T(8,128)(2,1)} collective-permute-done((bf16[2048,256]{1,0:T(8,128)(2,1)}, bf16[2048,256]{1,0:T(8,128)(2,1)}, u32[]{:S(2)}, u32[]{:S(2)}) %collective-permute-start.11) | collective-permute-done | bytes 1048608 | tf_op jit(solution)/shard_map/ppermute | solution.py:345
  61.2 5.4 %collective-permute-done.13.refs_2_.refs_9_ = bf16[2048,256]{1,0:T(8,128)(2,1)} collective-permute-done((bf16[2048,256]{1,0:T(8,128)(2,1)}, bf16[2048,256]{1,0:T(8,128)(2,1)}, u32[]{:S(2)}, u32[]{:S(2)}) %collective-permute-start.13) | collective-permute-done | bytes 1048608 | tf_op jit(solution)/shard_map/ppermute | solution.py:345
  66.6 1.9 shard_map.68
  68.5 1.9 collective-permute-start.16
  72.3 5.4 %collective-permute-done.12.refs_3_ = bf16[2048,256]{1,0:T(8,128)(2,1)S(1)} collective-permute-done((bf16[2048,256]{1,0:T(8,128)(2,1)S(1)}, bf16[2048,256]{1,0:T(8,128)(2,1)S(1)}, u32[]{:S(2)}, u32[]{:S(2)}) %collective-permute-start.12) | collective-permute-done | bytes 1048608 | tf_op jit(solution)/shard_map/ppermute | solution.py:345
  77.7 5.0 %shard_map.69 = (bf16[2048,256]{1,0:T(8,128)(2,1)S(1)}, bf16[2048,256]{1,0:T(8,128)(2,1)S(1)}, bf16[11,512,256]{2,1,0:T(8,128)(2,1)}, bf16[11,512,256]{2,1,0:T(8,128)(2,1)}) custom-call(s32[224]{0:T(256)S(1)} %bitcast.14, s32[192]{0:T(256)S(1)} %reshape.277.want, bf16[2048,256]{1,0:T(8,128)(2,1)S(1)} %collective-permute-done.10.refs_0_.refs_4_, ...), custom_call_target="tpu_custom_call" | custom-call | bytes 188743680 | tf_op jit(solution)/shard_map/pallas_call | solution.py:220
  82.8 1.9 collective-permute-start.14
  86.0 2.9 %collective-permute-done.17.refs_2_.refs_3_ = bf16[2048,256]{1,0:T(8,128)(2,1)S(1)} collective-permute-done((bf16[2048,256]{1,0:T(8,128)(2,1)S(1)}, bf16[2048,256]{1,0:T(8,128)(2,1)S(1)}, u32[]{:S(2)}, u32[]{:S(2)}) %collective-permute-start.17) | collective-permute-done | bytes 1048608 | tf_op jit(solution)/shard_map/ppermute | solution.py:345
  89.7 1.9 collective-permute-start.18
  92.9 6.5 %collective-permute-done.14.refs_0_ = bf16[2048,256]{1,0:T(8,128)(2,1)S(1)} collective-permute-done((bf16[2048,256]{1,0:T(8,128)(2,1)S(1)}, bf16[2048,256]{1,0:T(8,128)(2,1)S(1)}, u32[]{:S(2)}, u32[]{:S(2)}) %collective-permute-start.14) | collective-permute-done | bytes 1048608 | tf_op jit(solution)/shard_map/ppermute | solution.py:345
  99.5 1.9 collective-permute-done.15.refs_1_
  101.4 2.4 %shard_map.71 = (bf16[2048,256]{1,0:T(8,128)(2,1)S(1)}, bf16[2048,256]{1,0:T(8,128)(2,1)S(1)}, bf16[4,512,256]{2,1,0:T(8,128)(2,1)}, bf16[4,512,256]{2,1,0:T(8,128)(2,1)}) custom-call(s32[224]{0:T(256)S(1)} %bitcast.16, s32[192]{0:T(256)S(1)} %reshape.277.want, bf16[2048,256]{1,0:T(8,128)(2,1)S(1)} %collective-permute-done.14.refs_0_, ...), custom_call_target="tpu_custom_call" | custom-call | bytes 100663296 | tf_op jit(solution)/shard_map/pallas_call | solution.py:220
  103.8 1.9 collective-permute-start.20
  107.0 3.7 %collective-permute-done.18.refs_0_ = bf16[2048,256]{1,0:T(8,128)(2,1)S(1)} collective-permute-done((bf16[2048,256]{1,0:T(8,128)(2,1)S(1)}, bf16[2048,256]{1,0:T(8,128)(2,1)S(1)}, u32[]{:S(2)}, u32[]{:S(2)}) %collective-permute-start.18) | collective-permute-done | bytes 1048608 | tf_op jit(solution)/shard_map/ppermute | solution.py:345
  112.6 1.9 shard_map.72
  114.6 13.3 %collective-permute-done.20.refs_0_ = bf16[2048,256]{1,0:T(8,128)(2,1)S(1)} collective-permute-done((bf16[2048,256]{1,0:T(8,128)(2,1)S(1)}, bf16[2048,256]{1,0:T(8,128)(2,1)S(1)}, u32[]{:S(2)}, u32[]{:S(2)}) %collective-permute-start.20) | collective-permute-done | bytes 1048608 | tf_op jit(solution)/shard_map/ppermute | solution.py:345
  127.9 2.4 %shard_map.73 = (bf16[2,512,256]{2,1,0:T(8,128)(2,1)}, bf16[2,512,256]{2,1,0:T(8,128)(2,1)}) custom-call(s32[224]{0:T(256)S(1)} %bitcast.18, s32[192]{0:T(256)S(1)} %reshape.277.want, bf16[2048,256]{1,0:T(8,128)(2,1)S(1)} %collective-permute-done.20.refs_0_, bf16[2048,256]{1,0:T(8,128)(2,1)S(1)} %collective-permute-done.21.refs_1_, ...), custom_call_target="tpu_custom_call" | custom-call | bytes 25165824 | tf_op jit(solution)/shard_map/pallas_call | solution.py:220
  130.5 2.1 collective-permute-done.25.refs_7_
  133.4 22.7 %shard_map.74 = bf16[2048,512]{1,0:T(8,128)(2,1)S(1)} custom-call(s32[12]{0:T(128)S(1)} %reshape.276.info, s32[224]{0:T(256)S(1)} %bitcast.19, bf16[2048,512]{1,0:T(8,128)(2,1)} %q_ref.1, bf16[2048,256]{1,0:T(8,128)(2,1)} %constant_dynamic-update-slice_fusion.refs_1_.kv_ref, bf16[11,512,256]{2,1,0:T(8,128)(2,1)} %get-tuple-element.40.refs_0_, ...), custom_call_target="tpu_custom_call" | custom-call | flops 8589934592 | bytes 8388608 | tf_op jit(solution)/shard_map/pallas_call | solution.py:464
  156.1 34.5 %all_to_all.10.a_ref = bf16[8,256,512]{2,1,0:T(8,128)(2,1)S(1)} all-to-all(bf16[8,256,512]{2,1,0:T(8,128)(2,1)S(1)} %bitcast.5), channel_id=1, replica_groups=mesh['ctx'=32,'head'=8] {'head'}, dimensions={0} | all-to-all | bytes 4194304 | tf_op jit(solution)/shard_map/all_to_all | solution.py:565
  190.7 8.6 %shard_map.75 = bf16[8,256,256]{2,1,0:T(8,128)(2,1)S(1)} custom-call(s32[1]{0:T(128)} %bitcast.core, bf16[8,256,512]{2,1,0:T(8,128)(2,1)S(1)} %all_to_all.10.a_ref, bf16[8,256,2048]{2,1,0:T(8,128)(2,1)} %bitcast.21, bf16[8,256,2048]{2,1,0:T(8,128)(2,1)} %collective-permute-done.26.other_ref), custom_call_target="tpu_custom_call" | custom-call | flops 4294967296 | bytes 20971520 | tf_op jit(solution)/shard_map/pallas_call | solution.py:517
  199.2 19.3 %all_to_all.11 = bf16[8,256,256]{2,1,0:T(8,128)(2,1)S(1)} all-to-all(bf16[8,256,256]{2,1,0:T(8,128)(2,1)S(1)} %shard_map.75), channel_id=1, replica_groups=mesh['ctx'=32,'head'=8] {'head'}, dimensions={0} | all-to-all | bytes 2097152 | tf_op jit(solution)/shard_map/all_to_all | solution.py:569
  (74 shorter events, 27.0 us)
Async XLA Ops:
  6.5 126.1 %all-gather.3.cloned.1.call-start = ((), (), s32[]{:S(2)}) async-start(), calls=%async_computation.2 | async-start | bytes 9437184 | tf_op jit(solution)/shard_map/all_gather | solution.py:550
  10.9 23.6 %copy-start.9 = (s32[4,3]{1,0:T(4,128)S(1)}, s32[4,3]{1,0:T(4,128)}, u32[]{:S(2)}) copy-start(s32[4,3]{1,0:T(4,128)} %param.9) | copy-start | bytes 148
  10.9 3.4 %collective-permute-start.5 = (bf16[2048,256]{1,0:T(8,128)(2,1)}, bf16[2048,256]{1,0:T(8,128)(2,1)S(1)}, u32[]{:S(2)}, u32[]{:S(2)}) collective-permute-start(bf16[2048,256]{1,0:T(8,128)(2,1)} %constant_dynamic-update-slice_fusion.refs_1_.kv_ref), channel_id=1, source_target_pairs={{0,8},{8,0},{16,24},{24,16},{32,40},{40,32},{48,56},{56,48},{64,72... | collective-permute-start | bytes 3145736 | tf_op jit(solution)/shard_map/ppermute | solution.py:311
  10.9 17.0 %collective-permute-start.3 = (bf16[2048,256]{1,0:T(8,128)(2,1)}, bf16[2048,256]{1,0:T(8,128)(2,1)S(1)}, u32[]{:S(2)}, u32[]{:S(2)}) collective-permute-start(bf16[2048,256]{1,0:T(8,128)(2,1)} %constant_dynamic-update-slice_fusion.refs_1_.kv_ref), channel_id=1, source_target_pairs={{0,16},{8,120},{16,32},{24,8},{32,48},{40,24},{48,64},{64,80},{80,... | collective-permute-start | bytes 3145736 | tf_op jit(solution)/shard_map/ppermute | solution.py:345
  12.3 16.9 %collective-permute-start.4 = (bf16[2048,256]{1,0:T(8,128)(2,1)}, bf16[2048,256]{1,0:T(8,128)(2,1)S(1)}, u32[]{:S(2)}, u32[]{:S(2)}) collective-permute-start(bf16[2048,256]{1,0:T(8,128)(2,1)} %constant_dynamic-update-slice_fusion.refs_1_.kv_ref), channel_id=1, source_target_pairs={{8,136},{16,144},{40,168},{56,184},{72,200},{88,216},{104,232},{11... | collective-permute-start | bytes 3145736 | tf_op jit(solution)/shard_map/ppermute | solution.py:345
  14.3 17.0 %copy-start.2 = (bf16[2048,256]{1,0:T(8,128)(2,1)}, bf16[2048,256]{1,0:T(8,128)(2,1)S(1)}, u32[]{:S(2)}) copy-start(bf16[2048,256]{1,0:T(8,128)(2,1)S(1)} %collective-permute-done.5.refs_0_.refs_4_) | copy-start | bytes 3145732
  16.3 25.0 %collective-permute-start.7 = (bf16[2048,256]{1,0:T(8,128)(2,1)}, bf16[2048,256]{1,0:T(8,128)(2,1)}, u32[]{:S(2)}, u32[]{:S(2)}) collective-permute-start(bf16[2048,256]{1,0:T(8,128)(2,1)} %get-tuple-element.33), channel_id=1, source_target_pairs={{8,136},{16,144},{40,168},{56,184},{72,200},{88,216},{104,232},{11... | collective-permute-start | bytes 3145736 | tf_op jit(solution)/shard_map/ppermute | solution.py:345
  17.6 24.0 %collective-permute-start.9 = (bf16[2048,256]{1,0:T(8,128)(2,1)}, bf16[2048,256]{1,0:T(8,128)(2,1)}, u32[]{:S(2)}, u32[]{:S(2)}) collective-permute-start(bf16[2048,256]{1,0:T(8,128)(2,1)} %get-tuple-element.31.refs_2_), channel_id=1, source_target_pairs={{0,16},{8,120},{16,32},{24,8},{32,48},{48,64},{64,80},{80,96},{96,... | collective-permute-start | bytes 3145736 | tf_op jit(solution)/shard_map/ppermute | solution.py:345
  31.3 19.8 %collective-permute-start.6 = (bf16[2048,256]{1,0:T(8,128)(2,1)}, bf16[2048,256]{1,0:T(8,128)(2,1)S(1)}, u32[]{:S(2)}, u32[]{:S(2)}) collective-permute-start(bf16[2048,256]{1,0:T(8,128)(2,1)} %get-tuple-element.32.refs_2_), channel_id=1, source_target_pairs={{8,120},{16,32},{24,8},{32,48},{48,64},{64,80},{80,96},{96,112},{1... | collective-permute-start | bytes 3145736 | tf_op jit(solution)/shard_map/ppermute | solution.py:345
  33.2 18.6 %collective-permute-start.8 = (bf16[2048,256]{1,0:T(8,128)(2,1)}, bf16[2048,256]{1,0:T(8,128)(2,1)}, u32[]{:S(2)}, u32[]{:S(2)}) collective-permute-start(bf16[2048,256]{1,0:T(8,128)(2,1)} %get-tuple-element.34), channel_id=1, source_target_pairs={{8,136},{48,176},{64,192},{80,208},{104,232},{112,240},{9,137},{49... | collective-permute-start | bytes 3145736 | tf_op jit(solution)/shard_map/ppermute | solution.py:345
  34.5 1.2 collective-permute-start
  35.9 13.7 %collective-permute-start.2 = (s32[2,12]{1,0:T(2,128)S(1)}, s32[2,12]{1,0:T(2,128)S(1)}, u32[]{:S(2)}, u32[]{:S(2)}) collective-permute-start(s32[2,12]{1,0:T(2,128)S(1)} %add_select_fusion.2), channel_id=1, source_target_pairs={{128,0},{136,8},{144,16},{152,24},{160,32},{168,40},{176,48},{184,... | collective-permute-start | bytes 296 | tf_op jit(solution)/shard_map/ppermute | solution.py:319
  41.3 9.5 %collective-permute-start.1 = (s32[2,12]{1,0:T(2,128)S(1)}, s32[2,12]{1,0:T(2,128)S(1)}, u32[]{:S(2)}, u32[]{:S(2)}) collective-permute-start(s32[2,12]{1,0:T(2,128)S(1)} %add_select_fusion.2), channel_id=1, source_target_pairs={{16,0},{120,8},{32,16},{8,24},{48,32},{24,40},{64,48},{40,56},{80,... | collective-permute-start | bytes 296 | tf_op jit(solution)/shard_map/ppermute | solution.py:319
  44.8 16.4 %collective-permute-start.11 = (bf16[2048,256]{1,0:T(8,128)(2,1)}, bf16[2048,256]{1,0:T(8,128)(2,1)}, u32[]{:S(2)}, u32[]{:S(2)}) collective-permute-start(bf16[2048,256]{1,0:T(8,128)(2,1)} %get-tuple-element.35.refs_5_), channel_id=1, source_target_pairs={{8,120},{16,32},{32,48},{48,64},{64,80},{80,96},{96,112},{120,104}... | collective-permute-start | bytes 3145736 | tf_op jit(solution)/shard_map/ppermute | solution.py:345
  49.6 17.0 %collective-permute-start.13 = (bf16[2048,256]{1,0:T(8,128)(2,1)}, bf16[2048,256]{1,0:T(8,128)(2,1)}, u32[]{:S(2)}, u32[]{:S(2)}) collective-permute-start(bf16[2048,256]{1,0:T(8,128)(2,1)} %get-tuple-element.38), channel_id=1, source_target_pairs={{8,136},{80,208},{104,232},{112,240},{9,137},{81,209},{105,233},{1... | collective-permute-start | bytes 3145736 | tf_op jit(solution)/shard_map/ppermute | solution.py:345
  53.7 24.0 %copy-start.3 = (bf16[2048,256]{1,0:T(8,128)(2,1)S(1)}, bf16[2048,256]{1,0:T(8,128)(2,1)}, u32[]{:S(2)}) copy-start(bf16[2048,256]{1,0:T(8,128)(2,1)} %copy-done.2) | copy-start | bytes 3145732
  53.7 18.6 %collective-permute-start.10 = (bf16[2048,256]{1,0:T(8,128)(2,1)S(1)}, bf16[2048,256]{1,0:T(8,128)(2,1)S(1)}, u32[]{:S(2)}, u32[]{:S(2)}) collective-permute-start(bf16[2048,256]{1,0:T(8,128)(2,1)S(1)} %get-tuple-element.36.refs_4_), channel_id=1, source_target_pairs={{8,120},{32,48},{48,64},{64,80},{80,96},{96,112},{104,88},{120,104... | collective-permute-start | bytes 3145736 | tf_op jit(solution)/shard_map/ppermute | solution.py:345
  55.8 21.9 %collective-permute-start.12 = (bf16[2048,256]{1,0:T(8,128)(2,1)S(1)}, bf16[2048,256]{1,0:T(8,128)(2,1)S(1)}, u32[]{:S(2)}, u32[]{:S(2)}) collective-permute-start(bf16[2048,256]{1,0:T(8,128)(2,1)S(1)} %get-tuple-element.37), channel_id=1, source_target_pairs={{16,144},{32,160},{48,176},{64,192},{80,208},{96,224},{112,240},{1... | collective-permute-start | bytes 3145736 | tf_op jit(solution)/shard_map/ppermute | solution.py:345
  68.5 17.6 %collective-permute-start.16 = (bf16[2048,256]{1,0:T(8,128)(2,1)S(1)}, bf16[2048,256]{1,0:T(8,128)(2,1)S(1)}, u32[]{:S(2)}, u32[]{:S(2)}) collective-permute-start(bf16[2048,256]{1,0:T(8,128)(2,1)S(1)} %get-tuple-element.39.refs_11_), channel_id=1, source_target_pairs={{32,48},{48,64},{64,80},{80,96},{96,112},{104,88},{120,104},{128,1... | collective-permute-start | bytes 3145736 | tf_op jit(solution)/shard_map/ppermute | solution.py:345
  70.4 18.5 %collective-permute-start.17 = (bf16[2048,256]{1,0:T(8,128)(2,1)S(1)}, bf16[2048,256]{1,0:T(8,128)(2,1)S(1)}, u32[]{:S(2)}, u32[]{:S(2)}) collective-permute-start(bf16[2048,256]{1,0:T(8,128)(2,1)S(1)} %get-tuple-element.43), channel_id=1, source_target_pairs={{32,160},{48,176},{64,192},{80,208},{104,232},{112,240},{33,161},{... | collective-permute-start | bytes 3145736 | tf_op jit(solution)/shard_map/ppermute | solution.py:345
  82.7 45.2 %collective-permute-start.22 = (bf16[11,512,256]{2,1,0:T(8,128)(2,1)}, bf16[11,512,256]{2,1,0:T(8,128)(2,1)S(1)}, u32[]{:S(2)}, u32[]{:S(2)}) collective-permute-start(bf16[11,512,256]{2,1,0:T(8,128)(2,1)} %get-tuple-element.50), channel_id=1, source_target_pairs={{0,8},{8,0},{16,24},{24,16},{32,40},{40,32},{48,56},{56,48},{64,72... | collective-permute-start | bytes 8650760 | tf_op jit(solution)/shard_map/ppermute | solution.py:349
  82.8 16.7 %collective-permute-start.14 = (bf16[2048,256]{1,0:T(8,128)(2,1)S(1)}, bf16[2048,256]{1,0:T(8,128)(2,1)S(1)}, u32[]{:S(2)}, u32[]{:S(2)}) collective-permute-start(bf16[2048,256]{1,0:T(8,128)(2,1)S(1)} %get-tuple-element.41.refs_5_), channel_id=1, source_target_pairs={{48,64},{64,80},{80,96},{88,72},{96,112},{104,88},{120,104},{128,1... | collective-permute-start | bytes 3145736 | tf_op jit(solution)/shard_map/ppermute | solution.py:345
  84.7 16.7 %collective-permute-start.15 = (bf16[2048,256]{1,0:T(8,128)(2,1)S(1)}, bf16[2048,256]{1,0:T(8,128)(2,1)S(1)}, u32[]{:S(2)}, u32[]{:S(2)}) collective-permute-start(bf16[2048,256]{1,0:T(8,128)(2,1)S(1)} %get-tuple-element.42), channel_id=1, source_target_pairs={{48,176},{64,192},{80,208},{96,224},{112,240},{49,177},{65,193},{8... | collective-permute-start | bytes 3145736 | tf_op jit(solution)/shard_map/ppermute | solution.py:345
  89.7 21.0 %collective-permute-start.18 = (bf16[2048,256]{1,0:T(8,128)(2,1)S(1)}, bf16[2048,256]{1,0:T(8,128)(2,1)S(1)}, u32[]{:S(2)}, u32[]{:S(2)}) collective-permute-start(bf16[2048,256]{1,0:T(8,128)(2,1)S(1)} %get-tuple-element.44.refs_4_), channel_id=1, source_target_pairs={{96,112},{128,144},{136,248},{144,160},{152,136},{160,176},{168,15... | collective-permute-start | bytes 3145736 | tf_op jit(solution)/shard_map/ppermute | solution.py:345
  91.6 21.0 %collective-permute-start.19 = (bf16[2048,256]{1,0:T(8,128)(2,1)S(1)}, bf16[2048,256]{1,0:T(8,128)(2,1)S(1)}, u32[]{:S(2)}, u32[]{:S(2)}) collective-permute-start(bf16[2048,256]{1,0:T(8,128)(2,1)S(1)} %get-tuple-element.46), channel_id=1, source_target_pairs={{88,216},{104,232},{112,240},{89,217},{105,233},{113,241},{90,218}... | collective-permute-start | bytes 3145736 | tf_op jit(solution)/shard_map/ppermute | solution.py:345
  103.8 24.1 %collective-permute-start.20 = (bf16[2048,256]{1,0:T(8,128)(2,1)S(1)}, bf16[2048,256]{1,0:T(8,128)(2,1)S(1)}, u32[]{:S(2)}, u32[]{:S(2)}) collective-permute-start(bf16[2048,256]{1,0:T(8,128)(2,1)S(1)} %get-tuple-element.47.refs_2_), channel_id=1, source_target_pairs={{96,112},{128,144},{136,248},{144,160},{152,136},{160,176},{168,15... | collective-permute-start | bytes 3145736 | tf_op jit(solution)/shard_map/ppermute | solution.py:345
  105.7 22.2 %collective-permute-start.21 = (bf16[2048,256]{1,0:T(8,128)(2,1)S(1)}, bf16[2048,256]{1,0:T(8,128)(2,1)S(1)}, u32[]{:S(2)}, u32[]{:S(2)}) collective-permute-start(bf16[2048,256]{1,0:T(8,128)(2,1)S(1)} %get-tuple-element.49), channel_id=1, source_target_pairs={{72,200},{88,216},{96,224},{112,240},{73,201},{89,217},{97,225},{1... | collective-permute-start | bytes 3145736 | tf_op jit(solution)/shard_map/ppermute | solution.py:345
  110.7 17.2 %collective-permute-start.23 = (bf16[4,512,256]{2,1,0:T(8,128)(2,1)}, bf16[4,512,256]{2,1,0:T(8,128)(2,1)S(1)}, u32[]{:S(2)}, u32[]{:S(2)}) collective-permute-start(bf16[4,512,256]{2,1,0:T(8,128)(2,1)} %get-tuple-element.51), channel_id=1, source_target_pairs={{0,8},{8,0},{16,24},{24,16},{32,40},{40,32},{48,56},{56,48},{64,72... | collective-permute-start | bytes 3145736 | tf_op jit(solution)/shard_map/ppermute | solution.py:349
  114.5 13.4 %collective-permute-start.24 = (bf16[3,512,256]{2,1,0:T(8,128)(2,1)}, bf16[3,512,256]{2,1,0:T(8,128)(2,1)S(1)}, u32[]{:S(2)}, u32[]{:S(2)}) collective-permute-start(bf16[3,512,256]{2,1,0:T(8,128)(2,1)} %get-tuple-element.52), channel_id=1, source_target_pairs={{0,8},{8,0},{16,24},{24,16},{32,40},{40,32},{48,56},{56,48},{64,72... | collective-permute-start | bytes 2359304 | tf_op jit(solution)/shard_map/ppermute | solution.py:349
  130.5 2.1 collective-permute-start.25
  132.6 58.0 %collective-permute-start.26 = (bf16[8,256,2048]{2,1,0:T(8,128)(2,1)}, bf16[8,256,2048]{2,1,0:T(8,128)(2,1)}, u32[]{:S(2)}, u32[]{:S(2)}) collective-permute-start(bf16[8,256,2048]{2,1,0:T(8,128)(2,1)} %bitcast.20), channel_id=1, source_target_pairs={{0,8},{8,0},{16,24},{24,16},{32,40},{40,32},{48,56},{56,48},{64,72... | collective-permute-start | bytes 25165832 | tf_op jit(solution)/shard_map/ppermute | solution.py:563
  190.7 28.9 %copy-start.1 = (bf16[512,2048]{1,0:T(8,128)(2,1)S(1)}, bf16[512,2048]{1,0:T(8,128)(2,1)}, u32[]{:S(2)}) copy-start(bf16[512,2048]{1,0:T(8,128)(2,1)} %param.10) | copy-start | bytes 6291460
  (7 other events, 16.2 us)
Sparse Core Ops, SparseCore 0:
  9.3 94.8 all-gather.2
